TPU v7x, 128 devices: a whole 4x4x4 slice. The times are simulated.
128 devices in a mesh: dp: 32 (over z, x, core), sect: 4 (over y).
Axes of the slice: x: 4, y: 4, z: 4, core: 2. Of those that a mesh axis runs over, the one named last changes fastest.
Arguments:
- queries: bfloat16 [32, 16, 8192], P('dp', None, 'sect'), may hold values from -5 to 5
- keys: bfloat16 [32, 16, 8192], P('dp', None, 'sect'), may hold values from -5 to 5
- values: bfloat16 [32, 16, 8192], P('dp', None, 'sect'), may hold values from -6 to 6
- residual: bfloat16 [32, 16, 8192], P('dp'), may hold values from -6 to 6
- labels: int32 [32, 16], P('dp'), may hold values from 0 to 2, as said below
- slot_modality: int32 [4], replicated, may hold values from 0 to 2, as said below
- gains: float32 [3, 8192], replicated, may hold values from 0.1 to 1.9
- up_weight: bfloat16 [4, 11008, 8192], P('sect', 'dp'), may hold values from -0.0625 to 0.0625
- down_weight: bfloat16 [4, 11008, 8192], P('sect', 'dp'), may hold values from -0.0546875 to 0.0546875
- cotangent: bfloat16 [32, 16, 8192], P('dp'), may hold values from -6 to 6
Outputs:
- output: bfloat16 [32, 16, 8192], P('dp', 'sect')
- residual_grad: bfloat16 [32, 16, 8192], P('dp', 'sect')
- query_grad: bfloat16 [32, 16, 8192], P('dp', None, 'sect')
- key_grad: bfloat16 [32, 16, 8192], P('dp', None, 'sect')
- value_grad: bfloat16 [32, 16, 8192], P('dp', None, 'sect')
- up_grad: bfloat16 [4, 11008, 8192], P('sect', 'dp')
- down_grad: bfloat16 [4, 11008, 8192], P('sect', 'dp')
- gain_grad: float32 [3, 8192], replicated
Inputs may be any that keep to these rules, and one draw needn't show every extreme that they name: `labels`: every sequence holds exactly 8 text tokens (label 0); its other tokens are image or speech. `slot_modality`: text owns two slots, image one, speech one.
All inputs are finite; a program needn't handle non-finite values.
Results may differ from a plain program's by a relative error of at most 0.015.
The roundings to bfloat16 on the way count: a program that leaves them out, or rounds other values in their place, can miss the bound.
Values may be sent and summed in bfloat16 or wider, within the bound.
No kernel may reach another device: no remote copies, remote signals or barrier semaphores. Data moves between devices by JAX's collectives and lax.ppermute only.
A program may use at most 128 MiB of HBM per device.

v0:
```python
import jax
import jax.numpy as jnp
from jax import lax
from jax.sharding import PartitionSpec as P

HD = 128
MODALITIES = 3


def causal_forward(queries, keys, values):
    seq_count, length, width = queries.shape
    head_count = width // HD
    query_f = queries.astype(jnp.float32).reshape(seq_count, length, head_count, HD)
    key_f = keys.astype(jnp.float32).reshape(seq_count, length, head_count, HD)
    value_f = values.astype(jnp.float32).reshape(seq_count, length, head_count, HD)
    scores = jnp.einsum("sqhd,skhd->shqk", query_f, key_f) * HD ** (-0.5)
    position = jnp.arange(length)
    causal = position[:, None] >= position[None, :]
    scores = jnp.where(causal, scores, -1e30)
    probs = jax.nn.softmax(scores, axis=-1)
    probs_b = probs.astype(jnp.bfloat16)
    attended = jnp.einsum("shqk,skhd->sqhd", probs_b.astype(jnp.float32), value_f)
    return (attended.astype(jnp.bfloat16).reshape(seq_count, length, width), probs, probs_b)


def causal_backward(grad_out, queries, keys, values, attended, probs, probs_b):
    seq_count, length, width = queries.shape
    head_count = width // HD
    shape = (seq_count, length, head_count, HD)
    grad_f = grad_out.astype(jnp.float32).reshape(shape)
    query_f = queries.astype(jnp.float32).reshape(shape)
    key_f = keys.astype(jnp.float32).reshape(shape)
    value_f = values.astype(jnp.float32).reshape(shape)
    attended_f = attended.astype(jnp.float32).reshape(shape)
    value_grad = jnp.einsum("shqk,sqhd->skhd", probs_b.astype(jnp.float32), grad_f).astype(
        jnp.bfloat16
    )
    dprob = jnp.einsum("sqhd,skhd->shqk", grad_f, value_f)
    delta = jnp.einsum("sqhd,sqhd->shq", grad_f, attended_f)
    dscore = (
        (probs * (dprob - delta[..., None]) * HD ** (-0.5)).astype(jnp.bfloat16).astype(jnp.float32)
    )
    query_grad = jnp.einsum("shqk,skhd->sqhd", dscore, key_f).astype(jnp.bfloat16)
    key_grad = jnp.einsum("shqk,sqhd->skhd", dscore, query_f).astype(jnp.bfloat16)
    return (
        query_grad.reshape(seq_count, length, width),
        key_grad.reshape(seq_count, length, width),
        value_grad.reshape(seq_count, length, width),
    )


def spread(block):
    return lax.all_gather(block, "dp", axis=0, tiled=True)


def collect(term_fn, count):
    return lax.psum_scatter(
        term_fn(jnp.int32(0), lax.axis_size("dp") * count), "dp", scatter_dimension=0, tiled=True
    )


def pack(full_rows, selector):
    return jnp.dot(selector, full_rows, preferred_element_type=jnp.float32).astype(jnp.bfloat16)


def unpack(sums, selector):
    return jnp.dot(selector.astype(jnp.float32).T, sums, precision=lax.Precision.HIGHEST)


def over_slots(partial_rows):
    return lax.psum(partial_rows, "sect")


def contract_last(left, right):
    return lax.dot_general(
        left, right, (((1,), (1,)), ((), ())), preferred_element_type=jnp.float32
    )


def contract_first(left, right):
    return lax.dot_general(
        left, right, (((0,), (0,)), ((), ())), preferred_element_type=jnp.float32
    )


def on_device(
    queries, keys, values, residual, labels, slot_modality, gains, up_weight, down_weight, cotangent
):
    attended_block, probs, probs_b = causal_forward(queries, keys, values)
    attended = lax.all_gather(attended_block, "sect", axis=2, tiled=True)
    hidden = (residual.astype(jnp.float32) + attended.astype(jnp.float32)).astype(jnp.bfloat16)[0]
    hidden_f = hidden.astype(jnp.float32)
    length = hidden.shape[0]
    token_labels = labels[0]
    onehot = (token_labels[:, None] == jnp.arange(MODALITIES)[None, :]).astype(jnp.float32)
    gain_rows = jnp.dot(onehot, gains, precision=lax.Precision.HIGHEST)
    inverse = lax.rsqrt(jnp.mean(hidden_f * hidden_f, axis=-1, keepdims=True) + 1e-05)
    normed_f = hidden_f * inverse
    normed = (normed_f * gain_rows).astype(jnp.bfloat16)
    slot_index = lax.axis_index("sect")
    slot_count = lax.axis_size("sect")
    modality = jnp.sum(jnp.where(jnp.arange(slot_count) == slot_index, slot_modality, 0))
    keep_mask = token_labels == modality
    rank_of = jnp.cumsum(keep_mask.astype(jnp.int32)) - 1
    capacity = length // 2
    selector = ((rank_of[None, :] == jnp.arange(capacity)[:, None]) & keep_mask[None, :]).astype(
        jnp.bfloat16
    )
    up_local = up_weight[0]
    down_local = down_weight[0]
    own_rows = pack(normed, selector)
    count = own_rows.shape[0]
    token_rows = spread(own_rows)
    preact = contract_last(token_rows, up_local)
    activated = jax.nn.silu(preact).astype(jnp.bfloat16)

    def output_term(start, number):
        return jnp.dot(activated, down_local, preferred_element_type=jnp.float32)

    ffn = over_slots(unpack(collect(output_term, count), selector))
    output_full = (hidden_f + ffn).astype(jnp.bfloat16)
    quarter = length // slot_count
    output = lax.dynamic_slice_in_dim(output_full, slot_index * quarter, quarter, 0)[None]
    grad_full = cotangent[0]
    grad_rows = spread(pack(grad_full, selector))
    back = contract_last(grad_rows, down_local)
    sigma = jax.nn.sigmoid(preact)
    pre_grad = (back * sigma * (1.0 + preact * (1.0 - sigma))).astype(jnp.bfloat16)
    down_grad = contract_first(activated, grad_rows).astype(jnp.bfloat16)[None]
    up_grad = contract_first(pre_grad, token_rows).astype(jnp.bfloat16)[None]

    def norm_term(start, number):
        return jnp.dot(pre_grad, up_local, preferred_element_type=jnp.float32)

    norm_grad = over_slots(unpack(collect(norm_term, count), selector))
    scaled = norm_grad * gain_rows
    hidden_grad = grad_full.astype(jnp.float32) + inverse * (
        scaled - normed_f * jnp.mean(scaled * normed_f, axis=-1, keepdims=True)
    )
    residual_full = hidden_grad.astype(jnp.bfloat16)
    residual_grad = lax.dynamic_slice_in_dim(residual_full, slot_index * quarter, quarter, 0)[None]
    gain_part = jnp.dot(onehot.T, norm_grad * normed_f, precision=lax.Precision.HIGHEST)
    gain_grad = lax.psum(gain_part, "dp")
    block_width = queries.shape[2]
    grad_block = lax.dynamic_slice_in_dim(residual_full, slot_index * block_width, block_width, 1)[
        None
    ]
    query_grad, key_grad, value_grad = causal_backward(
        grad_block, queries, keys, values, attended_block, probs, probs_b
    )
    return (output, residual_grad, query_grad, key_grad, value_grad, up_grad, down_grad, gain_grad)


def solution(mesh):
    in_specs = (
        P("dp", None, "sect"),
        P("dp", None, "sect"),
        P("dp", None, "sect"),
        P("dp", None, None),
        P("dp", None),
        P(),
        P(),
        P("sect", "dp", None),
        P("sect", "dp", None),
        P("dp", None, None),
    )
    out_specs = (
        P("dp", "sect", None),
        P("dp", "sect", None),
        P("dp", None, "sect"),
        P("dp", None, "sect"),
        P("dp", None, "sect"),
        P("sect", "dp", None),
        P("sect", "dp", None),
        P(),
    )
    return jax.shard_map(
        on_device, mesh=mesh, in_specs=in_specs, out_specs=out_specs, check_vma=False
    )
```

profile of v0, /device:TPU:0, one launch (start us, length us, event | category | flops | bytes accessed | tf_op | source)
XLA Modules:
  0.0 488.7 jit_solution(6223628910422931385)
XLA Ops:
  7.2 0.0 all-gather.3.cloned.1.call-start
  7.2 0.9 copy.58
  8.1 0.9 copy.59
  9.0 0.9 copy.60
  9.8 0.2 fusion.74
  10.0 0.2 convolution_convert_fusion.7
  10.3 12.9 %all_gather.9 = bf16[1,16,8192]{2,1,0:T(8,128)(2,1)S(1)} all-gather(bf16[1,16,2048]{2,1,0:T(8,128)(2,1)S(1)} %copy_bitcast_fusion.3), channel_id=1, replica_groups=mesh['dp'=32,'sect'=4] {'sect'}, dimensions={2}, use_global_device_ids=true | all-gather | bytes 327680 | tf_op jit(solution)/shard_map/all_gather | solution.py:90
  23.1 1.0 fusion.72
  24.1 0.2 multiply_reduce_fusion.1
  24.3 1.3 fusion.69
  25.6 1.3 compare_bitcast_fusion
  26.9 0.1 copy.33
  27.1 0.1 add_reduce_fusion
  27.2 1.1 fusion.50
  28.3 0.9 convolution_convert_fusion.3
  29.2 0.0 all-gather.5.cloned.1.call-start
  29.2 1.8 convolution_convert_fusion.2
  31.0 0.0 reduce-scatter.5.cloned.1.call-start
  31.1 46.4 %all-gather.3.cloned.1.call-done = bf16[256,8192]{1,0:T(8,128)(2,1)} async-done(((bf16[8,8192]{1,0:T(8,128)(2,1)}), bf16[256,8192]{1,0:T(8,128)(2,1)}) %all-gather.3.cloned.1.call-update) | async-done | bytes 4194320 | tf_op jit(solution)/shard_map/all_gather | solution.py:53
  77.4 5.6 %fusion.9 = f32[256,344]{0,1:T(8,128)S(1)} fusion(bf16[256,8192]{1,0:T(8,128)(2,1)} %all-gather.3.cloned.1.call-done, bf16[1,344,8192]{2,1,0:T(8,128)(2,1)} %param.17), kind=kOutput, calls=%fused_computation.13 | convolution fusion | flops 1442840576 | bytes 10182656 | tf_op jit(solution)/shard_map/dot_general | solution.py:75
  83.0 43.0 %all-gather.5.cloned.1.call-done = bf16[256,8192]{1,0:T(8,128)(2,1)} async-done(((bf16[8,8192]{1,0:T(8,128)(2,1)}), bf16[256,8192]{1,0:T(8,128)(2,1)}) %all-gather.5.cloned.1.call-update) | async-done | bytes 4194320 | tf_op jit(solution)/shard_map/all_gather | solution.py:53
  126.0 5.6 %fusion.17 = bf16[256,344]{0,1:T(8,128)(2,1)S(1)} fusion(bf16[256,8192]{1,0:T(8,128)(2,1)} %all-gather.5.cloned.1.call-done, bf16[1,344,8192]{2,1,0:T(8,128)(2,1)} %param.18, f32[256,344]{0,1:T(8,128)S(1)} %fusion.9), kind=kOutput, calls=%fused_computation.17 | convolution fusion | flops 1443633152 | bytes 10358784 | tf_op jit(solution)/shard_map/dot_general | solution.py:75
  131.6 8.2 %fusion.7 = f32[256,8192]{1,0:T(8,128)} fusion(bf16[256,344]{0,1:T(8,128)(2,1)S(1)} %fusion.17, bf16[1,344,8192]{2,1,0:T(8,128)(2,1)} %param.17), kind=kOutput, calls=%fused_computation.11 | convolution fusion | flops 1442840576 | bytes 14200832 | tf_op jit(solution)/shard_map/dot_general | solution.py:133
  139.8 0.0 reduce-scatter.3.cloned.1.call-start
  139.8 8.2 %fusion.5 = f32[256,8192]{1,0:T(8,128)} fusion(bf16[1,344,8192]{2,1,0:T(8,128)(2,1)} %param.18, f32[256,344]{0,1:T(8,128)S(1)} %fusion.9), kind=kOutput, calls=%fused_computation.9 | convolution fusion | flops 1443280896 | bytes 14376960 | tf_op jit(solution)/shard_map/dot_general | solution.py:118
  148.1 0.0 all-reduce.6.cloned.1.call-start
  148.2 83.9 %reduce-scatter.5.cloned.1.call-done = f32[8,8192]{1,0:T(8,128)} async-done(((f32[256,8192]{1,0:T(8,128)}), f32[8,8192]{1,0:T(8,128)}) %reduce-scatter.5.cloned.1.call-update) | async-done | bytes 262160 | tf_op jit(solution)/shard_map/reduce_scatter | solution.py:57
  232.0 2.2 fusion.54
  234.3 93.8 %reduce-scatter.3.cloned.1.call-done = f32[8,8192]{1,0:T(8,128)} async-done(((f32[256,8192]{1,0:T(8,128)}), f32[8,8192]{1,0:T(8,128)}) %reduce-scatter.3.cloned.1.call-update) | async-done | bytes 262160 | tf_op jit(solution)/shard_map/reduce_scatter | solution.py:57
  328.1 2.2 fusion.57
  330.3 0.2 all-reduce.4.cloned.1.call-start
  330.5 6.5 %fusion.1 = bf16[1,344,8192]{2,1,0:T(8,128)(2,1)} fusion(bf16[256,344]{0,1:T(8,128)(2,1)S(1)} %fusion.17, bf16[256,8192]{1,0:T(8,128)(2,1)} %all-gather.3.cloned.1.call-done), kind=kOutput, calls=%fused_computation.3 | convolution fusion | flops 1445658624 | bytes 10006528 | tf_op jit(solution)/shard_map/dot_general | solution.py:81
  337.0 4.2 fusion.2
  341.2 34.4 %all-reduce.6.cloned.1.call-done = (f32[16,8192]{1,0:T(8,128)}, f32[16,8192]{1,0:T(8,128)}) async-done(((f32[16,8192]{1,0:T(8,128)}, f32[16,8192]{1,0:T(8,128)}), (f32[16,8192]{1,0:T(8,128)}, f32[16,8192]{1,0:T(8,128)})) %all-reduce.6.cloned.1.call-update) | async-done | bytes 1048592 | tf_op jit(solution)/shard_map/psum | solution.py:71
  375.6 2.1 fusion.29
  377.7 1.3 multiply_reduce_fusion
  379.0 0.2 add_convert_fusion
  379.3 0.2 fusion.28
  379.5 0.1 multiply_reduce_fusion.2
  379.6 0.2 fusion.25
  379.8 0.2 fusion.27
  379.9 0.7 dynamic-slice_bitcast_fusion
  380.6 0.7 copy_bitcast_fusion
  381.3 1.6 fusion.38
  382.9 0.2 fusion.26
  383.1 0.6 copy.91
  383.8 96.5 %all-reduce.4.cloned.1.call-done = f32[3,8192]{1,0:T(4,128)} async-done(((f32[3,8192]{1,0:T(4,128)}), f32[3,8192]{1,0:T(4,128)}) %all-reduce.4.cloned.1.call-update) | async-done | bytes 98320 | tf_op jit(solution)/shard_map/psum | solution.py:143
  480.3 1.6 copy.95
  (22 shorter events, 0.2 us)
Async XLA Ops:
  7.2 20.0 %copy-start = (f32[3,8192]{1,0:T(4,128)S(1)}, f32[3,8192]{1,0:T(4,128)}, u32[]{:S(2)}) copy-start(f32[3,8192]{1,0:T(4,128)} %param.16) | copy-start | bytes 294916
  7.2 70.3 %all-gather.3.cloned.1.call-start = ((), (), s32[]{:S(2)}) async-start(), calls=%async_computation.2 | async-start | bytes 4325376 | tf_op jit(solution)/shard_map/all_gather | solution.py:53
  29.2 96.8 %all-gather.5.cloned.1.call-start = ((), (), s32[]{:S(2)}) async-start(), calls=%async_computation.4 | async-start | bytes 4325376 | tf_op jit(solution)/shard_map/all_gather | solution.py:53
  31.0 201.0 %reduce-scatter.5.cloned.1.call-start = ((), (), s32[]{:S(2)}) async-start(), calls=%async_computation.5 | async-start | bytes 8650752 | tf_op jit(solution)/shard_map/reduce_scatter | solution.py:57
  139.8 188.3 %reduce-scatter.3.cloned.1.call-start = ((), (), s32[]{:S(2)}) async-start(), calls=%async_computation.3 | async-start | bytes 8650752 | tf_op jit(solution)/shard_map/reduce_scatter | solution.py:57
  148.1 227.5 %all-reduce.6.cloned.1.call-start = ((), (), s32[]{:S(2)}) async-start(), calls=%async_computation.7 | async-start | bytes 2097152 | tf_op jit(solution)/shard_map/psum | solution.py:71
  330.3 150.0 %all-reduce.4.cloned.1.call-start = ((), (), s32[]{:S(2)}) async-start(), calls=%async_computation.6 | async-start | bytes 262144 | tf_op jit(solution)/shard_map/psum | solution.py:143
  330.5 6.5 %copy-start.1 = (bf16[256,8192]{1,0:T(8,128)(2,1)S(1)}, bf16[256,8192]{1,0:T(8,128)(2,1)}, u32[]{:S(2)}) copy-start(bf16[256,8192]{1,0:T(8,128)(2,1)} %all-gather.5.cloned.1.call-done) | copy-start | bytes 12582916
  337.0 38.6 %copy-start.3 = (s32[1,16]{1,0:T(1,128)S(1)}, s32[1,16]{1,0:T(1,128)}, u32[]{:S(2)}) copy-start(s32[1,16]{1,0:T(1,128)} %param.14) | copy-start | bytes 196
  337.0 42.0 %copy-start.2 = (bf16[1,16,8192]{2,1,0:T(8,128)(2,1)S(1)}, bf16[1,16,8192]{2,1,0:T(8,128)(2,1)}, u32[]{:S(2)}) copy-start(bf16[1,16,8192]{2,1,0:T(8,128)(2,1)} %param.19) | copy-start | bytes 786436
Sparse Core Ops, SparseCore 0:
  29.3 48.0 all-gather.2
  80.3 45.6 all-gather.4
  139.9 92.0 reduce-scatter.4
  236.1 91.9 reduce-scatter.2
  330.4 45.1 all-reduce.5
  379.6 100.7 all-reduce.3
where the time goes:
time: 490 us; the launch traced here: 489 us
  waiting for transfers between devices  398 us (81%)
  matrix products  49.6 us (10%)
  between operations  14.3 us (3%)
  blocking collectives  12.9 us (3%)
  other arithmetic  7.23 us (1%)
  local copies, waits for them, and re-layouts  6.27 us (1%)
    reduce_scatter x2, waiting for transfers between devices, collect(): lax.psum_scatter(term_fn(jnp.int32(0), lax.axis_size('dp') * count), 'dp'...  178 us
    psum x1, waiting for transfers between devices, on_device(): gain_grad = lax.psum(gain_part, 'dp')  96.5 us
    all_gather x2, waiting for transfers between devices, spread(): return lax.all_gather(block, 'dp', axis=0, tiled=True)  89.3 us
    psum x1, waiting for transfers between devices, over_slots(): return lax.psum(partial_rows, 'sect')  34.4 us
    all_gather x1, blocking collectives, on_device(): attended = lax.all_gather(attended_block, 'sect', axis=2, tiled=True)  12.9 us
    dot_general x2, matrix products, contract_last(): lax.dot_general(left, right, (((1,), (1,)), ((), ())), preferred_element_...  11.2 us
    dot_general x2, matrix products, contract_first(): lax.dot_general(left, right, (((0,), (0,)), ((), ())), preferred_element_...  10.6 us
  transfers between devices with their start and end apart: 6, of which 6 were waited for; matrix products, arithmetic and copies ran while one was open for 7% of the time, Pallas kernels for 0%

commit v1 on v0

v1 whole, which is shorter than its diff:
```python
import functools

import jax
import jax.numpy as jnp
from jax import lax
from jax.experimental import pallas as pl
from jax.experimental.pallas import tpu as pltpu
from jax.sharding import PartitionSpec as P

HD = 128
MODALITIES = 3
NZ = 4
NX = 4
NC = 2
NS = 4
AXES = ("dp", "sect")
BF = jnp.bfloat16
F32 = jnp.float32
CAP = 8
VMEM = 48 * 1024 * 1024


def causal_forward(queries, keys, values):
    seq_count, length, width = queries.shape
    head_count = width // HD
    query_f = queries.astype(F32).reshape(seq_count, length, head_count, HD)
    key_f = keys.astype(F32).reshape(seq_count, length, head_count, HD)
    value_f = values.astype(F32).reshape(seq_count, length, head_count, HD)
    scores = jnp.einsum("sqhd,skhd->shqk", query_f, key_f) * HD ** (-0.5)
    position = jnp.arange(length)
    causal = position[:, None] >= position[None, :]
    scores = jnp.where(causal, scores, -1e30)
    probs = jax.nn.softmax(scores, axis=-1)
    probs_b = probs.astype(BF)
    attended = jnp.einsum("shqk,skhd->sqhd", probs_b.astype(F32), value_f)
    return (attended.astype(BF).reshape(seq_count, length, width), probs, probs_b)


def causal_backward(grad_out, queries, keys, values, attended, probs, probs_b):
    seq_count, length, width = queries.shape
    head_count = width // HD
    shape = (seq_count, length, head_count, HD)
    grad_f = grad_out.astype(F32).reshape(shape)
    query_f = queries.astype(F32).reshape(shape)
    key_f = keys.astype(F32).reshape(shape)
    value_f = values.astype(F32).reshape(shape)
    attended_f = attended.astype(F32).reshape(shape)
    value_grad = jnp.einsum("shqk,sqhd->skhd", probs_b.astype(F32), grad_f).astype(BF)
    dprob = jnp.einsum("sqhd,skhd->shqk", grad_f, value_f)
    delta = jnp.einsum("sqhd,sqhd->shq", grad_f, attended_f)
    dscore = (probs * (dprob - delta[..., None]) * HD ** (-0.5)).astype(BF).astype(F32)
    query_grad = jnp.einsum("shqk,skhd->sqhd", dscore, key_f).astype(BF)
    key_grad = jnp.einsum("shqk,sqhd->skhd", dscore, query_f).astype(BF)
    return (
        query_grad.reshape(seq_count, length, width),
        key_grad.reshape(seq_count, length, width),
        value_grad.reshape(seq_count, length, width),
    )


def _pairs(move):
    out = []
    for z in range(NZ):
        for x in range(NX):
            for c in range(NC):
                for s in range(NS):
                    z2, x2, c2, s2 = move(z, x, c, s)
                    source = ((z * NX + x) * NC + c) * NS + s
                    target = (((z2 % NZ) * NX + x2 % NX) * NC + c2) * NS + s2 % NS
                    out.append((source, target))
    return out


def along(first, shift):
    def move(z, x, c, s):
        if (c == 0) == first:
            return z, x + shift, c, s
        return z + shift, x, c, s

    return _pairs(move)


def send(block, pairs):
    return lax.ppermute(block, AXES, pairs)


def send_stage(block, first, shift):
    return send(block, along(first, shift))


def swap_core(block):
    return send(block, _pairs(lambda z, x, c, s: (z, x, 1 - c, s)))


def send_sect(block, shift):
    return send(block, _pairs(lambda z, x, c, s: (z, x, c, s + shift)))


def gather_rows(block):
    near = [block] + [send_stage(block, True, k) for k in (1, 2, 3)]
    near = jnp.concatenate(near, axis=0)
    own = [near] + [send_stage(near, False, k) for k in (1, 2, 3)]
    other = [swap_core(piece) for piece in own]
    return own + other


def _params():
    return pltpu.CompilerParams(vmem_limit_bytes=VMEM)


def _nt(left, right):
    return lax.dot_general(left, right, (((1,), (1,)), ((), ())), preferred_element_type=F32)


def _back_kernel(*refs):
    pieces, w_ref, out_ref = refs[:8], refs[8], refs[9]
    rows = jnp.concatenate([p[...] for p in pieces], axis=0)
    part = _nt(w_ref[...], rows)

    @pl.when(pl.program_id(0) == 0)
    def _():
        out_ref[...] = part

    @pl.when(pl.program_id(0) > 0)
    def _():
        out_ref[...] += part


def back_product(pieces, weight, tile=1024):
    hidden, width = weight.shape[1:]
    rows = sum(p.shape[0] for p in pieces)
    return pl.pallas_call(
        _back_kernel,
        grid=(width // tile,),
        in_specs=[pl.BlockSpec((p.shape[0], tile), lambda i: (0, i)) for p in pieces]
        + [pl.BlockSpec((None, hidden, tile), lambda i: (0, 0, i))],
        out_specs=pl.BlockSpec((hidden, rows), lambda i: (0, 0)),
        out_shape=jax.ShapeDtypeStruct((hidden, rows), F32),
        compiler_params=_params(),
        cost_estimate=pl.CostEstimate(
            flops=2 * hidden * rows * width, bytes_accessed=2 * width * (hidden + rows), transcendentals=0
        ),
    )(*pieces, weight)


def _pre_kernel(*refs):
    pieces, w_ref, back_ref = refs[:8], refs[8], refs[9]
    act_t_ref, grad_t_ref, act_ref, grad_ref, acc_ref = refs[10:]
    rows = jnp.concatenate([p[...] for p in pieces], axis=0)
    part = _nt(w_ref[...], rows)

    @pl.when(pl.program_id(0) == 0)
    def _():
        acc_ref[...] = part

    @pl.when(pl.program_id(0) > 0)
    def _():
        acc_ref[...] += part

    @pl.when(pl.program_id(0) == pl.num_programs(0) - 1)
    def _():
        pre = acc_ref[...]
        sigma = jax.nn.sigmoid(pre)
        act = pre * sigma
        grad = back_ref[...] * sigma * (1.0 + pre * (1.0 - sigma))
        act_t_ref[...] = act.astype(BF)
        grad_t_ref[...] = grad.astype(BF)
        act_ref[...] = act.T.astype(BF)
        grad_ref[...] = grad.T.astype(BF)


def pre_product(pieces, weight, back, tile=1024):
    hidden, width = weight.shape[1:]
    rows = sum(p.shape[0] for p in pieces)
    whole = lambda i: (0, 0)
    return pl.pallas_call(
        _pre_kernel,
        grid=(width // tile,),
        in_specs=[pl.BlockSpec((p.shape[0], tile), lambda i: (0, i)) for p in pieces]
        + [pl.BlockSpec((None, hidden, tile), lambda i: (0, 0, i)), pl.BlockSpec((hidden, rows), whole)],
        out_specs=[pl.BlockSpec((hidden, rows), whole)] * 2 + [pl.BlockSpec((rows, hidden), whole)] * 2,
        out_shape=[jax.ShapeDtypeStruct((hidden, rows), BF)] * 2 + [jax.ShapeDtypeStruct((rows, hidden), BF)] * 2,
        scratch_shapes=[pltpu.VMEM((hidden, rows), F32)],
        compiler_params=_params(),
        cost_estimate=pl.CostEstimate(
            flops=2 * hidden * rows * width, bytes_accessed=2 * width * (hidden + rows), transcendentals=hidden * rows
        ),
    )(*pieces, weight, back)


def _other_kernel(left_ref, w_ref, out_ref):
    out_ref[...] = jnp.dot(left_ref[...], w_ref[...], preferred_element_type=F32).astype(BF)


def other_product(left, weight, tile=1024):
    hidden, width = weight.shape[1:]
    half = left.shape[0] // 2
    return pl.pallas_call(
        _other_kernel,
        grid=(width // tile,),
        in_specs=[
            pl.BlockSpec((half, hidden), lambda i: (1, 0)),
            pl.BlockSpec((None, hidden, tile), lambda i: (0, 0, i)),
        ],
        out_specs=pl.BlockSpec((half, tile), lambda i: (0, i)),
        out_shape=jax.ShapeDtypeStruct((half, width), BF),
        compiler_params=_params(),
        cost_estimate=pl.CostEstimate(
            flops=2 * hidden * half * width, bytes_accessed=2 * width * (hidden + half), transcendentals=0
        ),
    )(left, weight)


def _own_kernel(left_ref, w_ref, in_ref, *out_refs):
    total = jnp.dot(left_ref[...], w_ref[...], preferred_element_type=F32)
    total = total + in_ref[...].astype(F32)
    part = total.shape[0] // 4
    for k, out_ref in enumerate(out_refs):
        out_ref[...] = total[k * part : (k + 1) * part].astype(out_ref.dtype)


def own_product(left, weight, arrived, tile=1024):
    hidden, width = weight.shape[1:]
    half = left.shape[0] // 2
    part = half // 4
    return pl.pallas_call(
        _own_kernel,
        grid=(width // tile,),
        in_specs=[
            pl.BlockSpec((half, hidden), lambda i: (0, 0)),
            pl.BlockSpec((None, hidden, tile), lambda i: (0, 0, i)),
            pl.BlockSpec((half, tile), lambda i: (0, i)),
        ],
        out_specs=[pl.BlockSpec((part, tile), lambda i: (0, i))] * 4,
        out_shape=[jax.ShapeDtypeStruct((part, width), F32)] + [jax.ShapeDtypeStruct((part, width), BF)] * 3,
        compiler_params=_params(),
        cost_estimate=pl.CostEstimate(
            flops=2 * hidden * half * width, bytes_accessed=2 * width * (hidden + 2 * half), transcendentals=0
        ),
    )(left, weight, arrived)


def _grads_kernel(*refs):
    cots, rows = refs[:8], refs[8:16]
    act_ref, grad_ref, up_ref, down_out, up_out, gain_out = refs[16:]
    cot = jnp.concatenate([p[...] for p in cots], axis=0)
    down_out[...] = jnp.dot(act_ref[...], cot, preferred_element_type=F32).astype(BF)
    row = jnp.concatenate([p[...] for p in rows], axis=0)
    up_grad = jnp.dot(grad_ref[...], row, preferred_element_type=F32)
    up_out[...] = up_grad.astype(BF)
    gain_out[...] = jnp.sum(up_grad * up_ref[...].astype(F32), axis=0, keepdims=True)


def grad_products(cots, rows, act_t, grad_t, weight, tile=1024):
    hidden, width = weight.shape[1:]
    count = act_t.shape[1]
    whole = lambda i: (0, 0)
    piece_specs = [pl.BlockSpec((p.shape[0], tile), lambda i: (0, i)) for p in cots]
    weight_spec = pl.BlockSpec((None, hidden, tile), lambda i: (0, 0, i))
    return pl.pallas_call(
        _grads_kernel,
        grid=(width // tile,),
        in_specs=piece_specs * 2 + [pl.BlockSpec((hidden, count), whole)] * 2 + [weight_spec],
        out_specs=[weight_spec, weight_spec, pl.BlockSpec((1, tile), lambda i: (0, i))],
        out_shape=[jax.ShapeDtypeStruct(weight.shape, BF)] * 2 + [jax.ShapeDtypeStruct((1, width), F32)],
        compiler_params=_params(),
        cost_estimate=pl.CostEstimate(
            flops=4 * hidden * count * width,
            bytes_accessed=2 * width * (3 * hidden + 2 * count),
            transcendentals=0,
        ),
    )(*cots, *rows, act_t, grad_t, weight)


def scatter_rows(left, weight):
    arrived = swap_core(other_product(left, weight))
    pieces = own_product(left, weight, arrived)
    total = pieces[0]
    for k in (1, 2, 3):
        total = total + send_stage(pieces[k], False, -k).astype(F32)
    blocks = [total[k * CAP : (k + 1) * CAP] for k in range(4)]
    result = blocks[0]
    for k in (1, 2, 3):
        result = result + send_stage(blocks[k].astype(BF), True, -k).astype(F32)
    return result


def sum_over_dp(row):
    moves = (
        lambda z, x, c, s: (z, x, 1 - c, s),
        lambda z, x, c, s: (z, x ^ 1, c, s),
        lambda z, x, c, s: (z, x ^ 2, c, s),
        lambda z, x, c, s: (z ^ 1, x, c, s),
        lambda z, x, c, s: (z ^ 2, x, c, s),
    )
    for move in moves:
        row = row + send(row, _pairs(move))
    return row


def roll_pieces(pieces, index, axis):
    ordered = [pieces[0], pieces[3], pieces[2], pieces[1]]
    size = pieces[0].shape[axis]
    twice = jnp.concatenate(ordered + ordered[:3], axis=axis)
    start = lax.rem(NS - index, NS) * size
    return lax.dynamic_slice_in_dim(twice, start, NS * size, axis)


def on_device(
    queries, keys, values, residual, labels, slot_modality, gains, up_weight, down_weight, cotangent
):
    slot_index = lax.axis_index("sect")
    token_labels = labels[0]
    length = token_labels.shape[0]
    modality = jnp.sum(jnp.where(jnp.arange(NS) == slot_index, slot_modality, 0))
    keep_mask = token_labels == modality
    before = jnp.arange(length)[:, None] >= jnp.arange(length)[None, :]
    rank_of = jnp.sum(jnp.where(before, keep_mask[None, :], False).astype(jnp.int32), axis=1) - 1
    selector = ((rank_of[None, :] == jnp.arange(CAP)[:, None]) & keep_mask[None, :]).astype(BF)

    def pack(rows):
        return jnp.dot(selector, rows, preferred_element_type=F32).astype(BF)

    grad_full = cotangent[0]
    cot_rows = gather_rows(pack(grad_full))

    attended_block, probs, probs_b = causal_forward(queries, keys, values)
    block = attended_block[0]
    attended = roll_pieces([block] + [send_sect(block, k) for k in (1, 2, 3)], slot_index, 1)
    hidden = (residual[0].astype(F32) + attended.astype(F32)).astype(BF)
    hidden_f = hidden.astype(F32)
    onehot = (token_labels[:, None] == jnp.arange(MODALITIES)[None, :]).astype(F32)
    gain_rows = jnp.dot(onehot, gains, precision=lax.Precision.HIGHEST)
    inverse = lax.rsqrt(jnp.mean(hidden_f * hidden_f, axis=-1, keepdims=True) + 1e-05)
    normed = (hidden_f * inverse * gain_rows).astype(BF)
    token_rows = gather_rows(pack(normed))

    back = back_product(cot_rows, down_weight)
    act_t, grad_t, act, grad = pre_product(token_rows, up_weight, back)
    ffn_rows = scatter_rows(act, down_weight)
    norm_rows = scatter_rows(grad, up_weight)
    down_grad, up_grad, gain_part = grad_products(cot_rows, token_rows, act_t, grad_t, up_weight)

    gain_sum = sum_over_dp(gain_part)
    gain_grad = jnp.zeros(gains.shape, F32)
    for k in range(NS):
        part = gain_sum if k == 0 else send_sect(gain_sum, k)
        owner = lax.rem(slot_index - k + NS, NS)
        kind = jnp.sum(jnp.where(jnp.arange(NS) == owner, slot_modality, 0))
        gain_grad = gain_grad + jnp.where(jnp.arange(MODALITIES)[:, None] == kind, part, 0.0)
    gain_grad = gain_grad / gains

    quarter = length // NS
    rows_two = jnp.concatenate([ffn_rows, norm_rows], axis=1).astype(BF)
    spread = jnp.dot(selector.T, rows_two, preferred_element_type=F32).astype(BF)

    def own_quarter(array, shift=0):
        return lax.dynamic_slice_in_dim(array, lax.rem(slot_index + shift, NS) * quarter, quarter, 0)

    total = own_quarter(spread).astype(F32)
    for k in (1, 2, 3):
        total = total + send_sect(own_quarter(spread, k), k).astype(F32)
    width = hidden.shape[1]
    ffn, norm_grad = total[:, :width], total[:, width:]
    hidden_q = own_quarter(hidden).astype(F32)
    output = (hidden_q + ffn).astype(BF)[None]
    normed_q = hidden_q * own_quarter(inverse)
    scaled = norm_grad * own_quarter(gain_rows)
    hidden_grad = own_quarter(grad_full).astype(F32) + own_quarter(inverse) * (
        scaled - normed_q * jnp.mean(scaled * normed_q, axis=-1, keepdims=True)
    )
    residual_grad = hidden_grad.astype(BF)
    block_width = queries.shape[2]

    def columns(shift):
        start = lax.rem(slot_index + shift, NS) * block_width
        return lax.dynamic_slice_in_dim(residual_grad, start, block_width, 1)

    grad_block = roll_pieces([columns(0)] + [send_sect(columns(k), k) for k in (1, 2, 3)], slot_index, 0)[None]
    query_grad, key_grad, value_grad = causal_backward(
        grad_block, queries, keys, values, attended_block, probs, probs_b
    )
    return (
        output,
        residual_grad[None],
        query_grad,
        key_grad,
        value_grad,
        up_grad,
        down_grad,
        gain_grad,
    )


def solution(mesh):
    in_specs = (
        P("dp", None, "sect"),
        P("dp", None, "sect"),
        P("dp", None, "sect"),
        P("dp", None, None),
        P("dp", None),
        P(),
        P(),
        P("sect", "dp", None),
        P("sect", "dp", None),
        P("dp", None, None),
    )
    out_specs = (
        P("dp", "sect", None),
        P("dp", "sect", None),
        P("dp", None, "sect"),
        P("dp", None, "sect"),
        P("dp", None, "sect"),
        P("sect", "dp", None),
        P("sect", "dp", None),
        P(),
    )
    return jax.shard_map(
        on_device, mesh=mesh, in_specs=in_specs, out_specs=out_specs, check_vma=False
    )
```

time: 490 us -> 189 us (0.39)
  waiting for transfers between devices: 398 us -> 38 us
  starting transfers between devices: 0.43 us -> 73.8 us
  Pallas kernels: 0 us -> 53.2 us
  matrix products: 49.6 us -> 4.16 us
  blocking collectives: 12.9 us -> 0 us
  between operations: 14.3 us -> 1.44 us
    reduce_scatter x2 -> x0, waiting for transfers between devices: 178 us -> none  [collect(): lax.psum_scatter(term_fn(jnp.int32(0), lax.axis_size('dp') * count), 'dp'...]
    psum x2 -> x0, waiting for transfers between devices: 131 us -> none  [the longest x1 96.5 us: on_device(): gain_grad = lax.psum(gain_part, 'dp')]
    all_gather x2 -> x0, waiting for transfers between devices: 89.3 us -> none  [spread(): return lax.all_gather(block, 'dp', axis=0, tiled=True)]
    ppermute x0 -> x51, starting transfers between devices: none -> 73.8 us  [send(): return lax.ppermute(block, AXES, pairs)]
    pallas_call x0 -> x7, Pallas kernels: none -> 53.2 us  [the longest x2 13.7 us: own_product(): pl.pallas_call(_own_kernel, grid=(width // tile,), in_specs=[pl.BlockSpec...]
    dot_general x15 -> x7, matrix products: 48.2 us -> 2.45 us  [the longest x2 1.36 us: pack(): return jnp.dot(selector, rows, preferred_element_type=F32).astype(BF)]
    ppermute x0 -> x51, waiting for transfers between devices: none -> 38 us  [send(): return lax.ppermute(block, AXES, pairs)]
    all_gather x1 -> x0, blocking collectives: 12.9 us -> none  [on_device(): attended = lax.all_gather(attended_block, 'sect', axis=2, tiled=True)]
  transfers between devices with their start and end apart: 6 -> 51, of which waited for: 6 -> 14; matrix products, arithmetic and copies ran while one was open for 7% -> 8% of each run, Pallas kernels for 0% -> 21%
where the time goes in v1:
time: 189 us; the launch traced here: 188 us
  starting transfers between devices  73.8 us (39%)
  Pallas kernels  53.2 us (28%)
  waiting for transfers between devices  38 us (20%)
  other arithmetic  11.7 us (6%)
  local copies, waits for them, and re-layouts  5.64 us (3%)
  matrix products  4.16 us (2%)
    ppermute x51, starting transfers between devices, send(): return lax.ppermute(block, AXES, pairs)  73.8 us
    ppermute x51, waiting for transfers between devices, send(): return lax.ppermute(block, AXES, pairs)  38 us
    pallas_call x2, Pallas kernels, own_product(): pl.pallas_call(_own_kernel, grid=(width // tile,), in_specs=[pl.BlockSpec...  13.7 us
    pallas_call x2, Pallas kernels, other_product(): pl.pallas_call(_other_kernel, grid=(width // tile,), in_specs=[pl.BlockSp...  13.7 us
    pallas_call x1, Pallas kernels, grad_products(): pl.pallas_call(_grads_kernel, grid=(width // tile,), in_specs=piece_specs...  11 us
    pallas_call x1, Pallas kernels, pre_product(): pl.pallas_call(_pre_kernel, grid=(width // tile,), in_specs=[pl.BlockSpec...  7.82 us
    pallas_call x1, Pallas kernels, back_product(): pl.pallas_call(_back_kernel, grid=(width // tile,), in_specs=[pl.BlockSpe...  7.08 us
    unnamed x66, local copies, waits for them, and re-layouts  3.82 us
  transfers between devices with their start and end apart: 51, of which 14 were waited for; matrix products, arithmetic and copies ran while one was open for 8% of the time, Pallas kernels for 21%

profile of v1, /device:TPU:0, one launch (start us, length us, event | category | flops | bytes accessed | tf_op | source)
XLA Modules:
  0.0 187.9 jit_solution(11490340749201403293)
XLA Ops:
  3.8 1.7 collective-permute-start.2
  5.5 2.9 %collective-permute-start.1 = (bf16[16,2048]{1,0:T(8,128)(2,1)S(1)}, bf16[16,2048]{1,0:T(8,128)(2,1)S(1)}, u32[]{:S(2)}, u32[]{:S(2)}) collective-permute-start(bf16[16,2048]{1,0:T(8,128)(2,1)S(1)} %bitcast.105), channel_id=1, source_target_pairs={{0,2},{1,3},{2,0},{3,1},{4,6},{5,7},{6,4},{7,5},{8,10},{9,11},{10,... | collective-permute-start | bytes 196616 | tf_op jit(solution)/shard_map/ppermute | solution.py:84
  8.4 1.3 collective-permute-start
  9.8 1.4 fusion.59
  11.2 1.3 compare_bitcast_fusion
  13.7 2.8 %collective-permute-start.15 = (bf16[8,8192]{1,0:T(8,128)(2,1)S(1)}, bf16[8,8192]{1,0:T(8,128)(2,1)S(1)}, u32[]{:S(2)}, u32[]{:S(2)}) collective-permute-start(bf16[8,8192]{1,0:T(8,128)(2,1)S(1)} %convolution_convert_fusion.1), channel_id=1, source_target_pairs={{0,24},{1,25},{2,26},{3,27},{4,100},{5,101},{6,102},{7,103},{8,0},... | collective-permute-start | bytes 393224 | tf_op jit(solution)/shard_map/ppermute | solution.py:84
  17.4 1.3 fusion.46
  21.3 2.4 %collective-permute-start.5 = (bf16[8,8192]{1,0:T(8,128)(2,1)S(1)}, bf16[8,8192]{1,0:T(8,128)(2,1)S(1)}, u32[]{:S(2)}, u32[]{:S(2)}) collective-permute-start(bf16[8,8192]{1,0:T(8,128)(2,1)S(1)} %convolution_convert_fusion.2), channel_id=1, source_target_pairs={{0,24},{1,25},{2,26},{3,27},{4,100},{5,101},{6,102},{7,103},{8,0},... | collective-permute-start | bytes 393224 | tf_op jit(solution)/shard_map/ppermute | solution.py:84
  23.7 1.5 collective-permute-start.4
  25.4 4.1 %collective-permute-start.18 = (bf16[32,8192]{1,0:T(8,128)(2,1)S(1)}, bf16[32,8192]{1,0:T(8,128)(2,1)S(1)}, u32[]{:S(2)}, u32[]{:S(2)}) collective-permute-start(bf16[32,8192]{1,0:T(8,128)(2,1)S(1)} %pad_maximum_fusion.1.refs_0_), channel_id=1, source_target_pairs={{0,96},{1,97},{2,98},{3,99},{4,28},{5,29},{6,30},{7,31},{8,104},{9... | collective-permute-start | bytes 1572872 | tf_op jit(solution)/shard_map/ppermute | solution.py:84
  29.5 2.0 %collective-permute-start.17 = (bf16[32,8192]{1,0:T(8,128)(2,1)S(1)}, bf16[32,8192]{1,0:T(8,128)(2,1)S(1)}, u32[]{:S(2)}, u32[]{:S(2)}) collective-permute-start(bf16[32,8192]{1,0:T(8,128)(2,1)S(1)} %pad_maximum_fusion.1.refs_0_), channel_id=1, source_target_pairs={{0,64},{1,65},{2,66},{3,67},{4,20},{5,21},{6,22},{7,23},{8,72},{9,... | collective-permute-start | bytes 1572872 | tf_op jit(solution)/shard_map/ppermute | solution.py:84
  32.6 3.2 %collective-permute-start.8 = (bf16[32,8192]{1,0:T(8,128)(2,1)S(1)}, bf16[32,8192]{1,0:T(8,128)(2,1)S(1)}, u32[]{:S(2)}, u32[]{:S(2)}) collective-permute-start(bf16[32,8192]{1,0:T(8,128)(2,1)S(1)} %pad_maximum_fusion.refs_0_.refs_8_), channel_id=1, source_target_pairs={{0,96},{1,97},{2,98},{3,99},{4,28},{5,29},{6,30},{7,31},{8,104},{9... | collective-permute-start | bytes 1572872 | tf_op jit(solution)/shard_map/ppermute | solution.py:84
  36.2 5.6 %collective-permute-done.18.refs_3_ = bf16[32,8192]{1,0:T(8,128)(2,1)S(1)} collective-permute-done((bf16[32,8192]{1,0:T(8,128)(2,1)S(1)}, bf16[32,8192]{1,0:T(8,128)(2,1)S(1)}, u32[]{:S(2)}, u32[]{:S(2)}) %collective-permute-start.18) | collective-permute-done | bytes 524320 | tf_op jit(solution)/shard_map/ppermute | solution.py:84
  41.8 4.0 %collective-permute-done.16.refs_1_ = bf16[32,8192]{1,0:T(8,128)(2,1)S(1)} collective-permute-done((bf16[32,8192]{1,0:T(8,128)(2,1)S(1)}, bf16[32,8192]{1,0:T(8,128)(2,1)S(1)}, u32[]{:S(2)}, u32[]{:S(2)}) %collective-permute-start.16) | collective-permute-done | bytes 524320 | tf_op jit(solution)/shard_map/ppermute | solution.py:84
  45.8 7.2 %collective-permute-done.8.refs_3_.refs_11_ = bf16[32,8192]{1,0:T(8,128)(2,1)S(1)} collective-permute-done((bf16[32,8192]{1,0:T(8,128)(2,1)S(1)}, bf16[32,8192]{1,0:T(8,128)(2,1)S(1)}, u32[]{:S(2)}, u32[]{:S(2)}) %collective-permute-start.8) | collective-permute-done | bytes 524320 | tf_op jit(solution)/shard_map/ppermute | solution.py:84
  53.6 3.5 %collective-permute-done.6.refs_1_.refs_9_ = bf16[32,8192]{1,0:T(8,128)(2,1)S(1)} collective-permute-done((bf16[32,8192]{1,0:T(8,128)(2,1)S(1)}, bf16[32,8192]{1,0:T(8,128)(2,1)S(1)}, u32[]{:S(2)}, u32[]{:S(2)}) %collective-permute-start.6) | collective-permute-done | bytes 524320 | tf_op jit(solution)/shard_map/ppermute | solution.py:84
  57.7 7.1 %shard_map.161.refs_9_ = f32[344,256]{1,0:T(8,128)S(1)} custom-call(bf16[32,8192]{1,0:T(8,128)(2,1)S(1)} %pad_maximum_fusion.1.refs_0_, bf16[32,8192]{1,0:T(8,128)(2,1)S(1)} %collective-permute-done.16.refs_1_, bf16[32,8192]{1,0:T(8,128)(2,1)S(1)} %collective-permute-done.17.refs_2_, bf16[32,8192]{1,0:T(8,128)(2,1)S(1)} %collective-permute-done.18.refs_3_, ...), custom_call_target="tpu_custom_call" | custom-call | flops 1442840576 | bytes 9830400 | tf_op jit(solution)/shard_map/pallas_call | solution.py:132
  64.9 7.8 %shard_map.162 = (bf16[344,256]{1,0:T(8,128)(2,1)S(1)}, bf16[344,256]{1,0:T(8,128)(2,1)S(1)}, bf16[256,344]{1,0:T(8,128)(2,1)S(1)}, bf16[256,344]{1,0:T(8,128)(2,1)S(1)}) custom-call(bf16[32,8192]{1,0:T(8,128)(2,1)S(1)} %pad_maximum_fusion.refs_0_.refs_8_, bf16[32,8192]{1,0:T(8,128)(2,1)S(1)} %collective-permute-done.6.refs_1_.refs_9_, ...), custom_call_target="tpu_custom_call" | custom-call | flops 1442840576 | bytes 9830400 | tf_op jit(solution)/shard_map/pallas_call | solution.py:176
  72.7 6.2 %shard_map.165 = bf16[128,8192]{1,0:T(8,128)(2,1)S(1)} custom-call(bf16[256,344]{1,0:T(8,128)(2,1)S(1)} %get-tuple-element.28.left_ref, bf16[1,344,8192]{2,1,0:T(8,128)(2,1)} %refs_18_.1), custom_call_target="tpu_custom_call" | custom-call | flops 721420288 | bytes 7733248 | tf_op jit(solution)/shard_map/pallas_call | solution.py:198
  79.5 7.5 %shard_map.163 = bf16[128,8192]{1,0:T(8,128)(2,1)} custom-call(bf16[256,344]{1,0:T(8,128)(2,1)S(1)} %get-tuple-element.23.left_ref, bf16[1,344,8192]{2,1,0:T(8,128)(2,1)} %w_ref.5), custom_call_target="tpu_custom_call" | custom-call | flops 721420288 | bytes 7733248 | tf_op jit(solution)/shard_map/pallas_call | solution.py:198
  87.0 7.4 %shard_map.166 = (f32[32,8192]{1,0:T(8,128)S(1)}, bf16[32,8192]{1,0:T(8,128)(2,1)}, bf16[32,8192]{1,0:T(8,128)(2,1)}, bf16[32,8192]{1,0:T(8,128)(2,1)}) custom-call(bf16[256,344]{1,0:T(8,128)(2,1)S(1)} %get-tuple-element.28.left_ref, bf16[1,344,8192]{2,1,0:T(8,128)(2,1)} %refs_18_.1, bf16[128,8192]{1,0:T(8,128)(2,1)S(1)} %collective-permute-done.30.in_ref), custom_call_target="tpu_custom_call" | custom-call | flops 721420288 | bytes 9830400 | tf_op jit(solution)/shard_map/pallas_call | solution.py:226
  95.5 2.1 %collective-permute-start.31 = (bf16[32,8192]{1,0:T(8,128)(2,1)}, bf16[32,8192]{1,0:T(8,128)(2,1)}, u32[]{:S(2)}, u32[]{:S(2)}) collective-permute-start(bf16[32,8192]{1,0:T(8,128)(2,1)} %get-tuple-element.30), channel_id=1, source_target_pairs={{0,96},{1,97},{2,98},{3,99},{4,28},{5,29},{6,30},{7,31},{8,104},{9... | collective-permute-start | bytes 1572872 | tf_op jit(solution)/shard_map/ppermute | solution.py:84
  98.9 11.0 %shard_map.167 = (bf16[1,344,8192]{2,1,0:T(8,128)(2,1)}, bf16[1,344,8192]{2,1,0:T(8,128)(2,1)}, f32[1,8192]{1,0:T(1,128)S(1)}) custom-call(bf16[32,8192]{1,0:T(8,128)(2,1)S(1)} %pad_maximum_fusion.1.refs_0_, bf16[32,8192]{1,0:T(8,128)(2,1)S(1)} %collective-permute-done.16.refs_1_, bf16[32,8192]{1,0:T(8,128)(2,1)S(1)} %collective-permute-done.17.refs_2_, ...), custom_call_target="tpu_custom_call" | custom-call | flops 2885681152 | bytes 25296896 | tf_op jit(solution)/shard_map/pallas_call | solution.py:260
  111.3 2.4 %collective-permute-start.44 = (f32[1,8192]{1,0:T(1,128)S(1)}, f32[1,8192]{1,0:T(1,128)S(1)}, u32[]{:S(2)}, u32[]{:S(2)}) collective-permute-start(f32[1,8192]{1,0:T(1,128)S(1)} %add.191), channel_id=1, source_target_pairs={{0,8},{1,9},{2,10},{3,11},{4,12},{5,13},{6,14},{7,15},{8,0},{9,1},... | collective-permute-start | bytes 98312 | tf_op jit(solution)/shard_map/ppermute | solution.py:84
  113.8 1.9 %collective-permute-done.44 = f32[1,8192]{1,0:T(1,128)S(1)} collective-permute-done((f32[1,8192]{1,0:T(1,128)S(1)}, f32[1,8192]{1,0:T(1,128)S(1)}, u32[]{:S(2)}, u32[]{:S(2)}) %collective-permute-start.44) | collective-permute-done | bytes 32800 | tf_op jit(solution)/shard_map/ppermute | solution.py:84
  115.7 2.4 %collective-permute-start.45 = (f32[1,8192]{1,0:T(1,128)S(1)}, f32[1,8192]{1,0:T(1,128)S(1)}, u32[]{:S(2)}, u32[]{:S(2)}) collective-permute-start(f32[1,8192]{1,0:T(1,128)S(1)} %add.192), channel_id=1, source_target_pairs={{0,16},{1,17},{2,18},{3,19},{4,20},{5,21},{6,22},{7,23},{8,24},{9,... | collective-permute-start | bytes 98312 | tf_op jit(solution)/shard_map/ppermute | solution.py:84
  118.1 3.1 %collective-permute-done.45 = f32[1,8192]{1,0:T(1,128)S(1)} collective-permute-done((f32[1,8192]{1,0:T(1,128)S(1)}, f32[1,8192]{1,0:T(1,128)S(1)}, u32[]{:S(2)}, u32[]{:S(2)}) %collective-permute-start.45) | collective-permute-done | bytes 32800 | tf_op jit(solution)/shard_map/ppermute | solution.py:84
  121.2 1.8 collective-permute-start.46
  123.0 6.3 %shard_map.164 = (f32[32,8192]{1,0:T(8,128)S(1)}, bf16[32,8192]{1,0:T(8,128)(2,1)S(1)}, bf16[32,8192]{1,0:T(8,128)(2,1)S(1)}, bf16[32,8192]{1,0:T(8,128)(2,1)S(1)}) custom-call(bf16[256,344]{1,0:T(8,128)(2,1)S(1)} %get-tuple-element.23.left_ref, bf16[1,344,8192]{2,1,0:T(8,128)(2,1)} %w_ref.5, bf16[128,8192]{1,0:T(8,128)(2,1)S(1)} %collective-permute-done.23.in_ref), custom_call_target="tpu_custom_call" | custom-call | flops 721420288 | bytes 9830400 | tf_op jit(solution)/shard_map/pallas_call | solution.py:226
  130.5 1.3 collective-permute-start.25
  132.5 1.6 fusion.67
  134.2 3.7 %collective-permute-start.34 = (bf16[8,8192]{1,0:T(8,128)(2,1)S(1)}, bf16[8,8192]{1,0:T(8,128)(2,1)S(1)}, u32[]{:S(2)}, u32[]{:S(2)}) collective-permute-start(bf16[8,8192]{1,0:T(8,128)(2,1)S(1)} %get-tuple-element.57), channel_id=1, source_target_pairs={{0,24},{1,25},{2,26},{3,27},{4,100},{5,101},{6,102},{7,103},{8,0},... | collective-permute-start | bytes 393224 | tf_op jit(solution)/shard_map/ppermute | solution.py:84
  137.9 2.1 %collective-permute-done.24 = bf16[32,8192]{1,0:T(8,128)(2,1)S(1)} collective-permute-done((bf16[32,8192]{1,0:T(8,128)(2,1)S(1)}, bf16[32,8192]{1,0:T(8,128)(2,1)S(1)}, u32[]{:S(2)}, u32[]{:S(2)}) %collective-permute-start.24) | collective-permute-done | bytes 524320 | tf_op jit(solution)/shard_map/ppermute | solution.py:84
  140.0 6.2 %collective-permute-start.36 = (bf16[8,8192]{1,0:T(8,128)(2,1)S(1)}, bf16[8,8192]{1,0:T(8,128)(2,1)S(1)}, u32[]{:S(2)}, u32[]{:S(2)}) collective-permute-start(bf16[8,8192]{1,0:T(8,128)(2,1)S(1)} %get-tuple-element.58), channel_id=1, source_target_pairs={{0,8},{1,9},{2,10},{3,11},{4,36},{5,37},{6,38},{7,39},{8,16},{9,17... | collective-permute-start | bytes 393224 | tf_op jit(solution)/shard_map/ppermute | solution.py:84
  146.2 2.8 %collective-permute-start.35 = (bf16[8,8192]{1,0:T(8,128)(2,1)S(1)}, bf16[8,8192]{1,0:T(8,128)(2,1)S(1)}, u32[]{:S(2)}, u32[]{:S(2)}) collective-permute-start(bf16[8,8192]{1,0:T(8,128)(2,1)S(1)} %get-tuple-element.59), channel_id=1, source_target_pairs={{0,16},{1,17},{2,18},{3,19},{4,68},{5,69},{6,70},{7,71},{8,24},{9,... | collective-permute-start | bytes 393224 | tf_op jit(solution)/shard_map/ppermute | solution.py:84
  149.3 2.5 %collective-permute-start.27 = (bf16[8,8192]{1,0:T(8,128)(2,1)S(1)}, bf16[8,8192]{1,0:T(8,128)(2,1)S(1)}, u32[]{:S(2)}, u32[]{:S(2)}) collective-permute-start(bf16[8,8192]{1,0:T(8,128)(2,1)S(1)} %get-tuple-element.54), channel_id=1, source_target_pairs={{0,24},{1,25},{2,26},{3,27},{4,100},{5,101},{6,102},{7,103},{8,0},... | collective-permute-start | bytes 393224 | tf_op jit(solution)/shard_map/ppermute | solution.py:84
  152.7 3.2 %collective-permute-start.28 = (bf16[8,8192]{1,0:T(8,128)(2,1)S(1)}, bf16[8,8192]{1,0:T(8,128)(2,1)S(1)}, u32[]{:S(2)}, u32[]{:S(2)}) collective-permute-start(bf16[8,8192]{1,0:T(8,128)(2,1)S(1)} %get-tuple-element.56), channel_id=1, source_target_pairs={{0,16},{1,17},{2,18},{3,19},{4,68},{5,69},{6,70},{7,71},{8,24},{9,... | collective-permute-start | bytes 393224 | tf_op jit(solution)/shard_map/ppermute | solution.py:84
  156.0 2.0 %collective-permute-done.29 = bf16[8,8192]{1,0:T(8,128)(2,1)S(1)} collective-permute-done((bf16[8,8192]{1,0:T(8,128)(2,1)S(1)}, bf16[8,8192]{1,0:T(8,128)(2,1)S(1)}, u32[]{:S(2)}, u32[]{:S(2)}) %collective-permute-start.29) | collective-permute-done | bytes 131104 | tf_op jit(solution)/shard_map/ppermute | solution.py:84
  158.0 2.2 %collective-permute-done.28 = bf16[8,8192]{1,0:T(8,128)(2,1)S(1)} collective-permute-done((bf16[8,8192]{1,0:T(8,128)(2,1)S(1)}, bf16[8,8192]{1,0:T(8,128)(2,1)S(1)}, u32[]{:S(2)}, u32[]{:S(2)}) %collective-permute-start.28) | collective-permute-done | bytes 131104 | tf_op jit(solution)/shard_map/ppermute | solution.py:84
  161.6 2.6 %collective-permute-start.39 = (bf16[4,16384]{1,0:T(4,128)(2,1)S(1)}, bf16[4,16384]{1,0:T(4,128)(2,1)S(1)}, u32[]{:S(2)}, u32[]{:S(2)}) collective-permute-start(bf16[4,16384]{1,0:T(4,128)(2,1)S(1)} %get-tuple-element.52), channel_id=1, source_target_pairs={{0,3},{1,0},{2,1},{3,2},{4,7},{5,4},{6,5},{7,6},{8,11},{9,8},{10,9... | collective-permute-start | bytes 393224 | tf_op jit(solution)/shard_map/ppermute | solution.py:84
  164.2 1.3 iota_compare_fusion.6
  165.6 1.3 collective-permute-start.47
  168.2 2.8 %collective-permute-done.47 = f32[1,8192]{1,0:T(1,128)S(1)} collective-permute-done((f32[1,8192]{1,0:T(1,128)S(1)}, f32[1,8192]{1,0:T(1,128)S(1)}, u32[]{:S(2)}, u32[]{:S(2)}) %collective-permute-start.47) | collective-permute-done | bytes 32800 | tf_op jit(solution)/shard_map/ppermute | solution.py:84
  171.1 2.2 %collective-permute-start.50 = (f32[1,8192]{1,0:T(1,128)S(1)}, f32[1,8192]{1,0:T(1,128)S(1)}, u32[]{:S(2)}, u32[]{:S(2)}) collective-permute-start(f32[1,8192]{1,0:T(1,128)S(1)} %add.195), channel_id=1, source_target_pairs={{0,3},{1,0},{2,1},{3,2},{4,7},{5,4},{6,5},{7,6},{8,11},{9,8},{10,9... | collective-permute-start | bytes 98312 | tf_op jit(solution)/shard_map/ppermute | solution.py:84
  173.3 1.5 collective-permute-start.49
  174.8 1.3 collective-permute-start.48
  176.6 1.7 fusion.32
  179.0 2.7 %collective-permute-start.41 = (bf16[4,2048]{1,0:T(4,128)(2,1)S(1)}, bf16[4,2048]{1,0:T(4,128)(2,1)S(1)}, u32[]{:S(2)}, u32[]{:S(2)}) collective-permute-start(bf16[4,2048]{1,0:T(4,128)(2,1)S(1)} %get-tuple-element.63), channel_id=1, source_target_pairs={{0,2},{1,3},{2,0},{3,1},{4,6},{5,7},{6,4},{7,5},{8,10},{9,11},{10,... | collective-permute-start | bytes 49160 | tf_op jit(solution)/shard_map/ppermute | solution.py:84
  (174 shorter events, 27.9 us)
Async XLA Ops:
  3.8 16.0 %collective-permute-start.2 = (bf16[16,2048]{1,0:T(8,128)(2,1)S(1)}, bf16[16,2048]{1,0:T(8,128)(2,1)S(1)}, u32[]{:S(2)}, u32[]{:S(2)}) collective-permute-start(bf16[16,2048]{1,0:T(8,128)(2,1)S(1)} %bitcast.104), channel_id=1, source_target_pairs={{0,1},{1,2},{2,3},{3,0},{4,5},{5,6},{6,7},{7,4},{8,9},{9,10},{10,1... | collective-permute-start | bytes 196616 | tf_op jit(solution)/shard_map/ppermute | solution.py:84
  5.5 14.2 %collective-permute-start.1 = (bf16[16,2048]{1,0:T(8,128)(2,1)S(1)}, bf16[16,2048]{1,0:T(8,128)(2,1)S(1)}, u32[]{:S(2)}, u32[]{:S(2)}) collective-permute-start(bf16[16,2048]{1,0:T(8,128)(2,1)S(1)} %bitcast.105), channel_id=1, source_target_pairs={{0,2},{1,3},{2,0},{3,1},{4,6},{5,7},{6,4},{7,5},{8,10},{9,11},{10,... | collective-permute-start | bytes 196616 | tf_op jit(solution)/shard_map/ppermute | solution.py:84
  8.4 10.3 %collective-permute-start = (bf16[16,2048]{1,0:T(8,128)(2,1)S(1)}, bf16[16,2048]{1,0:T(8,128)(2,1)S(1)}, u32[]{:S(2)}, u32[]{:S(2)}) collective-permute-start(bf16[16,2048]{1,0:T(8,128)(2,1)S(1)} %bitcast.106), channel_id=1, source_target_pairs={{0,3},{1,0},{2,1},{3,2},{4,7},{5,4},{6,5},{7,6},{8,11},{9,8},{10,9... | collective-permute-start | bytes 196616 | tf_op jit(solution)/shard_map/ppermute | solution.py:84
  13.7 11.5 %collective-permute-start.15 = (bf16[8,8192]{1,0:T(8,128)(2,1)S(1)}, bf16[8,8192]{1,0:T(8,128)(2,1)S(1)}, u32[]{:S(2)}, u32[]{:S(2)}) collective-permute-start(bf16[8,8192]{1,0:T(8,128)(2,1)S(1)} %convolution_convert_fusion.1), channel_id=1, source_target_pairs={{0,24},{1,25},{2,26},{3,27},{4,100},{5,101},{6,102},{7,103},{8,0},... | collective-permute-start | bytes 393224 | tf_op jit(solution)/shard_map/ppermute | solution.py:84
  16.5 8.7 %collective-permute-start.14 = (bf16[8,8192]{1,0:T(8,128)(2,1)S(1)}, bf16[8,8192]{1,0:T(8,128)(2,1)S(1)}, u32[]{:S(2)}, u32[]{:S(2)}) collective-permute-start(bf16[8,8192]{1,0:T(8,128)(2,1)S(1)} %convolution_convert_fusion.1), channel_id=1, source_target_pairs={{0,16},{1,17},{2,18},{3,19},{4,68},{5,69},{6,70},{7,71},{8,24},{9,... | collective-permute-start | bytes 393224 | tf_op jit(solution)/shard_map/ppermute | solution.py:84
  18.8 6.5 %collective-permute-start.13 = (bf16[8,8192]{1,0:T(8,128)(2,1)S(1)}, bf16[8,8192]{1,0:T(8,128)(2,1)S(1)}, u32[]{:S(2)}, u32[]{:S(2)}) collective-permute-start(bf16[8,8192]{1,0:T(8,128)(2,1)S(1)} %convolution_convert_fusion.1), channel_id=1, source_target_pairs={{0,8},{1,9},{2,10},{3,11},{4,36},{5,37},{6,38},{7,39},{8,16},{9,17... | collective-permute-start | bytes 393224 | tf_op jit(solution)/shard_map/ppermute | solution.py:84
  21.3 8.2 %collective-permute-start.5 = (bf16[8,8192]{1,0:T(8,128)(2,1)S(1)}, bf16[8,8192]{1,0:T(8,128)(2,1)S(1)}, u32[]{:S(2)}, u32[]{:S(2)}) collective-permute-start(bf16[8,8192]{1,0:T(8,128)(2,1)S(1)} %convolution_convert_fusion.2), channel_id=1, source_target_pairs={{0,24},{1,25},{2,26},{3,27},{4,100},{5,101},{6,102},{7,103},{8,0},... | collective-permute-start | bytes 393224 | tf_op jit(solution)/shard_map/ppermute | solution.py:84
  23.7 7.8 %collective-permute-start.4 = (bf16[8,8192]{1,0:T(8,128)(2,1)S(1)}, bf16[8,8192]{1,0:T(8,128)(2,1)S(1)}, u32[]{:S(2)}, u32[]{:S(2)}) collective-permute-start(bf16[8,8192]{1,0:T(8,128)(2,1)S(1)} %convolution_convert_fusion.2), channel_id=1, source_target_pairs={{0,16},{1,17},{2,18},{3,19},{4,68},{5,69},{6,70},{7,71},{8,24},{9,... | collective-permute-start | bytes 393224 | tf_op jit(solution)/shard_map/ppermute | solution.py:84
  25.2 7.3 %collective-permute-start.3 = (bf16[8,8192]{1,0:T(8,128)(2,1)S(1)}, bf16[8,8192]{1,0:T(8,128)(2,1)S(1)}, u32[]{:S(2)}, u32[]{:S(2)}) collective-permute-start(bf16[8,8192]{1,0:T(8,128)(2,1)S(1)} %convolution_convert_fusion.2), channel_id=1, source_target_pairs={{0,8},{1,9},{2,10},{3,11},{4,36},{5,37},{6,38},{7,39},{8,16},{9,17... | collective-permute-start | bytes 393224 | tf_op jit(solution)/shard_map/ppermute | solution.py:84
  25.3 10.4 %collective-permute-start.19 = (bf16[32,8192]{1,0:T(8,128)(2,1)S(1)}, bf16[32,8192]{1,0:T(8,128)(2,1)S(1)}, u32[]{:S(2)}, u32[]{:S(2)}) collective-permute-start(bf16[32,8192]{1,0:T(8,128)(2,1)S(1)} %pad_maximum_fusion.1.refs_0_), channel_id=1, source_target_pairs={{0,4},{1,5},{2,6},{3,7},{4,0},{5,1},{6,2},{7,3},{8,12},{9,13},{10,... | collective-permute-start | bytes 1572872 | tf_op jit(solution)/shard_map/ppermute | solution.py:84
  25.4 16.4 %collective-permute-start.18 = (bf16[32,8192]{1,0:T(8,128)(2,1)S(1)}, bf16[32,8192]{1,0:T(8,128)(2,1)S(1)}, u32[]{:S(2)}, u32[]{:S(2)}) collective-permute-start(bf16[32,8192]{1,0:T(8,128)(2,1)S(1)} %pad_maximum_fusion.1.refs_0_), channel_id=1, source_target_pairs={{0,96},{1,97},{2,98},{3,99},{4,28},{5,29},{6,30},{7,31},{8,104},{9... | collective-permute-start | bytes 1572872 | tf_op jit(solution)/shard_map/ppermute | solution.py:84
  29.5 12.3 %collective-permute-start.17 = (bf16[32,8192]{1,0:T(8,128)(2,1)S(1)}, bf16[32,8192]{1,0:T(8,128)(2,1)S(1)}, u32[]{:S(2)}, u32[]{:S(2)}) collective-permute-start(bf16[32,8192]{1,0:T(8,128)(2,1)S(1)} %pad_maximum_fusion.1.refs_0_), channel_id=1, source_target_pairs={{0,64},{1,65},{2,66},{3,67},{4,20},{5,21},{6,22},{7,23},{8,72},{9,... | collective-permute-start | bytes 1572872 | tf_op jit(solution)/shard_map/ppermute | solution.py:84
  31.5 14.3 %collective-permute-start.16 = (bf16[32,8192]{1,0:T(8,128)(2,1)S(1)}, bf16[32,8192]{1,0:T(8,128)(2,1)S(1)}, u32[]{:S(2)}, u32[]{:S(2)}) collective-permute-start(bf16[32,8192]{1,0:T(8,128)(2,1)S(1)} %pad_maximum_fusion.1.refs_0_), channel_id=1, source_target_pairs={{0,32},{1,33},{2,34},{3,35},{4,12},{5,13},{6,14},{7,15},{8,40},{9,... | collective-permute-start | bytes 1572872 | tf_op jit(solution)/shard_map/ppermute | solution.py:84
  32.6 20.5 %collective-permute-start.8 = (bf16[32,8192]{1,0:T(8,128)(2,1)S(1)}, bf16[32,8192]{1,0:T(8,128)(2,1)S(1)}, u32[]{:S(2)}, u32[]{:S(2)}) collective-permute-start(bf16[32,8192]{1,0:T(8,128)(2,1)S(1)} %pad_maximum_fusion.refs_0_.refs_8_), channel_id=1, source_target_pairs={{0,96},{1,97},{2,98},{3,99},{4,28},{5,29},{6,30},{7,31},{8,104},{9... | collective-permute-start | bytes 1572872 | tf_op jit(solution)/shard_map/ppermute | solution.py:84
  35.7 17.3 %collective-permute-start.7 = (bf16[32,8192]{1,0:T(8,128)(2,1)S(1)}, bf16[32,8192]{1,0:T(8,128)(2,1)S(1)}, u32[]{:S(2)}, u32[]{:S(2)}) collective-permute-start(bf16[32,8192]{1,0:T(8,128)(2,1)S(1)} %pad_maximum_fusion.refs_0_.refs_8_), channel_id=1, source_target_pairs={{0,64},{1,65},{2,66},{3,67},{4,20},{5,21},{6,22},{7,23},{8,72},{9,... | collective-permute-start | bytes 1572872 | tf_op jit(solution)/shard_map/ppermute | solution.py:84
  41.8 15.3 %collective-permute-start.6 = (bf16[32,8192]{1,0:T(8,128)(2,1)S(1)}, bf16[32,8192]{1,0:T(8,128)(2,1)S(1)}, u32[]{:S(2)}, u32[]{:S(2)}) collective-permute-start(bf16[32,8192]{1,0:T(8,128)(2,1)S(1)} %pad_maximum_fusion.refs_0_.refs_8_), channel_id=1, source_target_pairs={{0,32},{1,33},{2,34},{3,35},{4,12},{5,13},{6,14},{7,15},{8,40},{9,... | collective-permute-start | bytes 1572872 | tf_op jit(solution)/shard_map/ppermute | solution.py:84
  41.8 15.3 %collective-permute-start.22 = (bf16[32,8192]{1,0:T(8,128)(2,1)S(1)}, bf16[32,8192]{1,0:T(8,128)(2,1)S(1)}, u32[]{:S(2)}, u32[]{:S(2)}) collective-permute-start(bf16[32,8192]{1,0:T(8,128)(2,1)S(1)} %collective-permute-done.18.refs_3_), channel_id=1, source_target_pairs={{0,4},{1,5},{2,6},{3,7},{4,0},{5,1},{6,2},{7,3},{8,12},{9,13},{10,... | collective-permute-start | bytes 1572872 | tf_op jit(solution)/shard_map/ppermute | solution.py:84
  45.8 11.8 %collective-permute-start.21 = (bf16[32,8192]{1,0:T(8,128)(2,1)S(1)}, bf16[32,8192]{1,0:T(8,128)(2,1)S(1)}, u32[]{:S(2)}, u32[]{:S(2)}) collective-permute-start(bf16[32,8192]{1,0:T(8,128)(2,1)S(1)} %collective-permute-done.17.refs_2_), channel_id=1, source_target_pairs={{0,4},{1,5},{2,6},{3,7},{4,0},{5,1},{6,2},{7,3},{8,12},{9,13},{10,... | collective-permute-start | bytes 1572872 | tf_op jit(solution)/shard_map/ppermute | solution.py:84
  53.0 4.6 %collective-permute-start.20 = (bf16[32,8192]{1,0:T(8,128)(2,1)S(1)}, bf16[32,8192]{1,0:T(8,128)(2,1)S(1)}, u32[]{:S(2)}, u32[]{:S(2)}) collective-permute-start(bf16[32,8192]{1,0:T(8,128)(2,1)S(1)} %collective-permute-done.16.refs_1_), channel_id=1, source_target_pairs={{0,4},{1,5},{2,6},{3,7},{4,0},{5,1},{6,2},{7,3},{8,12},{9,13},{10,... | collective-permute-start | bytes 1572872 | tf_op jit(solution)/shard_map/ppermute | solution.py:84
  53.0 11.7 %collective-permute-start.9 = (bf16[32,8192]{1,0:T(8,128)(2,1)S(1)}, bf16[32,8192]{1,0:T(8,128)(2,1)S(1)}, u32[]{:S(2)}, u32[]{:S(2)}) collective-permute-start(bf16[32,8192]{1,0:T(8,128)(2,1)S(1)} %pad_maximum_fusion.refs_0_.refs_8_), channel_id=1, source_target_pairs={{0,4},{1,5},{2,6},{3,7},{4,0},{5,1},{6,2},{7,3},{8,12},{9,13},{10,... | collective-permute-start | bytes 1572872 | tf_op jit(solution)/shard_map/ppermute | solution.py:84
  57.1 7.7 %collective-permute-start.12 = (bf16[32,8192]{1,0:T(8,128)(2,1)S(1)}, bf16[32,8192]{1,0:T(8,128)(2,1)S(1)}, u32[]{:S(2)}, u32[]{:S(2)}) collective-permute-start(bf16[32,8192]{1,0:T(8,128)(2,1)S(1)} %collective-permute-done.8.refs_3_.refs_11_), channel_id=1, source_target_pairs={{0,4},{1,5},{2,6},{3,7},{4,0},{5,1},{6,2},{7,3},{8,12},{9,13},{10,... | collective-permute-start | bytes 1572872 | tf_op jit(solution)/shard_map/ppermute | solution.py:84
  57.1 7.7 %collective-permute-start.11 = (bf16[32,8192]{1,0:T(8,128)(2,1)S(1)}, bf16[32,8192]{1,0:T(8,128)(2,1)S(1)}, u32[]{:S(2)}, u32[]{:S(2)}) collective-permute-start(bf16[32,8192]{1,0:T(8,128)(2,1)S(1)} %collective-permute-done.7.refs_2_.refs_10_), channel_id=1, source_target_pairs={{0,4},{1,5},{2,6},{3,7},{4,0},{5,1},{6,2},{7,3},{8,12},{9,13},{10,... | collective-permute-start | bytes 1572872 | tf_op jit(solution)/shard_map/ppermute | solution.py:84
  57.6 7.3 %collective-permute-start.10 = (bf16[32,8192]{1,0:T(8,128)(2,1)S(1)}, bf16[32,8192]{1,0:T(8,128)(2,1)S(1)}, u32[]{:S(2)}, u32[]{:S(2)}) collective-permute-start(bf16[32,8192]{1,0:T(8,128)(2,1)S(1)} %collective-permute-done.6.refs_1_.refs_9_), channel_id=1, source_target_pairs={{0,4},{1,5},{2,6},{3,7},{4,0},{5,1},{6,2},{7,3},{8,12},{9,13},{10,... | collective-permute-start | bytes 1572872 | tf_op jit(solution)/shard_map/ppermute | solution.py:84
  79.0 8.1 %collective-permute-start.30 = (bf16[128,8192]{1,0:T(8,128)(2,1)S(1)}, bf16[128,8192]{1,0:T(8,128)(2,1)S(1)}, u32[]{:S(2)}, u32[]{:S(2)}) collective-permute-start(bf16[128,8192]{1,0:T(8,128)(2,1)S(1)} %shard_map.165), channel_id=1, source_target_pairs={{0,4},{1,5},{2,6},{3,7},{4,0},{5,1},{6,2},{7,3},{8,12},{9,13},{10,... | collective-permute-start | bytes 6291464 | tf_op jit(solution)/shard_map/ppermute | solution.py:84
  87.0 36.0 %collective-permute-start.23 = (bf16[128,8192]{1,0:T(8,128)(2,1)}, bf16[128,8192]{1,0:T(8,128)(2,1)S(1)}, u32[]{:S(2)}, u32[]{:S(2)}) collective-permute-start(bf16[128,8192]{1,0:T(8,128)(2,1)} %shard_map.163), channel_id=1, source_target_pairs={{0,4},{1,5},{2,6},{3,7},{4,0},{5,1},{6,2},{7,3},{8,12},{9,13},{10,... | collective-permute-start | bytes 6291464 | tf_op jit(solution)/shard_map/ppermute | solution.py:84
  95.5 35.0 %collective-permute-start.31 = (bf16[32,8192]{1,0:T(8,128)(2,1)}, bf16[32,8192]{1,0:T(8,128)(2,1)}, u32[]{:S(2)}, u32[]{:S(2)}) collective-permute-start(bf16[32,8192]{1,0:T(8,128)(2,1)} %get-tuple-element.30), channel_id=1, source_target_pairs={{0,96},{1,97},{2,98},{3,99},{4,28},{5,29},{6,30},{7,31},{8,104},{9... | collective-permute-start | bytes 1572872 | tf_op jit(solution)/shard_map/ppermute | solution.py:84
  97.6 34.2 %collective-permute-start.32 = (bf16[32,8192]{1,0:T(8,128)(2,1)}, bf16[32,8192]{1,0:T(8,128)(2,1)}, u32[]{:S(2)}, u32[]{:S(2)}) collective-permute-start(bf16[32,8192]{1,0:T(8,128)(2,1)} %get-tuple-element.31), channel_id=1, source_target_pairs={{0,64},{1,65},{2,66},{3,67},{4,20},{5,21},{6,22},{7,23},{8,72},{9,... | collective-permute-start | bytes 1572872 | tf_op jit(solution)/shard_map/ppermute | solution.py:84
  98.1 34.4 %collective-permute-start.33 = (bf16[32,8192]{1,0:T(8,128)(2,1)}, bf16[32,8192]{1,0:T(8,128)(2,1)}, u32[]{:S(2)}, u32[]{:S(2)}) collective-permute-start(bf16[32,8192]{1,0:T(8,128)(2,1)} %get-tuple-element.32), channel_id=1, source_target_pairs={{0,32},{1,33},{2,34},{3,35},{4,12},{5,13},{6,14},{7,15},{8,40},{9,... | collective-permute-start | bytes 1572872 | tf_op jit(solution)/shard_map/ppermute | solution.py:84
  115.7 5.5 %collective-permute-start.45 = (f32[1,8192]{1,0:T(1,128)S(1)}, f32[1,8192]{1,0:T(1,128)S(1)}, u32[]{:S(2)}, u32[]{:S(2)}) collective-permute-start(f32[1,8192]{1,0:T(1,128)S(1)} %add.192), channel_id=1, source_target_pairs={{0,16},{1,17},{2,18},{3,19},{4,20},{5,21},{6,22},{7,23},{8,24},{9,... | collective-permute-start | bytes 98312 | tf_op jit(solution)/shard_map/ppermute | solution.py:84
  121.2 44.3 %collective-permute-start.46 = (f32[1,8192]{1,0:T(1,128)S(1)}, f32[1,8192]{1,0:T(1,128)S(1)}, u32[]{:S(2)}, u32[]{:S(2)}) collective-permute-start(f32[1,8192]{1,0:T(1,128)S(1)} %add.193), channel_id=1, source_target_pairs={{0,32},{1,33},{2,34},{3,35},{4,36},{5,37},{6,38},{7,39},{8,40},{9,... | collective-permute-start | bytes 98312 | tf_op jit(solution)/shard_map/ppermute | solution.py:84
  129.3 10.7 %collective-permute-start.24 = (bf16[32,8192]{1,0:T(8,128)(2,1)S(1)}, bf16[32,8192]{1,0:T(8,128)(2,1)S(1)}, u32[]{:S(2)}, u32[]{:S(2)}) collective-permute-start(bf16[32,8192]{1,0:T(8,128)(2,1)S(1)} %get-tuple-element.25), channel_id=1, source_target_pairs={{0,96},{1,97},{2,98},{3,99},{4,28},{5,29},{6,30},{7,31},{8,104},{9... | collective-permute-start | bytes 1572872 | tf_op jit(solution)/shard_map/ppermute | solution.py:84
  130.5 15.7 %collective-permute-start.25 = (bf16[32,8192]{1,0:T(8,128)(2,1)S(1)}, bf16[32,8192]{1,0:T(8,128)(2,1)S(1)}, u32[]{:S(2)}, u32[]{:S(2)}) collective-permute-start(bf16[32,8192]{1,0:T(8,128)(2,1)S(1)} %get-tuple-element.26), channel_id=1, source_target_pairs={{0,64},{1,65},{2,66},{3,67},{4,20},{5,21},{6,22},{7,23},{8,72},{9,... | collective-permute-start | bytes 1572872 | tf_op jit(solution)/shard_map/ppermute | solution.py:84
  131.8 17.2 %collective-permute-start.26 = (bf16[32,8192]{1,0:T(8,128)(2,1)S(1)}, bf16[32,8192]{1,0:T(8,128)(2,1)S(1)}, u32[]{:S(2)}, u32[]{:S(2)}) collective-permute-start(bf16[32,8192]{1,0:T(8,128)(2,1)S(1)} %get-tuple-element.27), channel_id=1, source_target_pairs={{0,32},{1,33},{2,34},{3,35},{4,12},{5,13},{6,14},{7,15},{8,40},{9,... | collective-permute-start | bytes 1572872 | tf_op jit(solution)/shard_map/ppermute | solution.py:84
  134.2 17.7 %collective-permute-start.34 = (bf16[8,8192]{1,0:T(8,128)(2,1)S(1)}, bf16[8,8192]{1,0:T(8,128)(2,1)S(1)}, u32[]{:S(2)}, u32[]{:S(2)}) collective-permute-start(bf16[8,8192]{1,0:T(8,128)(2,1)S(1)} %get-tuple-element.57), channel_id=1, source_target_pairs={{0,24},{1,25},{2,26},{3,27},{4,100},{5,101},{6,102},{7,103},{8,0},... | collective-permute-start | bytes 393224 | tf_op jit(solution)/shard_map/ppermute | solution.py:84
  140.0 12.7 %collective-permute-start.36 = (bf16[8,8192]{1,0:T(8,128)(2,1)S(1)}, bf16[8,8192]{1,0:T(8,128)(2,1)S(1)}, u32[]{:S(2)}, u32[]{:S(2)}) collective-permute-start(bf16[8,8192]{1,0:T(8,128)(2,1)S(1)} %get-tuple-element.58), channel_id=1, source_target_pairs={{0,8},{1,9},{2,10},{3,11},{4,36},{5,37},{6,38},{7,39},{8,16},{9,17... | collective-permute-start | bytes 393224 | tf_op jit(solution)/shard_map/ppermute | solution.py:84
  146.2 9.7 %collective-permute-start.35 = (bf16[8,8192]{1,0:T(8,128)(2,1)S(1)}, bf16[8,8192]{1,0:T(8,128)(2,1)S(1)}, u32[]{:S(2)}, u32[]{:S(2)}) collective-permute-start(bf16[8,8192]{1,0:T(8,128)(2,1)S(1)} %get-tuple-element.59), channel_id=1, source_target_pairs={{0,16},{1,17},{2,18},{3,19},{4,68},{5,69},{6,70},{7,71},{8,24},{9,... | collective-permute-start | bytes 393224 | tf_op jit(solution)/shard_map/ppermute | solution.py:84
  149.3 6.7 %collective-permute-start.27 = (bf16[8,8192]{1,0:T(8,128)(2,1)S(1)}, bf16[8,8192]{1,0:T(8,128)(2,1)S(1)}, u32[]{:S(2)}, u32[]{:S(2)}) collective-permute-start(bf16[8,8192]{1,0:T(8,128)(2,1)S(1)} %get-tuple-element.54), channel_id=1, source_target_pairs={{0,24},{1,25},{2,26},{3,27},{4,100},{5,101},{6,102},{7,103},{8,0},... | collective-permute-start | bytes 393224 | tf_op jit(solution)/shard_map/ppermute | solution.py:84
  151.9 6.2 %collective-permute-start.29 = (bf16[8,8192]{1,0:T(8,128)(2,1)S(1)}, bf16[8,8192]{1,0:T(8,128)(2,1)S(1)}, u32[]{:S(2)}, u32[]{:S(2)}) collective-permute-start(bf16[8,8192]{1,0:T(8,128)(2,1)S(1)} %get-tuple-element.55), channel_id=1, source_target_pairs={{0,8},{1,9},{2,10},{3,11},{4,36},{5,37},{6,38},{7,39},{8,16},{9,17... | collective-permute-start | bytes 393224 | tf_op jit(solution)/shard_map/ppermute | solution.py:84
  152.7 7.6 %collective-permute-start.28 = (bf16[8,8192]{1,0:T(8,128)(2,1)S(1)}, bf16[8,8192]{1,0:T(8,128)(2,1)S(1)}, u32[]{:S(2)}, u32[]{:S(2)}) collective-permute-start(bf16[8,8192]{1,0:T(8,128)(2,1)S(1)} %get-tuple-element.56), channel_id=1, source_target_pairs={{0,16},{1,17},{2,18},{3,19},{4,68},{5,69},{6,70},{7,71},{8,24},{9,... | collective-permute-start | bytes 393224 | tf_op jit(solution)/shard_map/ppermute | solution.py:84
  160.9 13.9 %collective-permute-start.37 = (bf16[4,16384]{1,0:T(4,128)(2,1)S(1)}, bf16[4,16384]{1,0:T(4,128)(2,1)S(1)}, u32[]{:S(2)}, u32[]{:S(2)}) collective-permute-start(bf16[4,16384]{1,0:T(4,128)(2,1)S(1)} %get-tuple-element.51), channel_id=1, source_target_pairs={{0,1},{1,2},{2,3},{3,0},{4,5},{5,6},{6,7},{7,4},{8,9},{9,10},{10,1... | collective-permute-start | bytes 393224 | tf_op jit(solution)/shard_map/ppermute | solution.py:84
  161.6 14.5 %collective-permute-start.39 = (bf16[4,16384]{1,0:T(4,128)(2,1)S(1)}, bf16[4,16384]{1,0:T(4,128)(2,1)S(1)}, u32[]{:S(2)}, u32[]{:S(2)}) collective-permute-start(bf16[4,16384]{1,0:T(4,128)(2,1)S(1)} %get-tuple-element.52), channel_id=1, source_target_pairs={{0,3},{1,0},{2,1},{3,2},{4,7},{5,4},{6,5},{7,6},{8,11},{9,8},{10,9... | collective-permute-start | bytes 393224 | tf_op jit(solution)/shard_map/ppermute | solution.py:84
  164.2 11.9 %collective-permute-start.38 = (bf16[4,16384]{1,0:T(4,128)(2,1)S(1)}, bf16[4,16384]{1,0:T(4,128)(2,1)S(1)}, u32[]{:S(2)}, u32[]{:S(2)}) collective-permute-start(bf16[4,16384]{1,0:T(4,128)(2,1)S(1)} %get-tuple-element.53), channel_id=1, source_target_pairs={{0,2},{1,3},{2,0},{3,1},{4,6},{5,7},{6,4},{7,5},{8,10},{9,11},{10,... | collective-permute-start | bytes 393224 | tf_op jit(solution)/shard_map/ppermute | solution.py:84
  165.6 5.5 %collective-permute-start.47 = (f32[1,8192]{1,0:T(1,128)S(1)}, f32[1,8192]{1,0:T(1,128)S(1)}, u32[]{:S(2)}, u32[]{:S(2)}) collective-permute-start(f32[1,8192]{1,0:T(1,128)S(1)} %add.194), channel_id=1, source_target_pairs={{0,64},{1,65},{2,66},{3,67},{4,68},{5,69},{6,70},{7,71},{8,72},{9,... | collective-permute-start | bytes 98312 | tf_op jit(solution)/shard_map/ppermute | solution.py:84
  171.1 10.7 %collective-permute-start.50 = (f32[1,8192]{1,0:T(1,128)S(1)}, f32[1,8192]{1,0:T(1,128)S(1)}, u32[]{:S(2)}, u32[]{:S(2)}) collective-permute-start(f32[1,8192]{1,0:T(1,128)S(1)} %add.195), channel_id=1, source_target_pairs={{0,3},{1,0},{2,1},{3,2},{4,7},{5,4},{6,5},{7,6},{8,11},{9,8},{10,9... | collective-permute-start | bytes 98312 | tf_op jit(solution)/shard_map/ppermute | solution.py:84
  173.3 8.9 %collective-permute-start.49 = (f32[1,8192]{1,0:T(1,128)S(1)}, f32[1,8192]{1,0:T(1,128)S(1)}, u32[]{:S(2)}, u32[]{:S(2)}) collective-permute-start(f32[1,8192]{1,0:T(1,128)S(1)} %add.195), channel_id=1, source_target_pairs={{0,2},{1,3},{2,0},{3,1},{4,6},{5,7},{6,4},{7,5},{8,10},{9,11},{10,... | collective-permute-start | bytes 98312 | tf_op jit(solution)/shard_map/ppermute | solution.py:84
  174.8 7.4 %collective-permute-start.48 = (f32[1,8192]{1,0:T(1,128)S(1)}, f32[1,8192]{1,0:T(1,128)S(1)}, u32[]{:S(2)}, u32[]{:S(2)}) collective-permute-start(f32[1,8192]{1,0:T(1,128)S(1)} %add.195), channel_id=1, source_target_pairs={{0,1},{1,2},{2,3},{3,0},{4,5},{5,6},{6,7},{7,4},{8,9},{9,10},{10,1... | collective-permute-start | bytes 98312 | tf_op jit(solution)/shard_map/ppermute | solution.py:84
  178.3 5.0 %collective-permute-start.42 = (bf16[4,2048]{1,0:T(4,128)(2,1)S(1)}, bf16[4,2048]{1,0:T(4,128)(2,1)S(1)}, u32[]{:S(2)}, u32[]{:S(2)}) collective-permute-start(bf16[4,2048]{1,0:T(4,128)(2,1)S(1)} %get-tuple-element.62), channel_id=1, source_target_pairs={{0,1},{1,2},{2,3},{3,0},{4,5},{5,6},{6,7},{7,4},{8,9},{9,10},{10,1... | collective-permute-start | bytes 49160 | tf_op jit(solution)/shard_map/ppermute | solution.py:84
  179.0 5.2 %collective-permute-start.41 = (bf16[4,2048]{1,0:T(4,128)(2,1)S(1)}, bf16[4,2048]{1,0:T(4,128)(2,1)S(1)}, u32[]{:S(2)}, u32[]{:S(2)}) collective-permute-start(bf16[4,2048]{1,0:T(4,128)(2,1)S(1)} %get-tuple-element.63), channel_id=1, source_target_pairs={{0,2},{1,3},{2,0},{3,1},{4,6},{5,7},{6,4},{7,5},{8,10},{9,11},{10,... | collective-permute-start | bytes 49160 | tf_op jit(solution)/shard_map/ppermute | solution.py:84
  (30 other events, 642.8 us)

commit v2 on v1

v2 whole, which is shorter than its diff:
```python
import functools

import jax
import jax.numpy as jnp
from jax import lax
from jax.experimental import pallas as pl
from jax.experimental.pallas import tpu as pltpu
from jax.sharding import PartitionSpec as P

HD = 128
MODALITIES = 3
NZ = 4
NX = 4
NC = 2
NS = 4
AXES = ("dp", "sect")
BF = jnp.bfloat16
F32 = jnp.float32
CAP = 8
VMEM = 60 * 1024 * 1024


def causal_forward(queries, keys, values):
    seq_count, length, width = queries.shape
    head_count = width // HD
    query_f = queries.astype(F32).reshape(seq_count, length, head_count, HD)
    key_f = keys.astype(F32).reshape(seq_count, length, head_count, HD)
    value_f = values.astype(F32).reshape(seq_count, length, head_count, HD)
    scores = jnp.einsum("sqhd,skhd->shqk", query_f, key_f) * HD ** (-0.5)
    position = jnp.arange(length)
    causal = position[:, None] >= position[None, :]
    scores = jnp.where(causal, scores, -1e30)
    probs = jax.nn.softmax(scores, axis=-1)
    probs_b = probs.astype(BF)
    attended = jnp.einsum("shqk,skhd->sqhd", probs_b.astype(F32), value_f)
    return (attended.astype(BF).reshape(seq_count, length, width), probs, probs_b)


def causal_backward(grad_out, queries, keys, values, attended, probs, probs_b):
    seq_count, length, width = queries.shape
    head_count = width // HD
    shape = (seq_count, length, head_count, HD)
    grad_f = grad_out.astype(F32).reshape(shape)
    query_f = queries.astype(F32).reshape(shape)
    key_f = keys.astype(F32).reshape(shape)
    value_f = values.astype(F32).reshape(shape)
    attended_f = attended.astype(F32).reshape(shape)
    value_grad = jnp.einsum("shqk,sqhd->skhd", probs_b.astype(F32), grad_f).astype(BF)
    dprob = jnp.einsum("sqhd,skhd->shqk", grad_f, value_f)
    delta = jnp.einsum("sqhd,sqhd->shq", grad_f, attended_f)
    dscore = (probs * (dprob - delta[..., None]) * HD ** (-0.5)).astype(BF).astype(F32)
    query_grad = jnp.einsum("shqk,skhd->sqhd", dscore, key_f).astype(BF)
    key_grad = jnp.einsum("shqk,sqhd->skhd", dscore, query_f).astype(BF)
    return (
        query_grad.reshape(seq_count, length, width),
        key_grad.reshape(seq_count, length, width),
        value_grad.reshape(seq_count, length, width),
    )


def _pairs(move):
    out = []
    for z in range(NZ):
        for x in range(NX):
            for c in range(NC):
                for s in range(NS):
                    z2, x2, c2, s2 = move(z, x, c, s)
                    source = ((z * NX + x) * NC + c) * NS + s
                    target = (((z2 % NZ) * NX + x2 % NX) * NC + c2) * NS + s2 % NS
                    out.append((source, target))
    return out


def along(first, shift):
    def move(z, x, c, s):
        if (c == 0) == first:
            return z, x + shift, c, s
        return z + shift, x, c, s

    return _pairs(move)


def send(block, pairs):
    return lax.ppermute(block, AXES, pairs)


def send_stage(block, first, shift):
    return send(block, along(first, shift))


def swap_core(block):
    return send(block, _pairs(lambda z, x, c, s: (z, x, 1 - c, s)))


def send_sect(block, shift):
    return send(block, _pairs(lambda z, x, c, s: (z, x, c, s + shift)))


def gather_rows(block):
    near = [block] + [send_stage(block, True, k) for k in (1, 2, 3)]
    near = jnp.concatenate(near, axis=0)
    own = [near] + [send_stage(near, False, k) for k in (1, 2, 3)]
    other = [swap_core(piece) for piece in own]
    return own + other


def _params(limit=VMEM):
    return pltpu.CompilerParams(vmem_limit_bytes=limit)


def _nt(left, right):
    return lax.dot_general(left, right, (((1,), (1,)), ((), ())), preferred_element_type=F32)


def _slot_selector(labels, kind):
    length = labels.shape[1]
    keep = jnp.broadcast_to((labels == kind).astype(F32), (CAP, length))
    first = lax.broadcasted_iota(jnp.int32, (length, length), 0)
    second = lax.broadcasted_iota(jnp.int32, (length, length), 1)
    rank = jnp.dot(keep, (first <= second).astype(F32), preferred_element_type=F32)
    row = lax.broadcasted_iota(jnp.int32, (CAP, length), 0).astype(F32)
    return jnp.where((rank == row + 1.0) & (keep > 0.5), 1.0, 0.0)


def _slot_spreader(labels, kind):
    length = labels.shape[0]
    keep = jnp.broadcast_to((labels == kind).astype(F32), (length, CAP))
    first = lax.broadcasted_iota(jnp.int32, (length, length), 0)
    second = lax.broadcasted_iota(jnp.int32, (length, length), 1)
    rank = jnp.dot((second <= first).astype(F32), keep, preferred_element_type=F32)
    column = lax.broadcasted_iota(jnp.int32, (length, CAP), 1).astype(F32)
    return jnp.where((rank == column + 1.0) & (keep > 0.5), 1.0, 0.0)


SMALL_COST = pl.CostEstimate(flops=1000, bytes_accessed=1000, transcendentals=0)
SMALL = pl.BlockSpec(memory_space=pltpu.SMEM)
def _whole(*arrays):
    return [pl.BlockSpec(a.shape, lambda i, n=len(a.shape): (0,) * n) for a in arrays]


RAW = pl.BlockSpec(memory_space=pl.ANY)


def _pack_kernel(slot_ref, kinds_ref, labels_ref, rows_ref, out_ref):
    select = _slot_selector(labels_ref[...], kinds_ref[slot_ref[0]]).astype(BF)
    out_ref[...] = jnp.dot(select, rows_ref[...], preferred_element_type=F32).astype(BF)


def pack_rows(slot, kinds, labels, rows):
    out = jax.ShapeDtypeStruct((CAP, rows.shape[1]), BF)
    return pl.pallas_call(
        _pack_kernel,
        grid=(1,),
        in_specs=[SMALL, SMALL] + _whole(labels, rows),
        out_specs=_whole(out)[0],
        out_shape=out,
        compiler_params=_params(8 * 1024 * 1024),
        cost_estimate=SMALL_COST,
    )(slot, kinds, labels, rows)


def _gain_rows(labels, gains):
    return jnp.where(labels == 0, gains[0:1], jnp.where(labels == 1, gains[1:2], gains[2:3]))


def _norm_kernel(slot_ref, kinds_ref, labels_ref, column_ref, residual_ref, gains_ref, *refs):
    blocks, (hidden_ref, packed_ref, joined_ref) = refs[:NS], refs[NS:]
    slot = slot_ref[0]
    width = blocks[0].shape[1]
    for k, block in enumerate(blocks):
        owner = lax.rem(slot - k + NS, NS)
        joined_ref[:, pl.ds(pl.multiple_of(owner * width, width), width)] = block[...]
    hidden = (residual_ref[...].astype(F32) + joined_ref[...].astype(F32)).astype(BF)
    hidden_ref[...] = hidden
    hidden_f = hidden.astype(F32)
    inverse = lax.rsqrt(jnp.mean(hidden_f * hidden_f, axis=-1, keepdims=True) + 1e-05)
    normed = (hidden_f * inverse * _gain_rows(column_ref[...], gains_ref[...])).astype(BF)
    select = _slot_selector(labels_ref[...], kinds_ref[slot]).astype(BF)
    packed_ref[...] = jnp.dot(select, normed, preferred_element_type=F32).astype(BF)


def norm_rows_of(slot, kinds, labels, column, residual, gains, blocks):
    length, width = residual.shape
    outs = [jax.ShapeDtypeStruct((length, width), BF), jax.ShapeDtypeStruct((CAP, width), BF)]
    return pl.pallas_call(
        _norm_kernel,
        grid=(1,),
        in_specs=[SMALL, SMALL] + _whole(labels, column, residual, gains, *blocks),
        out_specs=_whole(*outs),
        out_shape=outs,
        scratch_shapes=[pltpu.VMEM((length, width), BF)],
        compiler_params=_params(8 * 1024 * 1024),
        cost_estimate=SMALL_COST,
    )(slot, kinds, labels, column, residual, gains, *blocks)


def _finish_kernel(slot_ref, kinds_ref, column_ref, hidden_ref, cot_ref, gains_ref, *refs):
    sums, (quarter_ref, block_ref, full_ref) = refs[:NS], refs[NS:]
    slot = slot_ref[0]
    labels = column_ref[...]
    spreaders = [
        _slot_spreader(labels, kinds_ref[lax.rem(slot - k + NS, NS)]) for k in range(NS)
    ]
    spread = jnp.concatenate(spreaders, axis=1).astype(BF)
    rows = jnp.concatenate([s[...].astype(F32) for s in sums], axis=0).astype(BF)
    norm_grad = jnp.dot(spread, rows, preferred_element_type=F32)
    hidden_f = hidden_ref[...].astype(F32)
    inverse = lax.rsqrt(jnp.mean(hidden_f * hidden_f, axis=-1, keepdims=True) + 1e-05)
    normed_f = hidden_f * inverse
    scaled = norm_grad * _gain_rows(labels, gains_ref[...])
    centre = jnp.mean(scaled * normed_f, axis=-1, keepdims=True)
    full = (cot_ref[...].astype(F32) + inverse * (scaled - normed_f * centre)).astype(BF)
    full_ref[...] = full
    width = block_ref.shape[1]
    block_ref[...] = full_ref[:, pl.ds(pl.multiple_of(slot * width, width), width)]
    wide = full.astype(F32)
    count = quarter_ref.shape[0]
    quarter = wide[:count]
    for t in range(1, NS):
        quarter = jnp.where(slot == t, wide[t * count : (t + 1) * count], quarter)
    quarter_ref[...] = quarter.astype(BF)


def finish_norm(slot, kinds, column, hidden, cot, gains, sums, block_width):
    length, width = hidden.shape
    outs = [
        jax.ShapeDtypeStruct((length // NS, width), BF),
        jax.ShapeDtypeStruct((length, block_width), BF),
    ]
    return pl.pallas_call(
        _finish_kernel,
        grid=(1,),
        in_specs=[SMALL, SMALL] + _whole(column, hidden, cot, gains, *sums),
        out_specs=_whole(*outs),
        out_shape=outs,
        scratch_shapes=[pltpu.VMEM((length, width), BF)],
        compiler_params=_params(12 * 1024 * 1024),
        cost_estimate=SMALL_COST,
    )(slot, kinds, column, hidden, cot, gains, *sums)


def _back_kernel(*refs):
    pieces, w_ref, out_ref = refs[:8], refs[8], refs[9]
    rows = jnp.concatenate([p[...] for p in pieces], axis=0)
    part = _nt(w_ref[...], rows)

    @pl.when(pl.program_id(0) == 0)
    def _():
        out_ref[...] = part

    @pl.when(pl.program_id(0) > 0)
    def _():
        out_ref[...] += part


def back_product(pieces, weight, tile=4096):
    hidden, width = weight.shape[1:]
    rows = sum(p.shape[0] for p in pieces)
    return pl.pallas_call(
        _back_kernel,
        grid=(width // tile,),
        in_specs=[pl.BlockSpec((p.shape[0], tile), lambda i: (0, i)) for p in pieces]
        + [pl.BlockSpec((None, hidden, tile), lambda i: (0, 0, i))],
        out_specs=pl.BlockSpec((hidden, rows), lambda i: (0, 0)),
        out_shape=jax.ShapeDtypeStruct((hidden, rows), F32),
        compiler_params=_params(),
        cost_estimate=SMALL_COST,
    )(*pieces, weight)


CHUNKS = 2
STEP = 1024
OUT_STEP = 2048


def _pre_kernel(*refs):
    pieces, w_hbm, back_ref = refs[:8], refs[8], refs[9]
    act_t_ref, grad_t_ref, act_ref, grad_ref, other_hbm = refs[10:15]
    rows_ref, w_ref, acc_ref, other_ref, sems, out_sems = refs[15:]
    width = w_ref.shape[1]
    size = width // CHUNKS
    part = pieces[0].shape[0]
    copies = []
    for c in range(CHUNKS):
        span = pl.ds(c * size, size)
        group = [pltpu.make_async_copy(w_hbm.at[0, :, span], w_ref.at[:, span], sems.at[c, 8])]
        for p, piece in enumerate(pieces):
            group.append(
                pltpu.make_async_copy(
                    piece.at[:, span], rows_ref.at[pl.ds(p * part, part), span], sems.at[c, p]
                )
            )
        for copy in group:
            copy.start()
        copies.append(group)
    acc_ref[...] = jnp.zeros_like(acc_ref)
    for c in range(CHUNKS):
        for copy in copies[c]:
            copy.wait()

        @pl.loop(0, size // STEP)
        def _(i):
            span = pl.ds(pl.multiple_of(c * size + i * STEP, STEP), STEP)
            acc_ref[...] += _nt(w_ref[:, span], rows_ref[:, span])

    pre = acc_ref[...]
    sigma = jax.nn.sigmoid(pre)
    act = pre * sigma
    grad = back_ref[...] * sigma * (1.0 + pre * (1.0 - sigma))
    grad_t_ref[...] = grad.astype(BF)
    grad_ref[...] = grad.T.astype(BF)
    half = other_ref.shape[0]
    left = grad_ref[half:, :]
    outs = []
    for n in range(width // OUT_STEP):
        span = pl.ds(n * OUT_STEP, OUT_STEP)
        other_ref[:, span] = jnp.dot(left, w_ref[:, span], preferred_element_type=F32).astype(BF)
        copy = pltpu.make_async_copy(other_ref.at[:, span], other_hbm.at[:, span], out_sems.at[n])
        copy.start()
        outs.append(copy)
    act_t_ref[...] = act.astype(BF)
    act_ref[...] = act.T.astype(BF)
    for copy in outs:
        copy.wait()


def pre_product(pieces, weight, back):
    hidden, width = weight.shape[1:]
    rows = sum(p.shape[0] for p in pieces)
    outs = (
        [jax.ShapeDtypeStruct((hidden, rows), BF)] * 2
        + [jax.ShapeDtypeStruct((rows, hidden), BF)] * 2
        + [jax.ShapeDtypeStruct((rows // 2, width), BF)]
    )
    return pl.pallas_call(
        _pre_kernel,
        grid=(1,),
        in_specs=[RAW] * 9 + _whole(back),
        out_specs=_whole(*outs[:4]) + [RAW],
        out_shape=outs,
        scratch_shapes=[
            pltpu.VMEM((rows, width), BF),
            pltpu.VMEM((hidden, width), BF),
            pltpu.VMEM((hidden, rows), F32),
            pltpu.VMEM((rows // 2, width), BF),
            pltpu.SemaphoreType.DMA((CHUNKS, 9)),
            pltpu.SemaphoreType.DMA((width // OUT_STEP,)),
        ],
        compiler_params=_params(),
        cost_estimate=SMALL_COST,
    )(*pieces, weight, back)


def _other_kernel(left_ref, w_ref, out_ref):
    out_ref[...] = jnp.dot(left_ref[...], w_ref[...], preferred_element_type=F32).astype(BF)


def other_product(left, weight, tile=4096):
    hidden, width = weight.shape[1:]
    half = left.shape[0] // 2
    return pl.pallas_call(
        _other_kernel,
        grid=(width // tile,),
        in_specs=[
            pl.BlockSpec((half, hidden), lambda i: (1, 0)),
            pl.BlockSpec((None, hidden, tile), lambda i: (0, 0, i)),
        ],
        out_specs=pl.BlockSpec((half, tile), lambda i: (0, i)),
        out_shape=jax.ShapeDtypeStruct((half, width), BF),
        compiler_params=_params(),
        cost_estimate=SMALL_COST,
    )(left, weight)


def _own_kernel(*refs):
    left_ref, w_ref, in_ref = refs[:3]
    rows, outs = refs[3:-4], refs[-4:]
    total = jnp.dot(left_ref[...], w_ref[...], preferred_element_type=F32)
    total = total + in_ref[...].astype(F32)
    part = total.shape[0] // 4
    if rows:
        rows, gain_ref, outs = rows[:4], rows[4], outs
        gain = None
        for k, row_ref in enumerate(rows):
            term = jnp.sum(row_ref[...].astype(F32) * total[k * part : (k + 1) * part], axis=0, keepdims=True)
            gain = term if gain is None else gain + term
        gain_ref[...] = gain
    for k, out_ref in enumerate(outs):
        out_ref[...] = total[k * part : (k + 1) * part].astype(out_ref.dtype)


def own_product(left, weight, arrived, rows=(), tile=4096):
    hidden, width = weight.shape[1:]
    half = left.shape[0] // 2
    part = half // 4
    piece = pl.BlockSpec((part, tile), lambda i: (0, i))
    gain_spec = [pl.BlockSpec((1, tile), lambda i: (0, i))] if rows else []
    gain_shape = [jax.ShapeDtypeStruct((1, width), F32)] if rows else []
    return pl.pallas_call(
        _own_kernel,
        grid=(width // tile,),
        in_specs=[
            pl.BlockSpec((half, hidden), lambda i: (0, 0)),
            pl.BlockSpec((None, hidden, tile), lambda i: (0, 0, i)),
            pl.BlockSpec((half, tile), lambda i: (0, i)),
        ]
        + [piece] * len(rows),
        out_specs=gain_spec + [piece] * 4,
        out_shape=gain_shape
        + [jax.ShapeDtypeStruct((part, width), F32)]
        + [jax.ShapeDtypeStruct((part, width), BF)] * 3,
        compiler_params=_params(),
        cost_estimate=SMALL_COST,
    )(left, weight, arrived, *rows)


def _grads_kernel(*refs):
    cots, rows = refs[:8], refs[8:16]
    act_ref, grad_ref, down_out, up_out = refs[16:]
    cot = jnp.concatenate([p[...] for p in cots], axis=0)
    down_out[...] = jnp.dot(act_ref[...], cot, preferred_element_type=F32).astype(BF)
    row = jnp.concatenate([p[...] for p in rows], axis=0)
    up_out[...] = jnp.dot(grad_ref[...], row, preferred_element_type=F32).astype(BF)


def grad_products(cots, rows, act_t, grad_t, shape, tile=2048):
    _, hidden, width = shape
    count = act_t.shape[1]
    whole = lambda i: (0, 0)
    piece_specs = [pl.BlockSpec((p.shape[0], tile), lambda i: (0, i)) for p in cots]
    weight_spec = pl.BlockSpec((None, hidden, tile), lambda i: (0, 0, i))
    return pl.pallas_call(
        _grads_kernel,
        grid=(width // tile,),
        in_specs=piece_specs * 2 + [pl.BlockSpec((hidden, count), whole)] * 2,
        out_specs=[weight_spec, weight_spec],
        out_shape=[jax.ShapeDtypeStruct(shape, BF)] * 2,
        compiler_params=_params(),
        cost_estimate=pl.CostEstimate(
            flops=4 * hidden * count * width,
            bytes_accessed=2 * width * (2 * hidden + 2 * count),
            transcendentals=0,
        ),
    )(*cots, *rows, act_t, grad_t)


def far_sum(pieces):
    total = pieces[0]
    for k in (1, 2, 3):
        total = total + send_stage(pieces[k], False, -k).astype(F32)
    return total


def near_sum(total, dtype):
    blocks = [total[k * CAP : (k + 1) * CAP] for k in range(4)]
    result = blocks[0]
    for k in (1, 2, 3):
        result = result + send_stage(blocks[k].astype(dtype), True, -k).astype(F32)
    return result


def sum_over_dp(row):
    moves = (
        lambda z, x, c, s: (z, x, 1 - c, s),
        lambda z, x, c, s: (z, x ^ 1, c, s),
        lambda z, x, c, s: (z, x ^ 2, c, s),
        lambda z, x, c, s: (z ^ 1, x, c, s),
        lambda z, x, c, s: (z ^ 2, x, c, s),
    )
    for move in moves:
        row = row + send(row, _pairs(move))
    return row


def after(value, *others):
    return lax.optimization_barrier((value, *others))[0]


def on_device(
    queries, keys, values, residual, labels, slot_modality, gains, up_weight, down_weight, cotangent
):
    slot_index = lax.axis_index("sect")
    slot = slot_index.astype(jnp.int32).reshape(1)
    column = labels.reshape(-1, 1)
    length = labels.shape[1]
    grad_full = cotangent[0]
    packed_cot = pack_rows(slot, slot_modality, labels, grad_full)
    cot_rows = gather_rows(packed_cot)
    queries, keys, values, _ = lax.optimization_barrier((queries, keys, values, packed_cot))

    attended_block, probs, probs_b = causal_forward(queries, keys, values)
    block = attended_block[0]
    blocks = [block] + [send_sect(block, k) for k in (1, 2, 3)]
    hidden, packed = norm_rows_of(slot, slot_modality, labels, column, residual[0], gains, blocks)
    token_rows = gather_rows(packed)

    back = back_product(cot_rows, down_weight)
    act_t, grad_t, act, grad, norm_other = pre_product(token_rows, up_weight, back)
    norm_arrived = swap_core(norm_other)
    ffn_other = other_product(after(act, norm_other), down_weight)
    ffn_arrived = swap_core(ffn_other)
    gain_part, *norm_pieces = own_product(after(grad, ffn_other), up_weight, norm_arrived, token_rows[:4])
    ffn_pieces = own_product(after(act, norm_pieces[0]), down_weight, ffn_arrived)
    down_grad, up_grad = grad_products(
        cot_rows, token_rows, after(act_t, ffn_pieces[0]), grad_t, up_weight.shape
    )
    norm_total = far_sum(norm_pieces)
    norm_rows = near_sum(norm_total, F32).astype(BF)
    sums = [norm_rows] + [send_sect(norm_rows, k) for k in (1, 2, 3)]
    residual_grad, grad_block = finish_norm(
        slot, slot_modality, column, hidden, grad_full, gains, sums, queries.shape[2]
    )
    query_grad, key_grad, value_grad = causal_backward(
        grad_block[None], queries, keys, values, attended_block, probs, probs_b
    )

    gain_sum = sum_over_dp(after(gain_part, norm_total))
    gain_grad = jnp.zeros(gains.shape, F32)
    for k in range(NS):
        part = gain_sum if k == 0 else send_sect(gain_sum, k)
        owner = lax.rem(slot_index - k + NS, NS)
        kind = jnp.sum(jnp.where(jnp.arange(NS) == owner, slot_modality, 0))
        gain_grad = gain_grad + jnp.where(jnp.arange(MODALITIES)[:, None] == kind, part, 0.0)
    gain_grad = gain_grad / gains

    quarter = length // NS
    ffn_rows = near_sum(far_sum(ffn_pieces), BF).astype(BF)
    keep = labels[0] == jnp.sum(jnp.where(jnp.arange(NS) == slot_index, slot_modality, 0))
    before = jnp.arange(length)[:, None] >= jnp.arange(length)[None, :]
    rank_of = jnp.sum(jnp.where(before, keep[None, :], False).astype(jnp.int32), axis=1) - 1
    spreader = ((rank_of[:, None] == jnp.arange(CAP)[None, :]) & keep[:, None]).astype(BF)
    spread = jnp.dot(spreader, ffn_rows, preferred_element_type=F32).astype(BF)

    def own_quarter(array, shift=0):
        return lax.dynamic_slice_in_dim(array, lax.rem(slot_index + shift, NS) * quarter, quarter, 0)

    total = own_quarter(spread).astype(F32)
    for k in (1, 2, 3):
        total = total + send_sect(own_quarter(spread, k), k).astype(F32)
    output = (own_quarter(hidden).astype(F32) + total).astype(BF)[None]
    return (
        output,
        residual_grad[None],
        query_grad,
        key_grad,
        value_grad,
        up_grad,
        down_grad,
        gain_grad,
    )


def solution(mesh):
    in_specs = (
        P("dp", None, "sect"),
        P("dp", None, "sect"),
        P("dp", None, "sect"),
        P("dp", None, None),
        P("dp", None),
        P(),
        P(),
        P("sect", "dp", None),
        P("sect", "dp", None),
        P("dp", None, None),
    )
    out_specs = (
        P("dp", "sect", None),
        P("dp", "sect", None),
        P("dp", None, "sect"),
        P("dp", None, "sect"),
        P("dp", None, "sect"),
        P("sect", "dp", None),
        P("sect", "dp", None),
        P(),
    )
    return jax.shard_map(
        on_device, mesh=mesh, in_specs=in_specs, out_specs=out_specs, check_vma=False
    )
```

time: 189 us -> 168 us (0.89)
  starting transfers between devices: 73.8 us -> 61.7 us
  Pallas kernels: 53.2 us -> 43.5 us
  local copies, waits for them, and re-layouts: 5.64 us -> 12.1 us
  other arithmetic: 11.7 us -> 7.77 us
  matrix products: 4.16 us -> 1.39 us
    ppermute x51, starting transfers between devices: 73.8 us -> 61.7 us  [send(): return lax.ppermute(block, AXES, pairs)]
    pallas_call x2 -> x1, Pallas kernels: 13.7 us -> 4.37 us  [other_product(): pl.pallas_call(_other_kernel, grid=(width // tile,), in_specs=[pl.BlockSp...]
    unnamed x66 -> x84, local copies, waits for them, and re-layouts: 3.82 us -> 10.5 us
    pallas_call x1 -> x4, Pallas kernels: 7.82 us -> 13.5 us  [the longest x1 9.73 us: pre_product(): pl.pallas_call(_pre_kernel, grid=(1,), in_specs=[RAW] * 9 + _whole(back),...]
    pallas_call x2, Pallas kernels: 13.7 us -> 10.8 us  [own_product(): pl.pallas_call(_own_kernel, grid=(width // tile,), in_specs=[pl.BlockSpec...]
    dot_general x4 -> x1, matrix products: 3.05 us -> 0.27 us  [on_device(): spread = jnp.dot(spreader, ffn_rows, preferred_element_type=F32).astype(BF)]
  transfers between devices with their start and end apart: 51 -> 51, of which waited for: 14 -> 17; matrix products, arithmetic and copies ran while one was open for 8% -> 5% of each run, Pallas kernels for 21% -> 18%
where the time goes in v2:
time: 168 us; the launch traced here: 167 us
  starting transfers between devices  61.7 us (37%)
  Pallas kernels  43.5 us (26%)
  waiting for transfers between devices  39.4 us (23%)
  local copies, waits for them, and re-layouts  12.1 us (7%)
  other arithmetic  7.77 us (5%)
    ppermute x51, starting transfers between devices, send(): return lax.ppermute(block, AXES, pairs)  61.7 us
    ppermute x51, waiting for transfers between devices, send(): return lax.ppermute(block, AXES, pairs)  39.4 us
    pallas_call x2, Pallas kernels, own_product(): pl.pallas_call(_own_kernel, grid=(width // tile,), in_specs=[pl.BlockSpec...  10.8 us
    unnamed x84, local copies, waits for them, and re-layouts  10.5 us
    pallas_call x1, Pallas kernels, pre_product(): pl.pallas_call(_pre_kernel, grid=(1,), in_specs=[RAW] * 9 + _whole(back),...  9.73 us
    pallas_call x1, Pallas kernels, grad_products(): pl.pallas_call(_grads_kernel, grid=(width // tile,), in_specs=piece_specs...  9.16 us
    pallas_call x1, Pallas kernels, back_product(): pl.pallas_call(_back_kernel, grid=(width // tile,), in_specs=[pl.BlockSpe...  5.64 us
    pallas_call x1, Pallas kernels, other_product(): pl.pallas_call(_other_kernel, grid=(width // tile,), in_specs=[pl.BlockSp...  4.37 us
  transfers between devices with their start and end apart: 51, of which 17 were waited for; matrix products, arithmetic and copies ran while one was open for 5% of the time, Pallas kernels for 18%

profile of v2, /device:TPU:0, one launch (start us, length us, event | category | flops | bytes accessed | tf_op | source)
XLA Modules:
  0.0 167.2 jit_solution(7930124180772307321)
XLA Ops:
  7.3 3.2 %collective-permute-start.2 = (bf16[16,2048]{1,0:T(8,128)(2,1)S(1)}, bf16[16,2048]{1,0:T(8,128)(2,1)S(1)}, u32[]{:S(2)}, u32[]{:S(2)}) collective-permute-start(bf16[16,2048]{1,0:T(8,128)(2,1)S(1)} %bitcast.78), channel_id=1, source_target_pairs={{0,3},{1,0},{2,1},{3,2},{4,7},{5,4},{6,5},{7,6},{8,11},{9,8},{10,9... | collective-permute-start | bytes 196616 | tf_op jit(solution)/shard_map/ppermute | solution.py:84
  11.1 1.0 collective-permute-start
  12.1 2.8 %collective-permute-start.15 = (bf16[8,8192]{1,0:T(8,128)(2,1)S(1)}, bf16[8,8192]{1,0:T(8,128)(2,1)S(1)}, u32[]{:S(2)}, u32[]{:S(2)}) collective-permute-start(bf16[8,8192]{1,0:T(8,128)(2,1)S(1)} %shard_map.161), channel_id=1, source_target_pairs={{0,24},{1,25},{2,26},{3,27},{4,100},{5,101},{6,102},{7,103},{8,0},... | collective-permute-start | bytes 393224 | tf_op jit(solution)/shard_map/ppermute | solution.py:84
  20.1 1.0 shard_map.162
  21.1 2.8 %collective-permute-start.5 = (bf16[8,8192]{1,0:T(8,128)(2,1)S(1)}, bf16[8,8192]{1,0:T(8,128)(2,1)S(1)}, u32[]{:S(2)}, u32[]{:S(2)}) collective-permute-start(bf16[8,8192]{1,0:T(8,128)(2,1)S(1)} %get-tuple-element.40), channel_id=1, source_target_pairs={{0,24},{1,25},{2,26},{3,27},{4,100},{5,101},{6,102},{7,103},{8,0},... | collective-permute-start | bytes 393224 | tf_op jit(solution)/shard_map/ppermute | solution.py:84
  25.9 4.1 %collective-permute-start.18 = (bf16[32,8192]{1,0:T(8,128)(2,1)S(1)}, bf16[32,8192]{1,0:T(8,128)(2,1)S(1)}, u32[]{:S(2)}, u32[]{:S(2)}) collective-permute-start(bf16[32,8192]{1,0:T(8,128)(2,1)S(1)} %pad_maximum_fusion.refs_0_), channel_id=1, source_target_pairs={{0,96},{1,97},{2,98},{3,99},{4,28},{5,29},{6,30},{7,31},{8,104},{9... | collective-permute-start | bytes 1572872 | tf_op jit(solution)/shard_map/ppermute | solution.py:84
  30.0 1.8 %collective-permute-done.3 = bf16[8,8192]{1,0:T(8,128)(2,1)S(1)} collective-permute-done((bf16[8,8192]{1,0:T(8,128)(2,1)S(1)}, bf16[8,8192]{1,0:T(8,128)(2,1)S(1)}, u32[]{:S(2)}, u32[]{:S(2)}) %collective-permute-start.3) | collective-permute-done | bytes 131104 | tf_op jit(solution)/shard_map/ppermute | solution.py:84
  31.8 3.9 %collective-permute-start.17 = (bf16[32,8192]{1,0:T(8,128)(2,1)S(1)}, bf16[32,8192]{1,0:T(8,128)(2,1)S(1)}, u32[]{:S(2)}, u32[]{:S(2)}) collective-permute-start(bf16[32,8192]{1,0:T(8,128)(2,1)S(1)} %pad_maximum_fusion.refs_0_), channel_id=1, source_target_pairs={{0,64},{1,65},{2,66},{3,67},{4,20},{5,21},{6,22},{7,23},{8,72},{9,... | collective-permute-start | bytes 1572872 | tf_op jit(solution)/shard_map/ppermute | solution.py:84
  35.7 1.1 collective-permute-start.16
  36.9 2.3 %collective-permute-start.8 = (bf16[32,8192]{1,0:T(8,128)(2,1)S(1)}, bf16[32,8192]{1,0:T(8,128)(2,1)S(1)}, u32[]{:S(2)}, u32[]{:S(2)}) collective-permute-start(bf16[32,8192]{1,0:T(8,128)(2,1)S(1)} %constant_dynamic-update-slice_fusion.refs_0_.refs_3_.refs_8_), channel_id=1, source_target_pairs={{0,96},{1,97},{2,98},{3,99},{4,28},{5,29},{6,30},{7,31},{8,104},{9... | collective-permute-start | bytes 1572872 | tf_op jit(solution)/shard_map/ppermute | solution.py:84
  40.1 2.8 %collective-permute-done.17.refs_2_ = bf16[32,8192]{1,0:T(8,128)(2,1)S(1)} collective-permute-done((bf16[32,8192]{1,0:T(8,128)(2,1)S(1)}, bf16[32,8192]{1,0:T(8,128)(2,1)S(1)}, u32[]{:S(2)}, u32[]{:S(2)}) %collective-permute-start.17) | collective-permute-done | bytes 524320 | tf_op jit(solution)/shard_map/ppermute | solution.py:84
  43.0 5.5 %collective-permute-done.16.refs_1_ = bf16[32,8192]{1,0:T(8,128)(2,1)S(1)} collective-permute-done((bf16[32,8192]{1,0:T(8,128)(2,1)S(1)}, bf16[32,8192]{1,0:T(8,128)(2,1)S(1)}, u32[]{:S(2)}, u32[]{:S(2)}) %collective-permute-start.16) | collective-permute-done | bytes 524320 | tf_op jit(solution)/shard_map/ppermute | solution.py:84
  48.5 1.1 collective-permute-done.8.refs_3_.refs_6_.refs_11_
  49.5 1.9 %collective-permute-start.9 = (bf16[32,8192]{1,0:T(8,128)(2,1)S(1)}, bf16[32,8192]{1,0:T(8,128)(2,1)}, u32[]{:S(2)}, u32[]{:S(2)}) collective-permute-start(bf16[32,8192]{1,0:T(8,128)(2,1)S(1)} %constant_dynamic-update-slice_fusion.refs_0_.refs_3_.refs_8_), channel_id=1, source_target_pairs={{0,4},{1,5},{2,6},{3,7},{4,0},{5,1},{6,2},{7,3},{8,12},{9,13},{10,... | collective-permute-start | bytes 1572872 | tf_op jit(solution)/shard_map/ppermute | solution.py:84
  51.4 2.8 %collective-permute-done.7.refs_2_.refs_5_.refs_10_ = bf16[32,8192]{1,0:T(8,128)(2,1)S(1)} collective-permute-done((bf16[32,8192]{1,0:T(8,128)(2,1)S(1)}, bf16[32,8192]{1,0:T(8,128)(2,1)S(1)}, u32[]{:S(2)}, u32[]{:S(2)}) %collective-permute-start.7) | collective-permute-done | bytes 524320 | tf_op jit(solution)/shard_map/ppermute | solution.py:84
  54.2 5.5 %collective-permute-done.6.refs_1_.refs_4_.refs_9_ = bf16[32,8192]{1,0:T(8,128)(2,1)S(1)} collective-permute-done((bf16[32,8192]{1,0:T(8,128)(2,1)S(1)}, bf16[32,8192]{1,0:T(8,128)(2,1)S(1)}, u32[]{:S(2)}, u32[]{:S(2)}) %collective-permute-start.6) | collective-permute-done | bytes 524320 | tf_op jit(solution)/shard_map/ppermute | solution.py:84
  61.1 5.6 %shard_map.163.refs_9_ = f32[344,256]{1,0:T(8,128)} custom-call(bf16[32,8192]{1,0:T(8,128)(2,1)} %copy-done.16, bf16[32,8192]{1,0:T(8,128)(2,1)} %copy-done.22, bf16[32,8192]{1,0:T(8,128)(2,1)} %copy-done.21, bf16[32,8192]{1,0:T(8,128)(2,1)} %copy-done.20, bf16[32,8192]{1,0:T(8,128)(2,1)} %copy-done.19, bf16[32,8192]{1,0:T(8,128)(2,1)} %collective-permute-done.20.refs_5_, ...), custom_call_target="tpu_custom_call" | custom-call | flops 1000 | bytes 1000 | tf_op jit(solution)/shard_map/pallas_call | solution.py:259
  66.8 9.7 %shard_map.164 = (bf16[344,256]{1,0:T(8,128)(2,1)}, bf16[344,256]{1,0:T(8,128)(2,1)}, bf16[256,344]{1,0:T(8,128)(2,1)}, bf16[256,344]{1,0:T(8,128)(2,1)}, bf16[128,8192]{1,0:T(8,128)(2,1)}) custom-call(bf16[32,8192]{1,0:T(8,128)(2,1)} %copy-done.11, bf16[32,8192]{1,0:T(8,128)(2,1)} %copy-done.15, bf16[32,8192]{1,0:T(8,128)(2,1)} %copy-done.14, ...), custom_call_target="tpu_custom_call" | custom-call | flops 1000 | bytes 1000 | tf_op jit(solution)/shard_map/pallas_call | solution.py:335
  77.0 4.4 %shard_map.165 = bf16[128,8192]{1,0:T(8,128)(2,1)} custom-call(bf16[256,344]{1,0:T(8,128)(2,1)} %get-tuple-element.47.left_ref.refs_0_, bf16[1,344,8192]{2,1,0:T(8,128)(2,1)} %refs_1_.3), custom_call_target="tpu_custom_call" | custom-call | flops 1000 | bytes 1000 | tf_op jit(solution)/shard_map/pallas_call | solution.py:361
  82.4 1.3 iota_compare_fusion.4
  83.7 1.2 iota_compare_fusion.2
  84.9 1.3 copy-done.12
  86.2 5.8 %shard_map.166 = (f32[1,8192]{1,0:T(1,128)}, f32[32,8192]{1,0:T(8,128)}, bf16[32,8192]{1,0:T(8,128)(2,1)}, bf16[32,8192]{1,0:T(8,128)(2,1)}, bf16[32,8192]{1,0:T(8,128)(2,1)}) custom-call(bf16[256,344]{1,0:T(8,128)(2,1)} %get-tuple-element.45.refs_0_, bf16[1,344,8192]{2,1,0:T(8,128)(2,1)} %refs_1_.2, bf16[128,8192]{1,0:T(8,128)(2,1)} %copy-done.12, ...), custom_call_target="tpu_custom_call" | custom-call | flops 1000 | bytes 1000 | tf_op jit(solution)/shard_map/pallas_call | solution.py:399
  92.7 3.5 %collective-permute-start.35 = (bf16[32,8192]{1,0:T(8,128)(2,1)}, bf16[32,8192]{1,0:T(8,128)(2,1)S(1)}, u32[]{:S(2)}, u32[]{:S(2)}) collective-permute-start(bf16[32,8192]{1,0:T(8,128)(2,1)} %get-tuple-element.53), channel_id=1, source_target_pairs={{0,64},{1,65},{2,66},{3,67},{4,20},{5,21},{6,22},{7,23},{8,72},{9,... | collective-permute-start | bytes 1572872 | tf_op jit(solution)/shard_map/ppermute | solution.py:84
  97.4 5.0 %shard_map.167 = (f32[32,8192]{1,0:T(8,128)}, bf16[32,8192]{1,0:T(8,128)(2,1)}, bf16[32,8192]{1,0:T(8,128)(2,1)}, bf16[32,8192]{1,0:T(8,128)(2,1)}) custom-call(bf16[256,344]{1,0:T(8,128)(2,1)} %get-tuple-element.47.left_ref.refs_0_, bf16[1,344,8192]{2,1,0:T(8,128)(2,1)} %refs_1_.3, bf16[128,8192]{1,0:T(8,128)(2,1)} %collective-permute-done.24.refs_2_), custom_call_target="tpu_custom_call" | custom-call | flops 1000 | bytes 1000 | tf_op jit(solution)/shard_map/pallas_call | solution.py:399
  102.4 2.8 %collective-permute-start.25 = (bf16[32,8192]{1,0:T(8,128)(2,1)}, bf16[32,8192]{1,0:T(8,128)(2,1)}, u32[]{:S(2)}, u32[]{:S(2)}) collective-permute-start(bf16[32,8192]{1,0:T(8,128)(2,1)} %get-tuple-element.49), channel_id=1, source_target_pairs={{0,96},{1,97},{2,98},{3,99},{4,28},{5,29},{6,30},{7,31},{8,104},{9... | collective-permute-start | bytes 1572872 | tf_op jit(solution)/shard_map/ppermute | solution.py:84
  106.2 3.0 %collective-permute-done.36 = bf16[32,8192]{1,0:T(8,128)(2,1)S(1)} collective-permute-done((bf16[32,8192]{1,0:T(8,128)(2,1)}, bf16[32,8192]{1,0:T(8,128)(2,1)S(1)}, u32[]{:S(2)}, u32[]{:S(2)}) %collective-permute-start.36) | collective-permute-done | bytes 524320 | tf_op jit(solution)/shard_map/ppermute | solution.py:84
  109.5 9.2 %shard_map.169 = (bf16[1,344,8192]{2,1,0:T(8,128)(2,1)}, bf16[1,344,8192]{2,1,0:T(8,128)(2,1)}) custom-call(bf16[32,8192]{1,0:T(8,128)(2,1)} %copy-done.16, bf16[32,8192]{1,0:T(8,128)(2,1)} %copy-done.22, bf16[32,8192]{1,0:T(8,128)(2,1)} %copy-done.21, bf16[32,8192]{1,0:T(8,128)(2,1)} %copy-done.20, bf16[32,8192]{1,0:T(8,128)(2,1)} %copy-done.19, ...), custom_call_target="tpu_custom_call" | custom-call | flops 2885681152 | bytes 19660800 | tf_op jit(solution)/shard_map/pallas_call | solution.py:432
  119.0 2.6 %collective-permute-done.27 = bf16[32,8192]{1,0:T(8,128)(2,1)} collective-permute-done((bf16[32,8192]{1,0:T(8,128)(2,1)}, bf16[32,8192]{1,0:T(8,128)(2,1)}, u32[]{:S(2)}, u32[]{:S(2)}) %collective-permute-start.27) | collective-permute-done | bytes 524320 | tf_op jit(solution)/shard_map/ppermute | solution.py:84
  121.6 1.6 fusion.40
  124.2 1.6 collective-permute-start.28
  126.3 2.7 %collective-permute-start.29 = (bf16[8,8192]{1,0:T(8,128)(2,1)S(1)}, bf16[8,8192]{1,0:T(8,128)(2,1)S(1)}, u32[]{:S(2)}, u32[]{:S(2)}) collective-permute-start(bf16[8,8192]{1,0:T(8,128)(2,1)S(1)} %get-tuple-element.76), channel_id=1, source_target_pairs={{0,16},{1,17},{2,18},{3,19},{4,68},{5,69},{6,70},{7,71},{8,24},{9,... | collective-permute-start | bytes 393224 | tf_op jit(solution)/shard_map/ppermute | solution.py:84
  129.0 1.7 %collective-permute-start.46 = (f32[1,8192]{1,0:T(1,128)S(1)}, f32[1,8192]{1,0:T(1,128)S(1)}, u32[]{:S(2)}, u32[]{:S(2)}) collective-permute-start(f32[1,8192]{1,0:T(1,128)S(1)} %add.140), channel_id=1, source_target_pairs={{0,32},{1,33},{2,34},{3,35},{4,36},{5,37},{6,38},{7,39},{8,40},{9,... | collective-permute-start | bytes 98312 | tf_op jit(solution)/shard_map/ppermute | solution.py:84
  131.6 1.8 %collective-permute-done.46 = f32[1,8192]{1,0:T(1,128)S(1)} collective-permute-done((f32[1,8192]{1,0:T(1,128)S(1)}, f32[1,8192]{1,0:T(1,128)S(1)}, u32[]{:S(2)}, u32[]{:S(2)}) %collective-permute-start.46) | collective-permute-done | bytes 32800 | tf_op jit(solution)/shard_map/ppermute | solution.py:84
  134.4 2.3 %collective-permute-start.47 = (f32[1,8192]{1,0:T(1,128)S(1)}, f32[1,8192]{1,0:T(1,128)S(1)}, u32[]{:S(2)}, u32[]{:S(2)}) collective-permute-start(f32[1,8192]{1,0:T(1,128)S(1)} %add.141), channel_id=1, source_target_pairs={{0,64},{1,65},{2,66},{3,67},{4,68},{5,69},{6,70},{7,71},{8,72},{9,... | collective-permute-start | bytes 98312 | tf_op jit(solution)/shard_map/ppermute | solution.py:84
  137.0 2.9 %collective-permute-done.47 = f32[1,8192]{1,0:T(1,128)S(1)} collective-permute-done((f32[1,8192]{1,0:T(1,128)S(1)}, f32[1,8192]{1,0:T(1,128)S(1)}, u32[]{:S(2)}, u32[]{:S(2)}) %collective-permute-start.47) | collective-permute-done | bytes 32800 | tf_op jit(solution)/shard_map/ppermute | solution.py:84
  140.0 1.9 %collective-permute-start.50 = (f32[1,8192]{1,0:T(1,128)S(1)}, f32[1,8192]{1,0:T(1,128)S(1)}, u32[]{:S(2)}, u32[]{:S(2)}) collective-permute-start(f32[1,8192]{1,0:T(1,128)S(1)} %add.142), channel_id=1, source_target_pairs={{0,3},{1,0},{2,1},{3,2},{4,7},{5,4},{6,5},{7,6},{8,11},{9,8},{10,9... | collective-permute-start | bytes 98312 | tf_op jit(solution)/shard_map/ppermute | solution.py:84
  141.9 1.7 %collective-permute-start.49 = (f32[1,8192]{1,0:T(1,128)S(1)}, f32[1,8192]{1,0:T(1,128)S(1)}, u32[]{:S(2)}, u32[]{:S(2)}) collective-permute-start(f32[1,8192]{1,0:T(1,128)S(1)} %add.142), channel_id=1, source_target_pairs={{0,2},{1,3},{2,0},{3,1},{4,6},{5,7},{6,4},{7,5},{8,10},{9,11},{10,... | collective-permute-start | bytes 98312 | tf_op jit(solution)/shard_map/ppermute | solution.py:84
  144.0 1.2 collective-permute-start.38
  145.2 2.5 %collective-permute-done.49 = f32[1,8192]{1,0:T(1,128)S(1)} collective-permute-done((f32[1,8192]{1,0:T(1,128)S(1)}, f32[1,8192]{1,0:T(1,128)S(1)}, u32[]{:S(2)}, u32[]{:S(2)}) %collective-permute-start.49) | collective-permute-done | bytes 32800 | tf_op jit(solution)/shard_map/ppermute | solution.py:84
  147.7 1.0 collective-permute-done.48
  148.7 2.2 %collective-permute-start.33 = (bf16[4,8192]{1,0:T(4,128)(2,1)S(1)}, bf16[4,8192]{1,0:T(4,128)(2,1)S(1)}, u32[]{:S(2)}, u32[]{:S(2)}) collective-permute-start(bf16[4,8192]{1,0:T(4,128)(2,1)S(1)} %get-tuple-element.78), channel_id=1, source_target_pairs={{0,3},{1,0},{2,1},{3,2},{4,7},{5,4},{6,5},{7,6},{8,11},{9,8},{10,9... | collective-permute-start | bytes 196616 | tf_op jit(solution)/shard_map/ppermute | solution.py:84
  151.9 3.1 %collective-permute-start.42 = (bf16[8,8192]{1,0:T(8,128)(2,1)S(1)}, bf16[8,8192]{1,0:T(8,128)(2,1)S(1)}, u32[]{:S(2)}, u32[]{:S(2)}) collective-permute-start(bf16[8,8192]{1,0:T(8,128)(2,1)S(1)} %fusion.12.refs_0_), channel_id=1, source_target_pairs={{0,3},{1,0},{2,1},{3,2},{4,7},{5,4},{6,5},{7,6},{8,11},{9,8},{10,9... | collective-permute-start | bytes 393224 | tf_op jit(solution)/shard_map/ppermute | solution.py:84
  155.7 1.2 collective-permute-start.40
  156.8 1.0 collective-permute-done.32
  158.6 3.0 %collective-permute-done.41.refs_2_ = bf16[8,8192]{1,0:T(8,128)(2,1)S(1)} collective-permute-done((bf16[8,8192]{1,0:T(8,128)(2,1)S(1)}, bf16[8,8192]{1,0:T(8,128)(2,1)S(1)}, u32[]{:S(2)}, u32[]{:S(2)}) %collective-permute-start.41) | collective-permute-done | bytes 131104 | tf_op jit(solution)/shard_map/ppermute | solution.py:84
  161.6 1.3 collective-permute-done.40.refs_1_
  162.9 2.0 %shard_map.168 = (bf16[4,8192]{1,0:T(4,128)(2,1)}, bf16[16,2048]{1,0:T(8,128)(2,1)S(1)}) custom-call(s32[1]{0:T(128)} %bitcast.2.slot_ref, s32[4]{0:T(128)S(1)} %copy-done.7, s32[16,1]{1,0:T(8,128)S(1)} %copy.37.column_ref, bf16[16,8192]{1,0:T(8,128)(2,1)S(1)} %get-tuple-element.39.hidden_ref, bf16[16,8192]{1,0:T(8,128)(2,1)S(1)} %bitcast.77, ...), custom_call_target="tpu_custom_call" | custom-call | flops 1000 | bytes 1000 | tf_op jit(solution)/shard_map/pallas_call | solution.py:230
  (182 shorter events, 30.1 us)
Async XLA Ops:
  7.3 8.4 %collective-permute-start.2 = (bf16[16,2048]{1,0:T(8,128)(2,1)S(1)}, bf16[16,2048]{1,0:T(8,128)(2,1)S(1)}, u32[]{:S(2)}, u32[]{:S(2)}) collective-permute-start(bf16[16,2048]{1,0:T(8,128)(2,1)S(1)} %bitcast.78), channel_id=1, source_target_pairs={{0,3},{1,0},{2,1},{3,2},{4,7},{5,4},{6,5},{7,6},{8,11},{9,8},{10,9... | collective-permute-start | bytes 196616 | tf_op jit(solution)/shard_map/ppermute | solution.py:84
  10.5 6.1 %collective-permute-start.1 = (bf16[16,2048]{1,0:T(8,128)(2,1)S(1)}, bf16[16,2048]{1,0:T(8,128)(2,1)S(1)}, u32[]{:S(2)}, u32[]{:S(2)}) collective-permute-start(bf16[16,2048]{1,0:T(8,128)(2,1)S(1)} %bitcast.79), channel_id=1, source_target_pairs={{0,2},{1,3},{2,0},{3,1},{4,6},{5,7},{6,4},{7,5},{8,10},{9,11},{10,... | collective-permute-start | bytes 196616 | tf_op jit(solution)/shard_map/ppermute | solution.py:84
  11.1 5.8 %collective-permute-start = (bf16[16,2048]{1,0:T(8,128)(2,1)S(1)}, bf16[16,2048]{1,0:T(8,128)(2,1)S(1)}, u32[]{:S(2)}, u32[]{:S(2)}) collective-permute-start(bf16[16,2048]{1,0:T(8,128)(2,1)S(1)} %bitcast.80), channel_id=1, source_target_pairs={{0,1},{1,2},{2,3},{3,0},{4,5},{5,6},{6,7},{7,4},{8,9},{9,10},{10,1... | collective-permute-start | bytes 196616 | tf_op jit(solution)/shard_map/ppermute | solution.py:84
  12.1 12.7 %collective-permute-start.15 = (bf16[8,8192]{1,0:T(8,128)(2,1)S(1)}, bf16[8,8192]{1,0:T(8,128)(2,1)S(1)}, u32[]{:S(2)}, u32[]{:S(2)}) collective-permute-start(bf16[8,8192]{1,0:T(8,128)(2,1)S(1)} %shard_map.161), channel_id=1, source_target_pairs={{0,24},{1,25},{2,26},{3,27},{4,100},{5,101},{6,102},{7,103},{8,0},... | collective-permute-start | bytes 393224 | tf_op jit(solution)/shard_map/ppermute | solution.py:84
  14.8 10.9 %collective-permute-start.14 = (bf16[8,8192]{1,0:T(8,128)(2,1)S(1)}, bf16[8,8192]{1,0:T(8,128)(2,1)S(1)}, u32[]{:S(2)}, u32[]{:S(2)}) collective-permute-start(bf16[8,8192]{1,0:T(8,128)(2,1)S(1)} %shard_map.161), channel_id=1, source_target_pairs={{0,16},{1,17},{2,18},{3,19},{4,68},{5,69},{6,70},{7,71},{8,24},{9,... | collective-permute-start | bytes 393224 | tf_op jit(solution)/shard_map/ppermute | solution.py:84
  15.7 10.0 %collective-permute-start.13 = (bf16[8,8192]{1,0:T(8,128)(2,1)S(1)}, bf16[8,8192]{1,0:T(8,128)(2,1)S(1)}, u32[]{:S(2)}, u32[]{:S(2)}) collective-permute-start(bf16[8,8192]{1,0:T(8,128)(2,1)S(1)} %shard_map.161), channel_id=1, source_target_pairs={{0,8},{1,9},{2,10},{3,11},{4,36},{5,37},{6,38},{7,39},{8,16},{9,17... | collective-permute-start | bytes 393224 | tf_op jit(solution)/shard_map/ppermute | solution.py:84
  21.1 15.7 %collective-permute-start.5 = (bf16[8,8192]{1,0:T(8,128)(2,1)S(1)}, bf16[8,8192]{1,0:T(8,128)(2,1)S(1)}, u32[]{:S(2)}, u32[]{:S(2)}) collective-permute-start(bf16[8,8192]{1,0:T(8,128)(2,1)S(1)} %get-tuple-element.40), channel_id=1, source_target_pairs={{0,24},{1,25},{2,26},{3,27},{4,100},{5,101},{6,102},{7,103},{8,0},... | collective-permute-start | bytes 393224 | tf_op jit(solution)/shard_map/ppermute | solution.py:84
  23.9 11.8 %collective-permute-start.4 = (bf16[8,8192]{1,0:T(8,128)(2,1)S(1)}, bf16[8,8192]{1,0:T(8,128)(2,1)S(1)}, u32[]{:S(2)}, u32[]{:S(2)}) collective-permute-start(bf16[8,8192]{1,0:T(8,128)(2,1)S(1)} %get-tuple-element.40), channel_id=1, source_target_pairs={{0,16},{1,17},{2,18},{3,19},{4,68},{5,69},{6,70},{7,71},{8,24},{9,... | collective-permute-start | bytes 393224 | tf_op jit(solution)/shard_map/ppermute | solution.py:84
  24.8 7.1 %collective-permute-start.3 = (bf16[8,8192]{1,0:T(8,128)(2,1)S(1)}, bf16[8,8192]{1,0:T(8,128)(2,1)S(1)}, u32[]{:S(2)}, u32[]{:S(2)}) collective-permute-start(bf16[8,8192]{1,0:T(8,128)(2,1)S(1)} %get-tuple-element.40), channel_id=1, source_target_pairs={{0,8},{1,9},{2,10},{3,11},{4,36},{5,37},{6,38},{7,39},{8,16},{9,17... | collective-permute-start | bytes 393224 | tf_op jit(solution)/shard_map/ppermute | solution.py:84
  25.8 13.4 %collective-permute-start.19 = (bf16[32,8192]{1,0:T(8,128)(2,1)S(1)}, bf16[32,8192]{1,0:T(8,128)(2,1)S(1)}, u32[]{:S(2)}, u32[]{:S(2)}) collective-permute-start(bf16[32,8192]{1,0:T(8,128)(2,1)S(1)} %pad_maximum_fusion.refs_0_), channel_id=1, source_target_pairs={{0,4},{1,5},{2,6},{3,7},{4,0},{5,1},{6,2},{7,3},{8,12},{9,13},{10,... | collective-permute-start | bytes 1572872 | tf_op jit(solution)/shard_map/ppermute | solution.py:84
  25.9 13.3 %collective-permute-start.18 = (bf16[32,8192]{1,0:T(8,128)(2,1)S(1)}, bf16[32,8192]{1,0:T(8,128)(2,1)S(1)}, u32[]{:S(2)}, u32[]{:S(2)}) collective-permute-start(bf16[32,8192]{1,0:T(8,128)(2,1)S(1)} %pad_maximum_fusion.refs_0_), channel_id=1, source_target_pairs={{0,96},{1,97},{2,98},{3,99},{4,28},{5,29},{6,30},{7,31},{8,104},{9... | collective-permute-start | bytes 1572872 | tf_op jit(solution)/shard_map/ppermute | solution.py:84
  31.8 11.1 %collective-permute-start.17 = (bf16[32,8192]{1,0:T(8,128)(2,1)S(1)}, bf16[32,8192]{1,0:T(8,128)(2,1)S(1)}, u32[]{:S(2)}, u32[]{:S(2)}) collective-permute-start(bf16[32,8192]{1,0:T(8,128)(2,1)S(1)} %pad_maximum_fusion.refs_0_), channel_id=1, source_target_pairs={{0,64},{1,65},{2,66},{3,67},{4,20},{5,21},{6,22},{7,23},{8,72},{9,... | collective-permute-start | bytes 1572872 | tf_op jit(solution)/shard_map/ppermute | solution.py:84
  35.7 12.8 %collective-permute-start.16 = (bf16[32,8192]{1,0:T(8,128)(2,1)S(1)}, bf16[32,8192]{1,0:T(8,128)(2,1)S(1)}, u32[]{:S(2)}, u32[]{:S(2)}) collective-permute-start(bf16[32,8192]{1,0:T(8,128)(2,1)S(1)} %pad_maximum_fusion.refs_0_), channel_id=1, source_target_pairs={{0,32},{1,33},{2,34},{3,35},{4,12},{5,13},{6,14},{7,15},{8,40},{9,... | collective-permute-start | bytes 1572872 | tf_op jit(solution)/shard_map/ppermute | solution.py:84
  36.9 12.7 %collective-permute-start.8 = (bf16[32,8192]{1,0:T(8,128)(2,1)S(1)}, bf16[32,8192]{1,0:T(8,128)(2,1)S(1)}, u32[]{:S(2)}, u32[]{:S(2)}) collective-permute-start(bf16[32,8192]{1,0:T(8,128)(2,1)S(1)} %constant_dynamic-update-slice_fusion.refs_0_.refs_3_.refs_8_), channel_id=1, source_target_pairs={{0,96},{1,97},{2,98},{3,99},{4,28},{5,29},{6,30},{7,31},{8,104},{9... | collective-permute-start | bytes 1572872 | tf_op jit(solution)/shard_map/ppermute | solution.py:84
  39.1 15.1 %collective-permute-start.7 = (bf16[32,8192]{1,0:T(8,128)(2,1)S(1)}, bf16[32,8192]{1,0:T(8,128)(2,1)S(1)}, u32[]{:S(2)}, u32[]{:S(2)}) collective-permute-start(bf16[32,8192]{1,0:T(8,128)(2,1)S(1)} %constant_dynamic-update-slice_fusion.refs_0_.refs_3_.refs_8_), channel_id=1, source_target_pairs={{0,64},{1,65},{2,66},{3,67},{4,20},{5,21},{6,22},{7,23},{8,72},{9,... | collective-permute-start | bytes 1572872 | tf_op jit(solution)/shard_map/ppermute | solution.py:84
  39.2 20.5 %collective-permute-start.6 = (bf16[32,8192]{1,0:T(8,128)(2,1)S(1)}, bf16[32,8192]{1,0:T(8,128)(2,1)S(1)}, u32[]{:S(2)}, u32[]{:S(2)}) collective-permute-start(bf16[32,8192]{1,0:T(8,128)(2,1)S(1)} %constant_dynamic-update-slice_fusion.refs_0_.refs_3_.refs_8_), channel_id=1, source_target_pairs={{0,32},{1,33},{2,34},{3,35},{4,12},{5,13},{6,14},{7,15},{8,40},{9,... | collective-permute-start | bytes 1572872 | tf_op jit(solution)/shard_map/ppermute | solution.py:84
  43.0 16.8 %collective-permute-start.22 = (bf16[32,8192]{1,0:T(8,128)(2,1)S(1)}, bf16[32,8192]{1,0:T(8,128)(2,1)S(1)}, u32[]{:S(2)}, u32[]{:S(2)}) collective-permute-start(bf16[32,8192]{1,0:T(8,128)(2,1)S(1)} %collective-permute-done.18.refs_3_), channel_id=1, source_target_pairs={{0,4},{1,5},{2,6},{3,7},{4,0},{5,1},{6,2},{7,3},{8,12},{9,13},{10,... | collective-permute-start | bytes 1572872 | tf_op jit(solution)/shard_map/ppermute | solution.py:84
  48.5 11.8 %collective-permute-start.21 = (bf16[32,8192]{1,0:T(8,128)(2,1)S(1)}, bf16[32,8192]{1,0:T(8,128)(2,1)S(1)}, u32[]{:S(2)}, u32[]{:S(2)}) collective-permute-start(bf16[32,8192]{1,0:T(8,128)(2,1)S(1)} %collective-permute-done.17.refs_2_), channel_id=1, source_target_pairs={{0,4},{1,5},{2,6},{3,7},{4,0},{5,1},{6,2},{7,3},{8,12},{9,13},{10,... | collective-permute-start | bytes 1572872 | tf_op jit(solution)/shard_map/ppermute | solution.py:84
  49.5 17.2 %collective-permute-start.9 = (bf16[32,8192]{1,0:T(8,128)(2,1)S(1)}, bf16[32,8192]{1,0:T(8,128)(2,1)}, u32[]{:S(2)}, u32[]{:S(2)}) collective-permute-start(bf16[32,8192]{1,0:T(8,128)(2,1)S(1)} %constant_dynamic-update-slice_fusion.refs_0_.refs_3_.refs_8_), channel_id=1, source_target_pairs={{0,4},{1,5},{2,6},{3,7},{4,0},{5,1},{6,2},{7,3},{8,12},{9,13},{10,... | collective-permute-start | bytes 1572872 | tf_op jit(solution)/shard_map/ppermute | solution.py:84
  54.2 6.8 %collective-permute-start.20 = (bf16[32,8192]{1,0:T(8,128)(2,1)S(1)}, bf16[32,8192]{1,0:T(8,128)(2,1)}, u32[]{:S(2)}, u32[]{:S(2)}) collective-permute-start(bf16[32,8192]{1,0:T(8,128)(2,1)S(1)} %collective-permute-done.16.refs_1_), channel_id=1, source_target_pairs={{0,4},{1,5},{2,6},{3,7},{4,0},{5,1},{6,2},{7,3},{8,12},{9,13},{10,... | collective-permute-start | bytes 1572872 | tf_op jit(solution)/shard_map/ppermute | solution.py:84
  59.7 7.0 %collective-permute-start.12 = (bf16[32,8192]{1,0:T(8,128)(2,1)S(1)}, bf16[32,8192]{1,0:T(8,128)(2,1)}, u32[]{:S(2)}, u32[]{:S(2)}) collective-permute-start(bf16[32,8192]{1,0:T(8,128)(2,1)S(1)} %collective-permute-done.8.refs_3_.refs_6_.refs_11_), channel_id=1, source_target_pairs={{0,4},{1,5},{2,6},{3,7},{4,0},{5,1},{6,2},{7,3},{8,12},{9,13},{10,... | collective-permute-start | bytes 1572872 | tf_op jit(solution)/shard_map/ppermute | solution.py:84
  59.7 7.0 %collective-permute-start.11 = (bf16[32,8192]{1,0:T(8,128)(2,1)S(1)}, bf16[32,8192]{1,0:T(8,128)(2,1)}, u32[]{:S(2)}, u32[]{:S(2)}) collective-permute-start(bf16[32,8192]{1,0:T(8,128)(2,1)S(1)} %collective-permute-done.7.refs_2_.refs_5_.refs_10_), channel_id=1, source_target_pairs={{0,4},{1,5},{2,6},{3,7},{4,0},{5,1},{6,2},{7,3},{8,12},{9,13},{10,... | collective-permute-start | bytes 1572872 | tf_op jit(solution)/shard_map/ppermute | solution.py:84
  60.2 6.5 %collective-permute-start.10 = (bf16[32,8192]{1,0:T(8,128)(2,1)S(1)}, bf16[32,8192]{1,0:T(8,128)(2,1)}, u32[]{:S(2)}, u32[]{:S(2)}) collective-permute-start(bf16[32,8192]{1,0:T(8,128)(2,1)S(1)} %collective-permute-done.6.refs_1_.refs_4_.refs_9_), channel_id=1, source_target_pairs={{0,4},{1,5},{2,6},{3,7},{4,0},{5,1},{6,2},{7,3},{8,12},{9,13},{10,... | collective-permute-start | bytes 1572872 | tf_op jit(solution)/shard_map/ppermute | solution.py:84
  76.5 8.3 %collective-permute-start.23 = (bf16[128,8192]{1,0:T(8,128)(2,1)}, bf16[128,8192]{1,0:T(8,128)(2,1)S(1)}, u32[]{:S(2)}, u32[]{:S(2)}) collective-permute-start(bf16[128,8192]{1,0:T(8,128)(2,1)} %get-tuple-element.43), channel_id=1, source_target_pairs={{0,4},{1,5},{2,6},{3,7},{4,0},{5,1},{6,2},{7,3},{8,12},{9,13},{10,... | collective-permute-start | bytes 6291464 | tf_op jit(solution)/shard_map/ppermute | solution.py:84
  81.4 16.0 %collective-permute-start.24 = (bf16[128,8192]{1,0:T(8,128)(2,1)}, bf16[128,8192]{1,0:T(8,128)(2,1)}, u32[]{:S(2)}, u32[]{:S(2)}) collective-permute-start(bf16[128,8192]{1,0:T(8,128)(2,1)} %shard_map.165), channel_id=1, source_target_pairs={{0,4},{1,5},{2,6},{3,7},{4,0},{5,1},{6,2},{7,3},{8,12},{9,13},{10,... | collective-permute-start | bytes 6291464 | tf_op jit(solution)/shard_map/ppermute | solution.py:84
  92.0 13.3 %collective-permute-start.34 = (bf16[32,8192]{1,0:T(8,128)(2,1)}, bf16[32,8192]{1,0:T(8,128)(2,1)S(1)}, u32[]{:S(2)}, u32[]{:S(2)}) collective-permute-start(bf16[32,8192]{1,0:T(8,128)(2,1)} %get-tuple-element.52), channel_id=1, source_target_pairs={{0,96},{1,97},{2,98},{3,99},{4,28},{5,29},{6,30},{7,31},{8,104},{9... | collective-permute-start | bytes 1572872 | tf_op jit(solution)/shard_map/ppermute | solution.py:84
  92.7 13.5 %collective-permute-start.35 = (bf16[32,8192]{1,0:T(8,128)(2,1)}, bf16[32,8192]{1,0:T(8,128)(2,1)S(1)}, u32[]{:S(2)}, u32[]{:S(2)}) collective-permute-start(bf16[32,8192]{1,0:T(8,128)(2,1)} %get-tuple-element.53), channel_id=1, source_target_pairs={{0,64},{1,65},{2,66},{3,67},{4,20},{5,21},{6,22},{7,23},{8,72},{9,... | collective-permute-start | bytes 1572872 | tf_op jit(solution)/shard_map/ppermute | solution.py:84
  96.2 13.0 %collective-permute-start.36 = (bf16[32,8192]{1,0:T(8,128)(2,1)}, bf16[32,8192]{1,0:T(8,128)(2,1)S(1)}, u32[]{:S(2)}, u32[]{:S(2)}) collective-permute-start(bf16[32,8192]{1,0:T(8,128)(2,1)} %get-tuple-element.54), channel_id=1, source_target_pairs={{0,32},{1,33},{2,34},{3,35},{4,12},{5,13},{6,14},{7,15},{8,40},{9,... | collective-permute-start | bytes 1572872 | tf_op jit(solution)/shard_map/ppermute | solution.py:84
  102.4 16.6 %collective-permute-start.25 = (bf16[32,8192]{1,0:T(8,128)(2,1)}, bf16[32,8192]{1,0:T(8,128)(2,1)}, u32[]{:S(2)}, u32[]{:S(2)}) collective-permute-start(bf16[32,8192]{1,0:T(8,128)(2,1)} %get-tuple-element.49), channel_id=1, source_target_pairs={{0,96},{1,97},{2,98},{3,99},{4,28},{5,29},{6,30},{7,31},{8,104},{9... | collective-permute-start | bytes 1572872 | tf_op jit(solution)/shard_map/ppermute | solution.py:84
  105.2 13.8 %collective-permute-start.26 = (bf16[32,8192]{1,0:T(8,128)(2,1)}, bf16[32,8192]{1,0:T(8,128)(2,1)}, u32[]{:S(2)}, u32[]{:S(2)}) collective-permute-start(bf16[32,8192]{1,0:T(8,128)(2,1)} %get-tuple-element.50), channel_id=1, source_target_pairs={{0,64},{1,65},{2,66},{3,67},{4,20},{5,21},{6,22},{7,23},{8,72},{9,... | collective-permute-start | bytes 1572872 | tf_op jit(solution)/shard_map/ppermute | solution.py:84
  105.2 16.3 %collective-permute-start.27 = (bf16[32,8192]{1,0:T(8,128)(2,1)}, bf16[32,8192]{1,0:T(8,128)(2,1)}, u32[]{:S(2)}, u32[]{:S(2)}) collective-permute-start(bf16[32,8192]{1,0:T(8,128)(2,1)} %get-tuple-element.51), channel_id=1, source_target_pairs={{0,32},{1,33},{2,34},{3,35},{4,12},{5,13},{6,14},{7,15},{8,40},{9,... | collective-permute-start | bytes 1572872 | tf_op jit(solution)/shard_map/ppermute | solution.py:84
  109.4 9.3 %collective-permute-start.43 = (f32[1,8192]{1,0:T(1,128)S(1)}, f32[1,8192]{1,0:T(1,128)S(1)}, u32[]{:S(2)}, u32[]{:S(2)}) collective-permute-start(f32[1,8192]{1,0:T(1,128)S(1)} %copy-done.33), channel_id=1, source_target_pairs={{0,4},{1,5},{2,6},{3,7},{4,0},{5,1},{6,2},{7,3},{8,12},{9,13},{10,... | collective-permute-start | bytes 98312 | tf_op jit(solution)/shard_map/ppermute | solution.py:84
  123.3 5.7 %collective-permute-start.45 = (f32[1,8192]{1,0:T(1,128)S(1)}, f32[1,8192]{1,0:T(1,128)S(1)}, u32[]{:S(2)}, u32[]{:S(2)}) collective-permute-start(f32[1,8192]{1,0:T(1,128)S(1)} %add.139), channel_id=1, source_target_pairs={{0,16},{1,17},{2,18},{3,19},{4,20},{5,21},{6,22},{7,23},{8,24},{9,... | collective-permute-start | bytes 98312 | tf_op jit(solution)/shard_map/ppermute | solution.py:84
  124.2 10.3 %collective-permute-start.28 = (bf16[8,8192]{1,0:T(8,128)(2,1)S(1)}, bf16[8,8192]{1,0:T(8,128)(2,1)S(1)}, u32[]{:S(2)}, u32[]{:S(2)}) collective-permute-start(bf16[8,8192]{1,0:T(8,128)(2,1)S(1)} %get-tuple-element.74), channel_id=1, source_target_pairs={{0,24},{1,25},{2,26},{3,27},{4,100},{5,101},{6,102},{7,103},{8,0},... | collective-permute-start | bytes 393224 | tf_op jit(solution)/shard_map/ppermute | solution.py:84
  125.8 10.9 %collective-permute-start.30 = (bf16[8,8192]{1,0:T(8,128)(2,1)S(1)}, bf16[8,8192]{1,0:T(8,128)(2,1)S(1)}, u32[]{:S(2)}, u32[]{:S(2)}) collective-permute-start(bf16[8,8192]{1,0:T(8,128)(2,1)S(1)} %get-tuple-element.75), channel_id=1, source_target_pairs={{0,8},{1,9},{2,10},{3,11},{4,36},{5,37},{6,38},{7,39},{8,16},{9,17... | collective-permute-start | bytes 393224 | tf_op jit(solution)/shard_map/ppermute | solution.py:84
  126.3 10.5 %collective-permute-start.29 = (bf16[8,8192]{1,0:T(8,128)(2,1)S(1)}, bf16[8,8192]{1,0:T(8,128)(2,1)S(1)}, u32[]{:S(2)}, u32[]{:S(2)}) collective-permute-start(bf16[8,8192]{1,0:T(8,128)(2,1)S(1)} %get-tuple-element.76), channel_id=1, source_target_pairs={{0,16},{1,17},{2,18},{3,19},{4,68},{5,69},{6,70},{7,71},{8,24},{9,... | collective-permute-start | bytes 393224 | tf_op jit(solution)/shard_map/ppermute | solution.py:84
  130.8 20.9 %collective-permute-start.37 = (f32[8,8192]{1,0:T(8,128)S(1)}, f32[8,8192]{1,0:T(8,128)S(1)}, u32[]{:S(2)}, u32[]{:S(2)}) collective-permute-start(f32[8,8192]{1,0:T(8,128)S(1)} %get-tuple-element.71), channel_id=1, source_target_pairs={{0,24},{1,25},{2,26},{3,27},{4,100},{5,101},{6,102},{7,103},{8,0},... | collective-permute-start | bytes 786440 | tf_op jit(solution)/shard_map/ppermute | solution.py:84
  133.5 18.4 %collective-permute-start.39 = (f32[8,8192]{1,0:T(8,128)S(1)}, f32[8,8192]{1,0:T(8,128)S(1)}, u32[]{:S(2)}, u32[]{:S(2)}) collective-permute-start(f32[8,8192]{1,0:T(8,128)S(1)} %get-tuple-element.72), channel_id=1, source_target_pairs={{0,8},{1,9},{2,10},{3,11},{4,36},{5,37},{6,38},{7,39},{8,16},{9,17... | collective-permute-start | bytes 786440 | tf_op jit(solution)/shard_map/ppermute | solution.py:84
  134.4 5.5 %collective-permute-start.47 = (f32[1,8192]{1,0:T(1,128)S(1)}, f32[1,8192]{1,0:T(1,128)S(1)}, u32[]{:S(2)}, u32[]{:S(2)}) collective-permute-start(f32[1,8192]{1,0:T(1,128)S(1)} %add.141), channel_id=1, source_target_pairs={{0,64},{1,65},{2,66},{3,67},{4,68},{5,69},{6,70},{7,71},{8,72},{9,... | collective-permute-start | bytes 98312 | tf_op jit(solution)/shard_map/ppermute | solution.py:84
  141.9 5.8 %collective-permute-start.49 = (f32[1,8192]{1,0:T(1,128)S(1)}, f32[1,8192]{1,0:T(1,128)S(1)}, u32[]{:S(2)}, u32[]{:S(2)}) collective-permute-start(f32[1,8192]{1,0:T(1,128)S(1)} %add.142), channel_id=1, source_target_pairs={{0,2},{1,3},{2,0},{3,1},{4,6},{5,7},{6,4},{7,5},{8,10},{9,11},{10,... | collective-permute-start | bytes 98312 | tf_op jit(solution)/shard_map/ppermute | solution.py:84
  143.6 5.1 %collective-permute-start.48 = (f32[1,8192]{1,0:T(1,128)S(1)}, f32[1,8192]{1,0:T(1,128)S(1)}, u32[]{:S(2)}, u32[]{:S(2)}) collective-permute-start(f32[1,8192]{1,0:T(1,128)S(1)} %add.142), channel_id=1, source_target_pairs={{0,1},{1,2},{2,3},{3,0},{4,5},{5,6},{6,7},{7,4},{8,9},{9,10},{10,1... | collective-permute-start | bytes 98312 | tf_op jit(solution)/shard_map/ppermute | solution.py:84
  144.0 7.9 %collective-permute-start.38 = (f32[8,8192]{1,0:T(8,128)S(1)}, f32[8,8192]{1,0:T(8,128)S(1)}, u32[]{:S(2)}, u32[]{:S(2)}) collective-permute-start(f32[8,8192]{1,0:T(8,128)S(1)} %get-tuple-element.73), channel_id=1, source_target_pairs={{0,16},{1,17},{2,18},{3,19},{4,68},{5,69},{6,70},{7,71},{8,24},{9,... | collective-permute-start | bytes 786440 | tf_op jit(solution)/shard_map/ppermute | solution.py:84
  147.7 8.0 %collective-permute-start.31 = (bf16[4,8192]{1,0:T(4,128)(2,1)S(1)}, bf16[4,8192]{1,0:T(4,128)(2,1)S(1)}, u32[]{:S(2)}, u32[]{:S(2)}) collective-permute-start(bf16[4,8192]{1,0:T(4,128)(2,1)S(1)} %get-tuple-element.77), channel_id=1, source_target_pairs={{0,1},{1,2},{2,3},{3,0},{4,5},{5,6},{6,7},{7,4},{8,9},{9,10},{10,1... | collective-permute-start | bytes 196616 | tf_op jit(solution)/shard_map/ppermute | solution.py:84
  148.7 8.1 %collective-permute-start.33 = (bf16[4,8192]{1,0:T(4,128)(2,1)S(1)}, bf16[4,8192]{1,0:T(4,128)(2,1)S(1)}, u32[]{:S(2)}, u32[]{:S(2)}) collective-permute-start(bf16[4,8192]{1,0:T(4,128)(2,1)S(1)} %get-tuple-element.78), channel_id=1, source_target_pairs={{0,3},{1,0},{2,1},{3,2},{4,7},{5,4},{6,5},{7,6},{8,11},{9,8},{10,9... | collective-permute-start | bytes 196616 | tf_op jit(solution)/shard_map/ppermute | solution.py:84
  151.7 6.1 %collective-permute-start.32 = (bf16[4,8192]{1,0:T(4,128)(2,1)S(1)}, bf16[4,8192]{1,0:T(4,128)(2,1)S(1)}, u32[]{:S(2)}, u32[]{:S(2)}) collective-permute-start(bf16[4,8192]{1,0:T(4,128)(2,1)S(1)} %get-tuple-element.79), channel_id=1, source_target_pairs={{0,2},{1,3},{2,0},{3,1},{4,6},{5,7},{6,4},{7,5},{8,10},{9,11},{10,... | collective-permute-start | bytes 196616 | tf_op jit(solution)/shard_map/ppermute | solution.py:84
  151.9 6.7 %collective-permute-start.42 = (bf16[8,8192]{1,0:T(8,128)(2,1)S(1)}, bf16[8,8192]{1,0:T(8,128)(2,1)S(1)}, u32[]{:S(2)}, u32[]{:S(2)}) collective-permute-start(bf16[8,8192]{1,0:T(8,128)(2,1)S(1)} %fusion.12.refs_0_), channel_id=1, source_target_pairs={{0,3},{1,0},{2,1},{3,2},{4,7},{5,4},{6,5},{7,6},{8,11},{9,8},{10,9... | collective-permute-start | bytes 393224 | tf_op jit(solution)/shard_map/ppermute | solution.py:84
  155.0 6.6 %collective-permute-start.41 = (bf16[8,8192]{1,0:T(8,128)(2,1)S(1)}, bf16[8,8192]{1,0:T(8,128)(2,1)S(1)}, u32[]{:S(2)}, u32[]{:S(2)}) collective-permute-start(bf16[8,8192]{1,0:T(8,128)(2,1)S(1)} %fusion.12.refs_0_), channel_id=1, source_target_pairs={{0,2},{1,3},{2,0},{3,1},{4,6},{5,7},{6,4},{7,5},{8,10},{9,11},{10,... | collective-permute-start | bytes 393224 | tf_op jit(solution)/shard_map/ppermute | solution.py:84
  155.7 7.2 %collective-permute-start.40 = (bf16[8,8192]{1,0:T(8,128)(2,1)S(1)}, bf16[8,8192]{1,0:T(8,128)(2,1)S(1)}, u32[]{:S(2)}, u32[]{:S(2)}) collective-permute-start(bf16[8,8192]{1,0:T(8,128)(2,1)S(1)} %fusion.12.refs_0_), channel_id=1, source_target_pairs={{0,1},{1,2},{2,3},{3,0},{4,5},{5,6},{6,7},{7,4},{8,9},{9,10},{10,1... | collective-permute-start | bytes 393224 | tf_op jit(solution)/shard_map/ppermute | solution.py:84
  (41 other events, 644.4 us)

commit v3 on v2

--- a/solution.py
+++ b/solution.py
@@ -17,7 +17,7 @@
 BF = jnp.bfloat16
 F32 = jnp.float32
 CAP = 8
-VMEM = 60 * 1024 * 1024
+VMEM = 46 * 1024 * 1024
 
 
 def causal_forward(queries, keys, values):
@@ -96,12 +96,12 @@
     return send(block, _pairs(lambda z, x, c, s: (z, x, c, s + shift)))
 
 
-def gather_rows(block):
-    near = [block] + [send_stage(block, True, k) for k in (1, 2, 3)]
-    near = jnp.concatenate(near, axis=0)
-    own = [near] + [send_stage(near, False, k) for k in (1, 2, 3)]
-    other = [swap_core(piece) for piece in own]
-    return own + other
+def gather_near(block):
+    return jnp.concatenate([block] + [send_stage(block, True, k) for k in (1, 2, 3)], axis=0)
+
+
+def gather_far(near):
+    return [near] + [send_stage(near, False, k) for k in (1, 2, 3)]
 
 
 def _params(limit=VMEM):
@@ -154,7 +154,7 @@
         in_specs=[SMALL, SMALL] + _whole(labels, rows),
         out_specs=_whole(out)[0],
         out_shape=out,
-        compiler_params=_params(8 * 1024 * 1024),
+        compiler_params=_params(),
         cost_estimate=SMALL_COST,
     )(slot, kinds, labels, rows)
 
@@ -189,20 +189,29 @@
         out_specs=_whole(*outs),
         out_shape=outs,
         scratch_shapes=[pltpu.VMEM((length, width), BF)],
-        compiler_params=_params(8 * 1024 * 1024),
+        compiler_params=_params(),
         cost_estimate=SMALL_COST,
     )(slot, kinds, labels, column, residual, gains, *blocks)
 
 
 def _finish_kernel(slot_ref, kinds_ref, column_ref, hidden_ref, cot_ref, gains_ref, *refs):
-    sums, (quarter_ref, block_ref, full_ref) = refs[:NS], refs[NS:]
+    sums, (quarter_ref, block_ref, gain_ref, full_ref) = refs[:NS], refs[NS:]
     slot = slot_ref[0]
     labels = column_ref[...]
-    spreaders = [
-        _slot_spreader(labels, kinds_ref[lax.rem(slot - k + NS, NS)]) for k in range(NS)
+    kinds = [kinds_ref[lax.rem(slot - k + NS, NS)] for k in range(NS)]
+    spreaders = [_slot_spreader(labels, kind) for kind in kinds]
+    spread = jnp.concatenate(spreaders, axis=1).astype(BF)
+    wide = hidden_ref.shape[1]
+    rows = jnp.concatenate([s[:, :wide].astype(F32) for s in sums], axis=0).astype(BF)
+    extra = wide // CAP
+    parts = [
+        s[:, wide : wide + extra].astype(F32) + s[:, wide + extra :].astype(F32) for s in sums
     ]
-    spread = jnp.concatenate(spreaders, axis=1).astype(BF)
-    rows = jnp.concatenate([s[...].astype(F32) for s in sums], axis=0).astype(BF)
+    for m in range(MODALITIES):
+        gain = jnp.zeros_like(parts[0])
+        for kind, part in zip(kinds, parts):
+            gain = gain + jnp.where(kind == m, part, 0.0)
+        gain_ref[m * CAP : (m + 1) * CAP, :] = gain
     norm_grad = jnp.dot(spread, rows, preferred_element_type=F32)
     hidden_f = hidden_ref[...].astype(F32)
     inverse = lax.rsqrt(jnp.mean(hidden_f * hidden_f, axis=-1, keepdims=True) + 1e-05)
@@ -226,6 +235,7 @@
     outs = [
         jax.ShapeDtypeStruct((length // NS, width), BF),
         jax.ShapeDtypeStruct((length, block_width), BF),
+        jax.ShapeDtypeStruct((MODALITIES * CAP, width // CAP), F32),
     ]
     return pl.pallas_call(
         _finish_kernel,
@@ -234,9 +244,30 @@
         out_specs=_whole(*outs),
         out_shape=outs,
         scratch_shapes=[pltpu.VMEM((length, width), BF)],
-        compiler_params=_params(12 * 1024 * 1024),
+        compiler_params=_params(),
         cost_estimate=SMALL_COST,
     )(slot, kinds, column, hidden, cot, gains, *sums)
+
+
+HELD = pl.BlockSpec(memory_space=pltpu.VMEM)
+
+
+def _load_kernel(w_hbm, out_ref, sem):
+    copy = pltpu.make_async_copy(w_hbm.at[0], out_ref, sem)
+    copy.start()
+    copy.wait()
+
+
+def load_weight(weight):
+    return pl.pallas_call(
+        _load_kernel,
+        in_specs=[RAW],
+        out_specs=HELD,
+        out_shape=pltpu.VMEM(weight.shape[1:], weight.dtype),
+        scratch_shapes=[pltpu.SemaphoreType.DMA],
+        compiler_params=_params(),
+        cost_estimate=SMALL_COST,
+    )(weight)
 
 
 def _back_kernel(*refs):
@@ -274,16 +305,16 @@
 
 
 def _pre_kernel(*refs):
-    pieces, w_hbm, back_ref = refs[:8], refs[8], refs[9]
+    pieces, w_ref, back_ref = refs[:8], refs[8], refs[9]
     act_t_ref, grad_t_ref, act_ref, grad_ref, other_hbm = refs[10:15]
-    rows_ref, w_ref, acc_ref, other_ref, sems, out_sems = refs[15:]
+    rows_ref, acc_ref, other_ref, sems, out_sems = refs[15:]
     width = w_ref.shape[1]
     size = width // CHUNKS
     part = pieces[0].shape[0]
     copies = []
     for c in range(CHUNKS):
         span = pl.ds(c * size, size)
-        group = [pltpu.make_async_copy(w_hbm.at[0, :, span], w_ref.at[:, span], sems.at[c, 8])]
+        group = []
         for p, piece in enumerate(pieces):
             group.append(
                 pltpu.make_async_copy(
@@ -325,7 +356,7 @@
 
 
 def pre_product(pieces, weight, back):
-    hidden, width = weight.shape[1:]
+    hidden, width = weight.shape
     rows = sum(p.shape[0] for p in pieces)
     outs = (
         [jax.ShapeDtypeStruct((hidden, rows), BF)] * 2
@@ -334,16 +365,14 @@
     )
     return pl.pallas_call(
         _pre_kernel,
-        grid=(1,),
-        in_specs=[RAW] * 9 + _whole(back),
-        out_specs=_whole(*outs[:4]) + [RAW],
+        in_specs=[RAW] * 8 + [HELD, HELD],
+        out_specs=[HELD] * 4 + [RAW],
         out_shape=outs,
         scratch_shapes=[
             pltpu.VMEM((rows, width), BF),
-            pltpu.VMEM((hidden, width), BF),
             pltpu.VMEM((hidden, rows), F32),
             pltpu.VMEM((rows // 2, width), BF),
-            pltpu.SemaphoreType.DMA((CHUNKS, 9)),
+            pltpu.SemaphoreType.DMA((CHUNKS, 8)),
             pltpu.SemaphoreType.DMA((width // OUT_STEP,)),
         ],
         compiler_params=_params(),
@@ -351,125 +380,242 @@
     )(*pieces, weight, back)
 
 
-def _other_kernel(left_ref, w_ref, out_ref):
-    out_ref[...] = jnp.dot(left_ref[...], w_ref[...], preferred_element_type=F32).astype(BF)
-
-
-def other_product(left, weight, tile=4096):
-    hidden, width = weight.shape[1:]
+def _other_kernel(left_ref, w_ref, out_hbm, out_ref, sems):
+    half = out_ref.shape[0]
+    left = left_ref[half:, :]
+    copies = []
+    for n in range(out_ref.shape[1] // OUT_STEP):
+        span = pl.ds(n * OUT_STEP, OUT_STEP)
+        out_ref[:, span] = jnp.dot(left, w_ref[:, span], preferred_element_type=F32).astype(BF)
+        copy = pltpu.make_async_copy(out_ref.at[:, span], out_hbm.at[:, span], sems.at[n])
+        copy.start()
+        copies.append(copy)
+    for copy in copies:
+        copy.wait()
+
+
+def other_product(left, weight):
+    width = weight.shape[1]
     half = left.shape[0] // 2
     return pl.pallas_call(
         _other_kernel,
-        grid=(width // tile,),
-        in_specs=[
-            pl.BlockSpec((half, hidden), lambda i: (1, 0)),
-            pl.BlockSpec((None, hidden, tile), lambda i: (0, 0, i)),
-        ],
-        out_specs=pl.BlockSpec((half, tile), lambda i: (0, i)),
+        in_specs=[HELD, HELD],
+        out_specs=RAW,
         out_shape=jax.ShapeDtypeStruct((half, width), BF),
+        scratch_shapes=[pltpu.VMEM((half, width), BF), pltpu.SemaphoreType.DMA((width // OUT_STEP,))],
         compiler_params=_params(),
         cost_estimate=SMALL_COST,
     )(left, weight)
 
 
-def _own_kernel(*refs):
-    left_ref, w_ref, in_ref = refs[:3]
-    rows, outs = refs[3:-4], refs[-4:]
-    total = jnp.dot(left_ref[...], w_ref[...], preferred_element_type=F32)
-    total = total + in_ref[...].astype(F32)
-    part = total.shape[0] // 4
-    if rows:
-        rows, gain_ref, outs = rows[:4], rows[4], outs
-        gain = None
-        for k, row_ref in enumerate(rows):
-            term = jnp.sum(row_ref[...].astype(F32) * total[k * part : (k + 1) * part], axis=0, keepdims=True)
-            gain = term if gain is None else gain + term
-        gain_ref[...] = gain
-    for k, out_ref in enumerate(outs):
-        out_ref[...] = total[k * part : (k + 1) * part].astype(out_ref.dtype)
-
-
-def own_product(left, weight, arrived, rows=(), tile=4096):
-    hidden, width = weight.shape[1:]
+def _split(value):
+    high = value.astype(BF)
+    return high, (value - high.astype(F32)).astype(BF)
+
+
+def _own_kernel(count, left_ref, w_ref, in_hbm, *refs):
+    rows_hbm, outs_hbm = refs[:count], refs[count : count + 4]
+    in_ref, rows_ref, gain_ref = refs[count + 4 : count + 7]
+    outs, (sems, out_sems) = refs[count + 7 : count + 11], refs[count + 11 :]
+    width = w_ref.shape[1]
+    half = in_ref.shape[0]
+    part = half // 4
+    short = width // part
+    groups = []
+    for n in range(width // OUT_STEP):
+        span = pl.ds(n * OUT_STEP, OUT_STEP)
+        group = [pltpu.make_async_copy(in_hbm.at[:, span], in_ref.at[:, span], sems.at[n, 0])]
+        for p, piece in enumerate(rows_hbm):
+            group.append(
+                pltpu.make_async_copy(
+                    piece.at[:, span], rows_ref.at[pl.ds(p * part, part), span], sems.at[n, p + 1]
+                )
+            )
+        for copy in group:
+            copy.start()
+        groups.append(group)
+    copies = []
+
+    def put(span, n):
+        for k in range(4):
+            copy = pltpu.make_async_copy(outs[k].at[:, span], outs_hbm[k].at[:, span], out_sems.at[n, k])
+            copy.start()
+            copies.append(copy)
+
+    for n, group in enumerate(groups):
+        span = pl.ds(n * OUT_STEP, OUT_STEP)
+        total = jnp.dot(left_ref[:half, :], w_ref[:, span], preferred_element_type=F32)
+        for copy in group:
+            copy.wait()
+        total = total + in_ref[:, span].astype(F32)
+        for k, out_ref in enumerate(outs):
+            out_ref[:, span] = total[k * part : (k + 1) * part].astype(out_ref.dtype)
+        put(span, n)
+        if count:
+            gain = jnp.sum(rows_ref[:, span].astype(F32) * total, axis=0, keepdims=True)
+            for j in range(OUT_STEP // short):
+                row = n * (OUT_STEP // short) + j
+                gain_ref[row : row + 1, :] = gain[:, j * short : (j + 1) * short]
+    if count:
+        high, low = _split(gain_ref[...])
+        outs[0][:, width : width + short] = high.astype(F32) + low.astype(F32)
+        outs[0][:, width + short :] = jnp.zeros((part, short), F32)
+        for out_ref in outs[1:]:
+            out_ref[:, width : width + short] = high
+            out_ref[:, width + short :] = low
+        put(pl.ds(width, 2 * short), len(groups))
+    for copy in copies:
+        copy.wait()
+
+
+def own_product(left, weight, arrived, rows=()):
+    hidden, width = weight.shape
     half = left.shape[0] // 2
     part = half // 4
-    piece = pl.BlockSpec((part, tile), lambda i: (0, i))
-    gain_spec = [pl.BlockSpec((1, tile), lambda i: (0, i))] if rows else []
-    gain_shape = [jax.ShapeDtypeStruct((1, width), F32)] if rows else []
-    return pl.pallas_call(
-        _own_kernel,
+    short = width // part
+    wide = width + (2 * short if rows else 0)
+    kinds = [F32, BF, BF, BF]
+    return pl.pallas_call(
+        functools.partial(_own_kernel, len(rows)),
+        in_specs=[HELD, HELD] + [RAW] * (1 + len(rows)),
+        out_specs=[RAW] * 4,
+        out_shape=[jax.ShapeDtypeStruct((part, wide), kind) for kind in kinds],
+        scratch_shapes=[
+            pltpu.VMEM((half, width), BF),
+            pltpu.VMEM((half, width) if rows else (16, 128), BF),
+            pltpu.VMEM((part, short), F32),
+        ]
+        + [pltpu.VMEM((part, wide), kind) for kind in kinds]
+        + [
+            pltpu.SemaphoreType.DMA((width // OUT_STEP, 1 + len(rows))),
+            pltpu.SemaphoreType.DMA((width // OUT_STEP + 1, 4)),
+        ],
+        compiler_params=_params(),
+        cost_estimate=SMALL_COST,
+    )(left, weight, arrived, *rows)
+
+
+def _far_norm_kernel(own_ref, *refs):
+    arrived, outs = refs[:3], refs[3:]
+    part = own_ref.shape[0]
+    width = outs[0].shape[1] * CAP // (CAP + 1)
+    short = width // part
+    total = own_ref[:, :width]
+    for ref in arrived:
+        total = total + ref[:, :width].astype(F32)
+    one, two, three = (
+        ref[:, width : width + short].astype(F32) + ref[:, width + short :].astype(F32) for ref in arrived
+    )
+    gain = (own_ref[:, width : width + short] + two) + (one + three)
+    for k, out_ref in enumerate(outs):
+        out_ref[:, :width] = total[k * CAP : (k + 1) * CAP]
+        for j in range(part // CAP):
+            start = width + j * short
+            out_ref[:, start : start + short] = gain[j * CAP : (j + 1) * CAP]
+
+
+def far_norm_sum(pieces, before):
+    arrived = [send_stage(pieces[k], False, -k) for k in (1, 2, 3)]
+    arrived[0] = after(arrived[0], before)
+    part = pieces[0].shape[0]
+    width = pieces[0].shape[1] * part // (part + 2)
+    outs = [jax.ShapeDtypeStruct((CAP, width + width // CAP), F32)] * 4
+    return pl.pallas_call(
+        _far_norm_kernel,
+        grid=(1,),
+        in_specs=_whole(pieces[0], *arrived),
+        out_specs=_whole(*outs),
+        out_shape=outs,
+        compiler_params=_params(),
+        cost_estimate=SMALL_COST,
+    )(pieces[0], *arrived)
+
+
+def _near_norm_kernel(*refs):
+    zero, one, two, three = (ref[...] for ref in refs[:4])
+    out_ref = refs[4]
+    width = zero.shape[1] * CAP // (CAP + 1)
+    total = (zero + two) + (one + three)
+    high, low = _split(total[:, width:])
+    out_ref[:, :width] = total[:, :width].astype(BF)
+    out_ref[:, width : width + width // CAP] = high
+    out_ref[:, width + width // CAP :] = low
+
+
+def near_norm_sum(blocks, *before):
+    arrived = [send_stage(blocks[k], True, -k) for k in (1, 2, 3)]
+    arrived[0] = after(arrived[0], *before)
+    width = blocks[0].shape[1] * CAP // (CAP + 1)
+    out = jax.ShapeDtypeStruct((CAP, width + 2 * (width // CAP)), BF)
+    return pl.pallas_call(
+        _near_norm_kernel,
+        grid=(1,),
+        in_specs=_whole(blocks[0], *arrived),
+        out_specs=_whole(out)[0],
+        out_shape=out,
+        compiler_params=_params(),
+        cost_estimate=SMALL_COST,
+    )(blocks[0], *arrived)
+
+
+def _near_ffn_kernel(slot_ref, kinds_ref, column_ref, *refs):
+    blocks, outs = refs[:4], refs[4:]
+    total = blocks[0][...]
+    for ref in blocks[1:]:
+        total = total + ref[...].astype(F32)
+    slot = slot_ref[0]
+    spreader = _slot_spreader(column_ref[...], kinds_ref[slot])
+    length = spreader.shape[0]
+    part = length // NS
+    row = lax.broadcasted_iota(jnp.int32, (length, length), 0)
+    token = lax.broadcasted_iota(jnp.int32, (length, length), 1)
+    turned = jnp.where(token == lax.rem(row + slot * part, length), 1.0, 0.0)
+    turned = jnp.dot(turned, spreader, preferred_element_type=F32).astype(BF)
+    rows = jnp.dot(turned, total.astype(BF), preferred_element_type=F32)
+    for k, out_ref in enumerate(outs):
+        out_ref[...] = rows[k * part : (k + 1) * part].astype(BF)
+
+
+def near_ffn_sum(slot, kinds, column, total, before):
+    blocks = [total[k * CAP : (k + 1) * CAP] for k in range(4)]
+    arrived = [send_stage(blocks[k].astype(BF), True, -k) for k in (1, 2, 3)]
+    arrived[0] = after(arrived[0], before)
+    outs = [jax.ShapeDtypeStruct((column.shape[0] // NS, total.shape[1]), BF)] * NS
+    return pl.pallas_call(
+        _near_ffn_kernel,
+        grid=(1,),
+        in_specs=[SMALL, SMALL] + _whole(column, blocks[0], *arrived),
+        out_specs=_whole(*outs),
+        out_shape=outs,
+        compiler_params=_params(),
+        cost_estimate=SMALL_COST,
+    )(slot, kinds, column, blocks[0], *arrived)
+
+
+def _down_kernel(*refs):
+    left_ref, out_ref = refs[8:]
+    rows = jnp.concatenate([p[...] for p in refs[:8]], axis=0)
+    out_ref[...] = jnp.dot(left_ref[...], rows, preferred_element_type=F32).astype(BF)
+
+
+def weight_grad(pieces, left, shape, tile=4096):
+    _, hidden, width = shape
+    count = left.shape[1]
+    weight_spec = pl.BlockSpec((None, hidden, tile), lambda i: (0, 0, i))
+    return pl.pallas_call(
+        _down_kernel,
         grid=(width // tile,),
-        in_specs=[
-            pl.BlockSpec((half, hidden), lambda i: (0, 0)),
-            pl.BlockSpec((None, hidden, tile), lambda i: (0, 0, i)),
-            pl.BlockSpec((half, tile), lambda i: (0, i)),
-        ]
-        + [piece] * len(rows),
-        out_specs=gain_spec + [piece] * 4,
-        out_shape=gain_shape
-        + [jax.ShapeDtypeStruct((part, width), F32)]
-        + [jax.ShapeDtypeStruct((part, width), BF)] * 3,
-        compiler_params=_params(),
-        cost_estimate=SMALL_COST,
-    )(left, weight, arrived, *rows)
-
-
-def _grads_kernel(*refs):
-    cots, rows = refs[:8], refs[8:16]
-    act_ref, grad_ref, down_out, up_out = refs[16:]
-    cot = jnp.concatenate([p[...] for p in cots], axis=0)
-    down_out[...] = jnp.dot(act_ref[...], cot, preferred_element_type=F32).astype(BF)
-    row = jnp.concatenate([p[...] for p in rows], axis=0)
-    up_out[...] = jnp.dot(grad_ref[...], row, preferred_element_type=F32).astype(BF)
-
-
-def grad_products(cots, rows, act_t, grad_t, shape, tile=2048):
-    _, hidden, width = shape
-    count = act_t.shape[1]
-    whole = lambda i: (0, 0)
-    piece_specs = [pl.BlockSpec((p.shape[0], tile), lambda i: (0, i)) for p in cots]
-    weight_spec = pl.BlockSpec((None, hidden, tile), lambda i: (0, 0, i))
-    return pl.pallas_call(
-        _grads_kernel,
-        grid=(width // tile,),
-        in_specs=piece_specs * 2 + [pl.BlockSpec((hidden, count), whole)] * 2,
-        out_specs=[weight_spec, weight_spec],
-        out_shape=[jax.ShapeDtypeStruct(shape, BF)] * 2,
+        in_specs=[pl.BlockSpec((p.shape[0], tile), lambda i: (0, i)) for p in pieces]
+        + [pl.BlockSpec((hidden, count), lambda i: (0, 0))],
+        out_specs=weight_spec,
+        out_shape=jax.ShapeDtypeStruct(shape, BF),
         compiler_params=_params(),
         cost_estimate=pl.CostEstimate(
-            flops=4 * hidden * count * width,
-            bytes_accessed=2 * width * (2 * hidden + 2 * count),
+            flops=2 * hidden * count * width,
+            bytes_accessed=2 * width * (hidden + count),
             transcendentals=0,
         ),
-    )(*cots, *rows, act_t, grad_t)
-
-
-def far_sum(pieces):
-    total = pieces[0]
-    for k in (1, 2, 3):
-        total = total + send_stage(pieces[k], False, -k).astype(F32)
-    return total
-
-
-def near_sum(total, dtype):
-    blocks = [total[k * CAP : (k + 1) * CAP] for k in range(4)]
-    result = blocks[0]
-    for k in (1, 2, 3):
-        result = result + send_stage(blocks[k].astype(dtype), True, -k).astype(F32)
-    return result
-
-
-def sum_over_dp(row):
-    moves = (
-        lambda z, x, c, s: (z, x, 1 - c, s),
-        lambda z, x, c, s: (z, x ^ 1, c, s),
-        lambda z, x, c, s: (z, x ^ 2, c, s),
-        lambda z, x, c, s: (z ^ 1, x, c, s),
-        lambda z, x, c, s: (z ^ 2, x, c, s),
-    )
-    for move in moves:
-        row = row + send(row, _pairs(move))
-    return row
+    )(*pieces, left)
 
 
 def after(value, *others):
@@ -485,59 +631,57 @@
     length = labels.shape[1]
     grad_full = cotangent[0]
     packed_cot = pack_rows(slot, slot_modality, labels, grad_full)
-    cot_rows = gather_rows(packed_cot)
     queries, keys, values, _ = lax.optimization_barrier((queries, keys, values, packed_cot))
+    cot_near = gather_near(packed_cot)
 
     attended_block, probs, probs_b = causal_forward(queries, keys, values)
     block = attended_block[0]
     blocks = [block] + [send_sect(block, k) for k in (1, 2, 3)]
-    hidden, packed = norm_rows_of(slot, slot_modality, labels, column, residual[0], gains, blocks)
-    token_rows = gather_rows(packed)
-
+    hidden, packed = norm_rows_of(
+        slot, slot_modality, labels, column, after(residual[0], cot_near), gains, blocks
+    )
+    cot_far = gather_far(cot_near)
+    cot_rows = cot_far + [swap_core(piece) for piece in cot_far]
+    near = gather_near(after(packed, *cot_far[1:]))
+    far = gather_far(near)
     back = back_product(cot_rows, down_weight)
-    act_t, grad_t, act, grad, norm_other = pre_product(token_rows, up_weight, back)
+    up_held = load_weight(up_weight)
+    down_held = load_weight(down_weight)
+    far[3] = after(far[3], back, up_held, down_held)
+    token_rows = far + [swap_core(piece) for piece in far]
+
+    act_t, grad_t, act, grad, norm_other = pre_product(token_rows, up_held, back)
     norm_arrived = swap_core(norm_other)
-    ffn_other = other_product(after(act, norm_other), down_weight)
+    ffn_other = other_product(after(act, norm_other), down_held)
     ffn_arrived = swap_core(ffn_other)
-    gain_part, *norm_pieces = own_product(after(grad, ffn_other), up_weight, norm_arrived, token_rows[:4])
-    ffn_pieces = own_product(after(act, norm_pieces[0]), down_weight, ffn_arrived)
-    down_grad, up_grad = grad_products(
-        cot_rows, token_rows, after(act_t, ffn_pieces[0]), grad_t, up_weight.shape
-    )
-    norm_total = far_sum(norm_pieces)
-    norm_rows = near_sum(norm_total, F32).astype(BF)
+    norm_pieces = own_product(after(grad, ffn_other), up_held, norm_arrived, far)
+    ffn_pieces = own_product(after(act, norm_pieces[0]), down_held, ffn_arrived)
+    down_grad = weight_grad(cot_rows, after(act_t, ffn_pieces[0]), up_weight.shape)
+    norm_blocks = far_norm_sum(norm_pieces, down_grad)
+    up_grad = weight_grad(token_rows, after(grad_t, norm_blocks[0]), up_weight.shape)
+    ffn_arrived = [send_stage(ffn_pieces[k], False, -k) for k in (1, 2, 3)]
+    norm_rows = near_norm_sum(norm_blocks, up_grad, *ffn_arrived)
+    ffn_total = after(ffn_pieces[0], norm_rows) + sum(piece.astype(F32) for piece in ffn_arrived)
     sums = [norm_rows] + [send_sect(norm_rows, k) for k in (1, 2, 3)]
-    residual_grad, grad_block = finish_norm(
+    residual_grad, grad_block, gain_part = finish_norm(
         slot, slot_modality, column, hidden, grad_full, gains, sums, queries.shape[2]
     )
+    parts = near_ffn_sum(slot, slot_modality, column, ffn_total, grad_block)
     query_grad, key_grad, value_grad = causal_backward(
-        grad_block[None], queries, keys, values, attended_block, probs, probs_b
-    )
-
-    gain_sum = sum_over_dp(after(gain_part, norm_total))
-    gain_grad = jnp.zeros(gains.shape, F32)
-    for k in range(NS):
-        part = gain_sum if k == 0 else send_sect(gain_sum, k)
-        owner = lax.rem(slot_index - k + NS, NS)
-        kind = jnp.sum(jnp.where(jnp.arange(NS) == owner, slot_modality, 0))
-        gain_grad = gain_grad + jnp.where(jnp.arange(MODALITIES)[:, None] == kind, part, 0.0)
-    gain_grad = gain_grad / gains
+        after(grad_block, parts[0])[None], queries, keys, values, attended_block, probs, probs_b
+    )
+
+    gain_sum = gain_part + swap_core(gain_part)
+    width = hidden.shape[1]
+    gain_sum = gain_sum.reshape(MODALITIES, CAP, 4, -1).transpose(0, 2, 1, 3).reshape(MODALITIES, width)
+    gain_grad = gain_sum / gains
 
     quarter = length // NS
-    ffn_rows = near_sum(far_sum(ffn_pieces), BF).astype(BF)
-    keep = labels[0] == jnp.sum(jnp.where(jnp.arange(NS) == slot_index, slot_modality, 0))
-    before = jnp.arange(length)[:, None] >= jnp.arange(length)[None, :]
-    rank_of = jnp.sum(jnp.where(before, keep[None, :], False).astype(jnp.int32), axis=1) - 1
-    spreader = ((rank_of[:, None] == jnp.arange(CAP)[None, :]) & keep[:, None]).astype(BF)
-    spread = jnp.dot(spreader, ffn_rows, preferred_element_type=F32).astype(BF)
-
-    def own_quarter(array, shift=0):
-        return lax.dynamic_slice_in_dim(array, lax.rem(slot_index + shift, NS) * quarter, quarter, 0)
-
-    total = own_quarter(spread).astype(F32)
+    total = parts[0].astype(F32)
     for k in (1, 2, 3):
-        total = total + send_sect(own_quarter(spread, k), k).astype(F32)
-    output = (own_quarter(hidden).astype(F32) + total).astype(BF)[None]
+        total = total + send_sect(parts[k], k).astype(F32)
+    hidden_q = lax.dynamic_slice_in_dim(hidden, slot_index * quarter, quarter, 0)
+    output = (hidden_q.astype(F32) + total).astype(BF)[None]
     return (
         output,
         residual_grad[None],

time: 168 us -> 149 us (0.89)
  waiting for transfers between devices: 39.4 us -> 26.5 us
  starting transfers between devices: 61.7 us -> 55.1 us
  Pallas kernels: 43.5 us -> 49.5 us
  other arithmetic: 7.77 us -> 1.9 us
    ppermute x51 -> x44, waiting for transfers between devices: 39.4 us -> 26.5 us  [send(): return lax.ppermute(block, AXES, pairs)]
    ppermute x51 -> x44, starting transfers between devices: 61.7 us -> 55.1 us  [send(): return lax.ppermute(block, AXES, pairs)]
    pallas_call x5 -> x11, Pallas kernels: 34 us -> 39.8 us  [the longest x2 13.1 us: own_product(): pl.pallas_call(functools.partial(_own_kernel, len(rows)), in_specs=[HELD,...]
    eq x2 -> x0, other arithmetic: 2.47 us -> none  [on_device(): jnp.arange(MODALITIES)[:, None] == kind]
    unnamed x84 -> x115, local copies, waits for them, and re-layouts: 10.5 us -> 9.7 us
  transfers between devices with their start and end apart: 51 -> 44, of which waited for: 17 -> 18; matrix products, arithmetic and copies ran while one was open for 5% -> 6% of each run, Pallas kernels for 18% -> 27%
where the time goes in v3:
time: 149 us
  starting transfers between devices  55.1 us (37%)
  Pallas kernels  49.5 us (33%)
  waiting for transfers between devices  26.5 us (18%)
  local copies, waits for them, and re-layouts  11.8 us (8%)
  matrix products  2.51 us (2%)
  other arithmetic  1.9 us (1%)
    ppermute x44, starting transfers between devices, send(): return lax.ppermute(block, AXES, pairs)  55.1 us
    ppermute x44, waiting for transfers between devices, send(): return lax.ppermute(block, AXES, pairs)  26.5 us
    pallas_call x2, Pallas kernels, own_product(): pl.pallas_call(functools.partial(_own_kernel, len(rows)), in_specs=[HELD,...  13.1 us
    unnamed x115, local copies, waits for them, and re-layouts  9.7 us
    pallas_call x1, Pallas kernels, pre_product(): pl.pallas_call(_pre_kernel, in_specs=[RAW] * 8 + [HELD, HELD], out_specs=...  8.62 us
    pallas_call x2, Pallas kernels, weight_grad(): pl.pallas_call(_down_kernel, grid=(width // tile,), in_specs=[pl.BlockSpe...  7.53 us
    pallas_call x2, Pallas kernels, load_weight(): pl.pallas_call(_load_kernel, in_specs=[RAW], out_specs=HELD, out_shape=pl...  7.25 us
    pallas_call x1, Pallas kernels, back_product(): pl.pallas_call(_back_kernel, grid=(width // tile,), in_specs=[pl.BlockSpe...  5.85 us
  transfers between devices with their start and end apart: 44, of which 18 were waited for; matrix products, arithmetic and copies ran while one was open for 6% of the time, Pallas kernels for 27%

profile of v3, /device:TPU:0, one launch (start us, length us, event | category | flops | bytes accessed | tf_op | source)
XLA Modules:
  0.0 148.8 jit_solution(2098901089902271153)
XLA Ops:
  3.7 1.6 %collective-permute-start = (bf16[8,8192]{1,0:T(8,128)(2,1)S(1)}, bf16[8,8192]{1,0:T(8,128)(2,1)S(1)}, u32[]{:S(2)}, u32[]{:S(2)}) collective-permute-start(bf16[8,8192]{1,0:T(8,128)(2,1)S(1)} %shard_map.161), channel_id=1, source_target_pairs={{0,8},{1,9},{2,10},{3,11},{4,36},{5,37},{6,38},{7,39},{8,16},{9,17... | collective-permute-start | bytes 393224 | tf_op jit(solution)/shard_map/ppermute | solution.py:84
  5.4 2.7 %collective-permute-start.1 = (bf16[8,8192]{1,0:T(8,128)(2,1)S(1)}, bf16[8,8192]{1,0:T(8,128)(2,1)S(1)}, u32[]{:S(2)}, u32[]{:S(2)}) collective-permute-start(bf16[8,8192]{1,0:T(8,128)(2,1)S(1)} %shard_map.161), channel_id=1, source_target_pairs={{0,16},{1,17},{2,18},{3,19},{4,68},{5,69},{6,70},{7,71},{8,24},{9,... | collective-permute-start | bytes 393224 | tf_op jit(solution)/shard_map/ppermute | solution.py:84
  8.1 1.4 collective-permute-start.2
  13.1 2.0 %collective-permute-start.6 = (bf16[32,8192]{1,0:T(8,128)(2,1)S(1)}, bf16[32,8192]{1,0:T(8,128)(2,1)S(1)}, u32[]{:S(2)}, u32[]{:S(2)}) collective-permute-start(bf16[32,8192]{1,0:T(8,128)(2,1)S(1)} %pad_maximum_fusion.refs_0_), channel_id=1, source_target_pairs={{0,32},{1,33},{2,34},{3,35},{4,12},{5,13},{6,14},{7,15},{8,40},{9,... | collective-permute-start | bytes 1572872 | tf_op jit(solution)/shard_map/ppermute | solution.py:84
  15.1 3.6 %collective-permute-start.7 = (bf16[32,8192]{1,0:T(8,128)(2,1)S(1)}, bf16[32,8192]{1,0:T(8,128)(2,1)S(1)}, u32[]{:S(2)}, u32[]{:S(2)}) collective-permute-start(bf16[32,8192]{1,0:T(8,128)(2,1)S(1)} %pad_maximum_fusion.refs_0_), channel_id=1, source_target_pairs={{0,64},{1,65},{2,66},{3,67},{4,20},{5,21},{6,22},{7,23},{8,72},{9,... | collective-permute-start | bytes 1572872 | tf_op jit(solution)/shard_map/ppermute | solution.py:84
  18.7 1.0 collective-permute-start.8
  20.7 1.6 %collective-permute-start.3 = (bf16[16,2048]{1,0:T(8,128)(2,1)S(1)}, bf16[16,2048]{1,0:T(8,128)(2,1)S(1)}, u32[]{:S(2)}, u32[]{:S(2)}) collective-permute-start(bf16[16,2048]{1,0:T(8,128)(2,1)S(1)} %bitcast.78), channel_id=1, source_target_pairs={{0,1},{1,2},{2,3},{3,0},{4,5},{5,6},{6,7},{7,4},{8,9},{9,10},{10,1... | collective-permute-start | bytes 196616 | tf_op jit(solution)/shard_map/ppermute | solution.py:84
  22.3 2.9 %collective-permute-start.4 = (bf16[16,2048]{1,0:T(8,128)(2,1)S(1)}, bf16[16,2048]{1,0:T(8,128)(2,1)S(1)}, u32[]{:S(2)}, u32[]{:S(2)}) collective-permute-start(bf16[16,2048]{1,0:T(8,128)(2,1)S(1)} %bitcast.79), channel_id=1, source_target_pairs={{0,2},{1,3},{2,0},{3,1},{4,6},{5,7},{6,4},{7,5},{8,10},{9,11},{10,... | collective-permute-start | bytes 196616 | tf_op jit(solution)/shard_map/ppermute | solution.py:84
  25.2 1.0 collective-permute-done.3.refs_1_
  26.2 1.8 %collective-permute-start.5 = (bf16[16,2048]{1,0:T(8,128)(2,1)S(1)}, bf16[16,2048]{1,0:T(8,128)(2,1)S(1)}, u32[]{:S(2)}, u32[]{:S(2)}) collective-permute-start(bf16[16,2048]{1,0:T(8,128)(2,1)S(1)} %bitcast.80), channel_id=1, source_target_pairs={{0,3},{1,0},{2,1},{3,2},{4,7},{5,4},{6,5},{7,6},{8,11},{9,8},{10,9... | collective-permute-start | bytes 196616 | tf_op jit(solution)/shard_map/ppermute | solution.py:84
  28.8 1.6 %collective-permute-done.5.refs_3_ = bf16[16,2048]{1,0:T(8,128)(2,1)S(1)} collective-permute-done((bf16[16,2048]{1,0:T(8,128)(2,1)S(1)}, bf16[16,2048]{1,0:T(8,128)(2,1)S(1)}, u32[]{:S(2)}, u32[]{:S(2)}) %collective-permute-start.5) | collective-permute-done | bytes 65568 | tf_op jit(solution)/shard_map/ppermute | solution.py:84
  33.6 1.0 shard_map.162
  34.7 1.3 collective-permute-start.9
  36.0 2.9 %collective-permute-start.10 = (bf16[8,8192]{1,0:T(8,128)(2,1)S(1)}, bf16[8,8192]{1,0:T(8,128)(2,1)S(1)}, u32[]{:S(2)}, u32[]{:S(2)}) collective-permute-start(bf16[8,8192]{1,0:T(8,128)(2,1)S(1)} %get-tuple-element.56), channel_id=1, source_target_pairs={{0,16},{1,17},{2,18},{3,19},{4,68},{5,69},{6,70},{7,71},{8,24},{9,... | collective-permute-start | bytes 393224 | tf_op jit(solution)/shard_map/ppermute | solution.py:84
  39.8 1.1 collective-permute-done.9
  40.9 2.2 %collective-permute-done.10 = bf16[8,8192]{1,0:T(8,128)(2,1)S(1)} collective-permute-done((bf16[8,8192]{1,0:T(8,128)(2,1)S(1)}, bf16[8,8192]{1,0:T(8,128)(2,1)S(1)}, u32[]{:S(2)}, u32[]{:S(2)}) %collective-permute-start.10) | collective-permute-done | bytes 131104 | tf_op jit(solution)/shard_map/ppermute | solution.py:84
  44.0 2.0 %collective-permute-start.12 = (bf16[32,8192]{1,0:T(8,128)(2,1)S(1)}, bf16[32,8192]{1,0:T(8,128)(2,1)S(1)}, u32[]{:S(2)}, u32[]{:S(2)}) collective-permute-start(bf16[32,8192]{1,0:T(8,128)(2,1)S(1)} %constant_dynamic-update-slice_fusion.refs_0_), channel_id=1, source_target_pairs={{0,32},{1,33},{2,34},{3,35},{4,12},{5,13},{6,14},{7,15},{8,40},{9,... | collective-permute-start | bytes 1572872 | tf_op jit(solution)/shard_map/ppermute | solution.py:84
  46.0 1.2 collective-permute-start.13
  47.2 2.6 %shard_map.164.refs_8_.w_ref = bf16[344,8192]{1,0:T(8,128)(2,1)S(1)} custom-call(bf16[1,344,8192]{2,1,0:T(8,128)(2,1)} %w_hbm.2), custom_call_target="tpu_custom_call" | custom-call | flops 1000 | bytes 1000 | tf_op jit(solution)/shard_map/pallas_call | solution.py:262
  49.8 4.6 %shard_map.165.w_ref = bf16[344,8192]{1,0:T(8,128)(2,1)S(1)} custom-call(bf16[1,344,8192]{2,1,0:T(8,128)(2,1)} %w_hbm.3), custom_call_target="tpu_custom_call" | custom-call | flops 1000 | bytes 1000 | tf_op jit(solution)/shard_map/pallas_call | solution.py:262
  54.8 5.8 %shard_map.163.refs_9_ = f32[344,256]{1,0:T(8,128)S(1)} custom-call(bf16[32,8192]{1,0:T(8,128)(2,1)S(1)} %pad_maximum_fusion.refs_0_, bf16[32,8192]{1,0:T(8,128)(2,1)S(1)} %collective-permute-done.6.refs_1_, bf16[32,8192]{1,0:T(8,128)(2,1)S(1)} %collective-permute-done.7.refs_2_, bf16[32,8192]{1,0:T(8,128)(2,1)S(1)} %collective-permute-done.8.refs_3_, ...), custom_call_target="tpu_custom_call" | custom-call | flops 1000 | bytes 1000 | tf_op jit(solution)/shard_map/pallas_call | solution.py:290
  61.3 1.3 collective-permute-done.22.refs_7_
  64.1 8.6 %shard_map.166 = (bf16[344,256]{1,0:T(8,128)(2,1)S(1)}, bf16[344,256]{1,0:T(8,128)(2,1)S(1)}, bf16[256,344]{1,0:T(8,128)(2,1)S(1)}, bf16[256,344]{1,0:T(8,128)(2,1)S(1)}, bf16[128,8192]{1,0:T(8,128)(2,1)}) custom-call(bf16[32,8192]{1,0:T(8,128)(2,1)S(1)} %constant_dynamic-update-slice_fusion.refs_0_, bf16[32,8192]{1,0:T(8,128)(2,1)S(1)} %collective-permute-done.12.refs_1_, ...), custom_call_target="tpu_custom_call" | custom-call | flops 1000 | bytes 1000 | tf_op jit(solution)/shard_map/pallas_call | solution.py:366
  73.2 2.0 %shard_map.167 = bf16[128,8192]{1,0:T(8,128)(2,1)S(1)} custom-call(bf16[256,344]{1,0:T(8,128)(2,1)S(1)} %get-tuple-element.64.left_ref, bf16[344,8192]{1,0:T(8,128)(2,1)S(1)} %shard_map.165.w_ref), custom_call_target="tpu_custom_call" | custom-call | flops 1000 | bytes 1000 | tf_op jit(solution)/shard_map/pallas_call | solution.py:400
  75.6 1.8 %collective-permute-done.23.in_hbm = bf16[128,8192]{1,0:T(8,128)(2,1)S(1)} collective-permute-done((bf16[128,8192]{1,0:T(8,128)(2,1)}, bf16[128,8192]{1,0:T(8,128)(2,1)S(1)}, u32[]{:S(2)}, u32[]{:S(2)}) %collective-permute-start.23) | collective-permute-done | bytes 2097184 | tf_op jit(solution)/shard_map/ppermute | solution.py:84
  77.4 7.1 %shard_map.168 = (f32[32,8704]{1,0:T(8,128)S(1)}, bf16[32,8704]{1,0:T(8,128)(2,1)S(1)}, bf16[32,8704]{1,0:T(8,128)(2,1)S(1)}, bf16[32,8704]{1,0:T(8,128)(2,1)S(1)}) custom-call(bf16[256,344]{1,0:T(8,128)(2,1)S(1)} %get-tuple-element.62.left_ref, bf16[344,8192]{1,0:T(8,128)(2,1)} %copy-done.1, bf16[128,8192]{1,0:T(8,128)(2,1)S(1)} %collective-permute-done.23.in_hbm, ...), custom_call_target="tpu_custom_call" | custom-call | flops 1000 | bytes 1000 | tf_op jit(solution)/shard_map/pallas_call | solution.py:478
  84.6 2.7 %collective-permute-start.25 = (bf16[32,8704]{1,0:T(8,128)(2,1)S(1)}, bf16[32,8704]{1,0:T(8,128)(2,1)S(1)}, u32[]{:S(2)}, u32[]{:S(2)}) collective-permute-start(bf16[32,8704]{1,0:T(8,128)(2,1)S(1)} %get-tuple-element.66), channel_id=1, source_target_pairs={{0,96},{1,97},{2,98},{3,99},{4,28},{5,29},{6,30},{7,31},{8,104},{9... | collective-permute-start | bytes 1671176 | tf_op jit(solution)/shard_map/ppermute | solution.py:84
  89.5 6.1 %shard_map.169 = (f32[32,8192]{1,0:T(8,128)S(1)}, bf16[32,8192]{1,0:T(8,128)(2,1)}, bf16[32,8192]{1,0:T(8,128)(2,1)}, bf16[32,8192]{1,0:T(8,128)(2,1)S(1)}) custom-call(bf16[256,344]{1,0:T(8,128)(2,1)S(1)} %copy-done.27, bf16[344,8192]{1,0:T(8,128)(2,1)} %copy-done, bf16[128,8192]{1,0:T(8,128)(2,1)S(1)} %collective-permute-done.24.in_hbm), custom_call_target="tpu_custom_call" | custom-call | flops 1000 | bytes 1000 | tf_op jit(solution)/shard_map/pallas_call | solution.py:478
  95.5 2.6 %collective-permute-start.29 = (bf16[32,8192]{1,0:T(8,128)(2,1)}, bf16[32,8192]{1,0:T(8,128)(2,1)S(1)}, u32[]{:S(2)}, u32[]{:S(2)}) collective-permute-start(bf16[32,8192]{1,0:T(8,128)(2,1)} %get-tuple-element.76), channel_id=1, source_target_pairs={{0,96},{1,97},{2,98},{3,99},{4,28},{5,29},{6,30},{7,31},{8,104},{9... | collective-permute-start | bytes 1572872 | tf_op jit(solution)/shard_map/ppermute | solution.py:84
  98.1 1.8 %collective-permute-start.30 = (bf16[32,8192]{1,0:T(8,128)(2,1)}, bf16[32,8192]{1,0:T(8,128)(2,1)S(1)}, u32[]{:S(2)}, u32[]{:S(2)}) collective-permute-start(bf16[32,8192]{1,0:T(8,128)(2,1)} %get-tuple-element.77), channel_id=1, source_target_pairs={{0,64},{1,65},{2,66},{3,67},{4,20},{5,21},{6,22},{7,23},{8,72},{9,... | collective-permute-start | bytes 1572872 | tf_op jit(solution)/shard_map/ppermute | solution.py:84
  100.5 3.8 %shard_map.170 = bf16[1,344,8192]{2,1,0:T(8,128)(2,1)} custom-call(bf16[32,8192]{1,0:T(8,128)(2,1)S(1)} %pad_maximum_fusion.refs_0_, bf16[32,8192]{1,0:T(8,128)(2,1)S(1)} %collective-permute-done.6.refs_1_, bf16[32,8192]{1,0:T(8,128)(2,1)S(1)} %copy-done.3, bf16[32,8192]{1,0:T(8,128)(2,1)S(1)} %copy-done.5, bf16[32,8192]{1,0:T(8,128)(2,1)S(1)} %copy-done.7, ...), custom_call_target="tpu_custom_call" | custom-call | flops 1442840576 | bytes 9830400 | tf_op jit(solution)/shard_map/pallas_call | solution.py:605
  104.5 2.1 %collective-permute-start.28 = (f32[8,9216]{1,0:T(8,128)S(1)}, f32[8,9216]{1,0:T(8,128)S(1)}, u32[]{:S(2)}, u32[]{:S(2)}) collective-permute-start(f32[8,9216]{1,0:T(8,128)S(1)} %get-tuple-element.73), channel_id=1, source_target_pairs={{0,24},{1,25},{2,26},{3,27},{4,100},{5,101},{6,102},{7,103},{8,0},... | collective-permute-start | bytes 884744 | tf_op jit(solution)/shard_map/ppermute | solution.py:84
  106.6 1.1 collective-permute-start.32
  107.8 1.1 collective-permute-start.33
  108.9 3.8 %shard_map.172 = bf16[1,344,8192]{2,1,0:T(8,128)(2,1)} custom-call(bf16[32,8192]{1,0:T(8,128)(2,1)S(1)} %constant_dynamic-update-slice_fusion.refs_0_, bf16[32,8192]{1,0:T(8,128)(2,1)S(1)} %collective-permute-done.12.refs_1_, bf16[32,8192]{1,0:T(8,128)(2,1)S(1)} %collective-permute-done.13.refs_2_, bf16[32,8192]{1,0:T(8,128)(2,1)S(1)} %collective-permute-done.14.refs_3_, ...), custom_call_target="tpu_custom_call" | custom-call | flops 1442840576 | bytes 9830400 | tf_op jit(solution)/shard_map/pallas_call | solution.py:605
  112.8 9.1 %collective-permute-done.31 = bf16[32,8192]{1,0:T(8,128)(2,1)S(1)} collective-permute-done((bf16[32,8192]{1,0:T(8,128)(2,1)S(1)}, bf16[32,8192]{1,0:T(8,128)(2,1)S(1)}, u32[]{:S(2)}, u32[]{:S(2)}) %collective-permute-start.31) | collective-permute-done | bytes 524320 | tf_op jit(solution)/shard_map/ppermute | solution.py:84
  122.4 4.1 %collective-permute-start.36 = (bf16[8,10240]{1,0:T(8,128)(2,1)S(1)}, bf16[8,10240]{1,0:T(8,128)(2,1)S(1)}, u32[]{:S(2)}, u32[]{:S(2)}) collective-permute-start(bf16[8,10240]{1,0:T(8,128)(2,1)S(1)} %shard_map.173.refs_0_), channel_id=1, source_target_pairs={{0,2},{1,3},{2,0},{3,1},{4,6},{5,7},{6,4},{7,5},{8,10},{9,11},{10,... | collective-permute-start | bytes 491528 | tf_op jit(solution)/shard_map/ppermute | solution.py:84
  126.9 1.4 collective-permute-start.34
  128.3 1.8 %collective-permute-start.38 = (bf16[8,8192]{1,0:T(8,128)(2,1)S(1)}, bf16[8,8192]{1,0:T(8,128)(2,1)S(1)}, u32[]{:S(2)}, u32[]{:S(2)}) collective-permute-start(bf16[8,8192]{1,0:T(8,128)(2,1)S(1)} %get-tuple-element.95), channel_id=1, source_target_pairs={{0,16},{1,17},{2,18},{3,19},{4,68},{5,69},{6,70},{7,71},{8,24},{9,... | collective-permute-start | bytes 393224 | tf_op jit(solution)/shard_map/ppermute | solution.py:84
  130.1 1.0 collective-permute-start.39
  131.2 1.9 %collective-permute-done.36.refs_2_ = bf16[8,10240]{1,0:T(8,128)(2,1)S(1)} collective-permute-done((bf16[8,10240]{1,0:T(8,128)(2,1)S(1)}, bf16[8,10240]{1,0:T(8,128)(2,1)S(1)}, u32[]{:S(2)}, u32[]{:S(2)}) %collective-permute-start.36) | collective-permute-done | bytes 163872 | tf_op jit(solution)/shard_map/ppermute | solution.py:84
  133.1 2.0 %shard_map.174 = (bf16[4,8192]{1,0:T(4,128)(2,1)}, bf16[16,2048]{1,0:T(8,128)(2,1)S(1)}, f32[24,1024]{1,0:T(8,128)S(1)}) custom-call(s32[1]{0:T(128)} %bitcast.2.slot_ref, s32[4]{0:T(128)S(1)} %copy-done.39, s32[16,1]{1,0:T(8,128)S(1)} %copy-done.36, bf16[16,8192]{1,0:T(8,128)(2,1)S(1)} %copy-done.29, bf16[16,8192]{1,0:T(8,128)(2,1)S(1)} %bitcast.77, ...), custom_call_target="tpu_custom_call" | custom-call | flops 1000 | bytes 1000 | tf_op jit(solution)/shard_map/pallas_call | solution.py:240
  135.1 1.2 collective-permute-done.39.refs_3_
  136.3 1.1 shard_map.175
  139.5 2.0 %collective-permute-start.40 = (bf16[4,8192]{1,0:T(4,128)(2,1)S(1)}, bf16[4,8192]{1,0:T(4,128)(2,1)S(1)}, u32[]{:S(2)}, u32[]{:S(2)}) collective-permute-start(bf16[4,8192]{1,0:T(4,128)(2,1)S(1)} %get-tuple-element.86), channel_id=1, source_target_pairs={{0,1},{1,2},{2,3},{3,0},{4,5},{5,6},{6,7},{7,4},{8,9},{9,10},{10,1... | collective-permute-start | bytes 196616 | tf_op jit(solution)/shard_map/ppermute | solution.py:84
  141.5 1.3 collective-permute-start.41
  142.7 1.5 %collective-permute-start.42 = (bf16[4,8192]{1,0:T(4,128)(2,1)S(1)}, bf16[4,8192]{1,0:T(4,128)(2,1)S(1)}, u32[]{:S(2)}, u32[]{:S(2)}) collective-permute-start(bf16[4,8192]{1,0:T(4,128)(2,1)S(1)} %get-tuple-element.88), channel_id=1, source_target_pairs={{0,3},{1,0},{2,1},{3,2},{4,7},{5,4},{6,5},{7,6},{8,11},{9,8},{10,9... | collective-permute-start | bytes 196616 | tf_op jit(solution)/shard_map/ppermute | solution.py:84
  145.7 1.5 %collective-permute-done.41 = bf16[4,8192]{1,0:T(4,128)(2,1)S(1)} collective-permute-done((bf16[4,8192]{1,0:T(4,128)(2,1)S(1)}, bf16[4,8192]{1,0:T(4,128)(2,1)S(1)}, u32[]{:S(2)}, u32[]{:S(2)}) %collective-permute-start.41) | collective-permute-done | bytes 65568 | tf_op jit(solution)/shard_map/ppermute | solution.py:84
  (191 shorter events, 25.6 us)
Async XLA Ops:
  3.7 8.5 %collective-permute-start = (bf16[8,8192]{1,0:T(8,128)(2,1)S(1)}, bf16[8,8192]{1,0:T(8,128)(2,1)S(1)}, u32[]{:S(2)}, u32[]{:S(2)}) collective-permute-start(bf16[8,8192]{1,0:T(8,128)(2,1)S(1)} %shard_map.161), channel_id=1, source_target_pairs={{0,8},{1,9},{2,10},{3,11},{4,36},{5,37},{6,38},{7,39},{8,16},{9,17... | collective-permute-start | bytes 393224 | tf_op jit(solution)/shard_map/ppermute | solution.py:84
  5.4 7.1 %collective-permute-start.1 = (bf16[8,8192]{1,0:T(8,128)(2,1)S(1)}, bf16[8,8192]{1,0:T(8,128)(2,1)S(1)}, u32[]{:S(2)}, u32[]{:S(2)}) collective-permute-start(bf16[8,8192]{1,0:T(8,128)(2,1)S(1)} %shard_map.161), channel_id=1, source_target_pairs={{0,16},{1,17},{2,18},{3,19},{4,68},{5,69},{6,70},{7,71},{8,24},{9,... | collective-permute-start | bytes 393224 | tf_op jit(solution)/shard_map/ppermute | solution.py:84
  8.1 5.0 %collective-permute-start.2 = (bf16[8,8192]{1,0:T(8,128)(2,1)S(1)}, bf16[8,8192]{1,0:T(8,128)(2,1)S(1)}, u32[]{:S(2)}, u32[]{:S(2)}) collective-permute-start(bf16[8,8192]{1,0:T(8,128)(2,1)S(1)} %shard_map.161), channel_id=1, source_target_pairs={{0,24},{1,25},{2,26},{3,27},{4,100},{5,101},{6,102},{7,103},{8,0},... | collective-permute-start | bytes 393224 | tf_op jit(solution)/shard_map/ppermute | solution.py:84
  13.1 21.5 %collective-permute-start.6 = (bf16[32,8192]{1,0:T(8,128)(2,1)S(1)}, bf16[32,8192]{1,0:T(8,128)(2,1)S(1)}, u32[]{:S(2)}, u32[]{:S(2)}) collective-permute-start(bf16[32,8192]{1,0:T(8,128)(2,1)S(1)} %pad_maximum_fusion.refs_0_), channel_id=1, source_target_pairs={{0,32},{1,33},{2,34},{3,35},{4,12},{5,13},{6,14},{7,15},{8,40},{9,... | collective-permute-start | bytes 1572872 | tf_op jit(solution)/shard_map/ppermute | solution.py:84
  15.1 19.5 %collective-permute-start.7 = (bf16[32,8192]{1,0:T(8,128)(2,1)S(1)}, bf16[32,8192]{1,0:T(8,128)(2,1)S(1)}, u32[]{:S(2)}, u32[]{:S(2)}) collective-permute-start(bf16[32,8192]{1,0:T(8,128)(2,1)S(1)} %pad_maximum_fusion.refs_0_), channel_id=1, source_target_pairs={{0,64},{1,65},{2,66},{3,67},{4,20},{5,21},{6,22},{7,23},{8,72},{9,... | collective-permute-start | bytes 1572872 | tf_op jit(solution)/shard_map/ppermute | solution.py:84
  18.7 15.9 %collective-permute-start.8 = (bf16[32,8192]{1,0:T(8,128)(2,1)S(1)}, bf16[32,8192]{1,0:T(8,128)(2,1)S(1)}, u32[]{:S(2)}, u32[]{:S(2)}) collective-permute-start(bf16[32,8192]{1,0:T(8,128)(2,1)S(1)} %pad_maximum_fusion.refs_0_), channel_id=1, source_target_pairs={{0,96},{1,97},{2,98},{3,99},{4,28},{5,29},{6,30},{7,31},{8,104},{9... | collective-permute-start | bytes 1572872 | tf_op jit(solution)/shard_map/ppermute | solution.py:84
  20.7 5.5 %collective-permute-start.3 = (bf16[16,2048]{1,0:T(8,128)(2,1)S(1)}, bf16[16,2048]{1,0:T(8,128)(2,1)S(1)}, u32[]{:S(2)}, u32[]{:S(2)}) collective-permute-start(bf16[16,2048]{1,0:T(8,128)(2,1)S(1)} %bitcast.78), channel_id=1, source_target_pairs={{0,1},{1,2},{2,3},{3,0},{4,5},{5,6},{6,7},{7,4},{8,9},{9,10},{10,1... | collective-permute-start | bytes 196616 | tf_op jit(solution)/shard_map/ppermute | solution.py:84
  22.3 6.4 %collective-permute-start.4 = (bf16[16,2048]{1,0:T(8,128)(2,1)S(1)}, bf16[16,2048]{1,0:T(8,128)(2,1)S(1)}, u32[]{:S(2)}, u32[]{:S(2)}) collective-permute-start(bf16[16,2048]{1,0:T(8,128)(2,1)S(1)} %bitcast.79), channel_id=1, source_target_pairs={{0,2},{1,3},{2,0},{3,1},{4,6},{5,7},{6,4},{7,5},{8,10},{9,11},{10,... | collective-permute-start | bytes 196616 | tf_op jit(solution)/shard_map/ppermute | solution.py:84
  26.2 4.3 %collective-permute-start.5 = (bf16[16,2048]{1,0:T(8,128)(2,1)S(1)}, bf16[16,2048]{1,0:T(8,128)(2,1)S(1)}, u32[]{:S(2)}, u32[]{:S(2)}) collective-permute-start(bf16[16,2048]{1,0:T(8,128)(2,1)S(1)} %bitcast.80), channel_id=1, source_target_pairs={{0,3},{1,0},{2,1},{3,2},{4,7},{5,4},{6,5},{7,6},{8,11},{9,8},{10,9... | collective-permute-start | bytes 196616 | tf_op jit(solution)/shard_map/ppermute | solution.py:84
  28.7 15.3 %collective-permute-start.15 = (bf16[32,8192]{1,0:T(8,128)(2,1)S(1)}, bf16[32,8192]{1,0:T(8,128)(2,1)S(1)}, u32[]{:S(2)}, u32[]{:S(2)}) collective-permute-start(bf16[32,8192]{1,0:T(8,128)(2,1)S(1)} %pad_maximum_fusion.refs_0_), channel_id=1, source_target_pairs={{0,4},{1,5},{2,6},{3,7},{4,0},{5,1},{6,2},{7,3},{8,12},{9,13},{10,... | collective-permute-start | bytes 1572872 | tf_op jit(solution)/shard_map/ppermute | solution.py:84
  34.7 6.2 %collective-permute-start.9 = (bf16[8,8192]{1,0:T(8,128)(2,1)S(1)}, bf16[8,8192]{1,0:T(8,128)(2,1)S(1)}, u32[]{:S(2)}, u32[]{:S(2)}) collective-permute-start(bf16[8,8192]{1,0:T(8,128)(2,1)S(1)} %get-tuple-element.56), channel_id=1, source_target_pairs={{0,8},{1,9},{2,10},{3,11},{4,36},{5,37},{6,38},{7,39},{8,16},{9,17... | collective-permute-start | bytes 393224 | tf_op jit(solution)/shard_map/ppermute | solution.py:84
  36.0 7.2 %collective-permute-start.10 = (bf16[8,8192]{1,0:T(8,128)(2,1)S(1)}, bf16[8,8192]{1,0:T(8,128)(2,1)S(1)}, u32[]{:S(2)}, u32[]{:S(2)}) collective-permute-start(bf16[8,8192]{1,0:T(8,128)(2,1)S(1)} %get-tuple-element.56), channel_id=1, source_target_pairs={{0,16},{1,17},{2,18},{3,19},{4,68},{5,69},{6,70},{7,71},{8,24},{9,... | collective-permute-start | bytes 393224 | tf_op jit(solution)/shard_map/ppermute | solution.py:84
  38.9 5.0 %collective-permute-start.11 = (bf16[8,8192]{1,0:T(8,128)(2,1)S(1)}, bf16[8,8192]{1,0:T(8,128)(2,1)S(1)}, u32[]{:S(2)}, u32[]{:S(2)}) collective-permute-start(bf16[8,8192]{1,0:T(8,128)(2,1)S(1)} %get-tuple-element.56), channel_id=1, source_target_pairs={{0,24},{1,25},{2,26},{3,27},{4,100},{5,101},{6,102},{7,103},{8,0},... | collective-permute-start | bytes 393224 | tf_op jit(solution)/shard_map/ppermute | solution.py:84
  39.8 6.2 %collective-permute-start.16 = (bf16[32,8192]{1,0:T(8,128)(2,1)S(1)}, bf16[32,8192]{1,0:T(8,128)(2,1)S(1)}, u32[]{:S(2)}, u32[]{:S(2)}) collective-permute-start(bf16[32,8192]{1,0:T(8,128)(2,1)S(1)} %collective-permute-done.6.refs_1_), channel_id=1, source_target_pairs={{0,4},{1,5},{2,6},{3,7},{4,0},{5,1},{6,2},{7,3},{8,12},{9,13},{10,... | collective-permute-start | bytes 1572872 | tf_op jit(solution)/shard_map/ppermute | solution.py:84
  40.9 13.6 %collective-permute-start.17 = (bf16[32,8192]{1,0:T(8,128)(2,1)S(1)}, bf16[32,8192]{1,0:T(8,128)(2,1)S(1)}, u32[]{:S(2)}, u32[]{:S(2)}) collective-permute-start(bf16[32,8192]{1,0:T(8,128)(2,1)S(1)} %collective-permute-done.7.refs_2_), channel_id=1, source_target_pairs={{0,4},{1,5},{2,6},{3,7},{4,0},{5,1},{6,2},{7,3},{8,12},{9,13},{10,... | collective-permute-start | bytes 1572872 | tf_op jit(solution)/shard_map/ppermute | solution.py:84
  43.2 11.5 %collective-permute-start.18 = (bf16[32,8192]{1,0:T(8,128)(2,1)S(1)}, bf16[32,8192]{1,0:T(8,128)(2,1)S(1)}, u32[]{:S(2)}, u32[]{:S(2)}) collective-permute-start(bf16[32,8192]{1,0:T(8,128)(2,1)S(1)} %collective-permute-done.8.refs_3_), channel_id=1, source_target_pairs={{0,4},{1,5},{2,6},{3,7},{4,0},{5,1},{6,2},{7,3},{8,12},{9,13},{10,... | collective-permute-start | bytes 1572872 | tf_op jit(solution)/shard_map/ppermute | solution.py:84
  43.9 16.7 %collective-permute-start.14 = (bf16[32,8192]{1,0:T(8,128)(2,1)S(1)}, bf16[32,8192]{1,0:T(8,128)(2,1)S(1)}, u32[]{:S(2)}, u32[]{:S(2)}) collective-permute-start(bf16[32,8192]{1,0:T(8,128)(2,1)S(1)} %constant_dynamic-update-slice_fusion.refs_0_), channel_id=1, source_target_pairs={{0,96},{1,97},{2,98},{3,99},{4,28},{5,29},{6,30},{7,31},{8,104},{9... | collective-permute-start | bytes 1572872 | tf_op jit(solution)/shard_map/ppermute | solution.py:84
  44.0 16.8 %collective-permute-start.12 = (bf16[32,8192]{1,0:T(8,128)(2,1)S(1)}, bf16[32,8192]{1,0:T(8,128)(2,1)S(1)}, u32[]{:S(2)}, u32[]{:S(2)}) collective-permute-start(bf16[32,8192]{1,0:T(8,128)(2,1)S(1)} %constant_dynamic-update-slice_fusion.refs_0_), channel_id=1, source_target_pairs={{0,32},{1,33},{2,34},{3,35},{4,12},{5,13},{6,14},{7,15},{8,40},{9,... | collective-permute-start | bytes 1572872 | tf_op jit(solution)/shard_map/ppermute | solution.py:84
  46.0 15.2 %collective-permute-start.13 = (bf16[32,8192]{1,0:T(8,128)(2,1)S(1)}, bf16[32,8192]{1,0:T(8,128)(2,1)S(1)}, u32[]{:S(2)}, u32[]{:S(2)}) collective-permute-start(bf16[32,8192]{1,0:T(8,128)(2,1)S(1)} %constant_dynamic-update-slice_fusion.refs_0_), channel_id=1, source_target_pairs={{0,64},{1,65},{2,66},{3,67},{4,20},{5,21},{6,22},{7,23},{8,72},{9,... | collective-permute-start | bytes 1572872 | tf_op jit(solution)/shard_map/ppermute | solution.py:84
  54.5 6.8 %collective-permute-start.19 = (bf16[32,8192]{1,0:T(8,128)(2,1)S(1)}, bf16[32,8192]{1,0:T(8,128)(2,1)S(1)}, u32[]{:S(2)}, u32[]{:S(2)}) collective-permute-start(bf16[32,8192]{1,0:T(8,128)(2,1)S(1)} %constant_dynamic-update-slice_fusion.refs_0_), channel_id=1, source_target_pairs={{0,4},{1,5},{2,6},{3,7},{4,0},{5,1},{6,2},{7,3},{8,12},{9,13},{10,... | collective-permute-start | bytes 1572872 | tf_op jit(solution)/shard_map/ppermute | solution.py:84
  60.6 2.0 %collective-permute-start.22 = (bf16[32,8192]{1,0:T(8,128)(2,1)S(1)}, bf16[32,8192]{1,0:T(8,128)(2,1)S(1)}, u32[]{:S(2)}, u32[]{:S(2)}) collective-permute-start(bf16[32,8192]{1,0:T(8,128)(2,1)S(1)} %collective-permute-done.14.refs_3_), channel_id=1, source_target_pairs={{0,4},{1,5},{2,6},{3,7},{4,0},{5,1},{6,2},{7,3},{8,12},{9,13},{10,... | collective-permute-start | bytes 1572872 | tf_op jit(solution)/shard_map/ppermute | solution.py:84
  60.8 2.6 %collective-permute-start.20 = (bf16[32,8192]{1,0:T(8,128)(2,1)S(1)}, bf16[32,8192]{1,0:T(8,128)(2,1)S(1)}, u32[]{:S(2)}, u32[]{:S(2)}) collective-permute-start(bf16[32,8192]{1,0:T(8,128)(2,1)S(1)} %collective-permute-done.12.refs_1_), channel_id=1, source_target_pairs={{0,4},{1,5},{2,6},{3,7},{4,0},{5,1},{6,2},{7,3},{8,12},{9,13},{10,... | collective-permute-start | bytes 1572872 | tf_op jit(solution)/shard_map/ppermute | solution.py:84
  61.2 2.9 %collective-permute-start.21 = (bf16[32,8192]{1,0:T(8,128)(2,1)S(1)}, bf16[32,8192]{1,0:T(8,128)(2,1)S(1)}, u32[]{:S(2)}, u32[]{:S(2)}) collective-permute-start(bf16[32,8192]{1,0:T(8,128)(2,1)S(1)} %collective-permute-done.13.refs_2_), channel_id=1, source_target_pairs={{0,4},{1,5},{2,6},{3,7},{4,0},{5,1},{6,2},{7,3},{8,12},{9,13},{10,... | collective-permute-start | bytes 1572872 | tf_op jit(solution)/shard_map/ppermute | solution.py:84
  72.8 4.6 %collective-permute-start.23 = (bf16[128,8192]{1,0:T(8,128)(2,1)}, bf16[128,8192]{1,0:T(8,128)(2,1)S(1)}, u32[]{:S(2)}, u32[]{:S(2)}) collective-permute-start(bf16[128,8192]{1,0:T(8,128)(2,1)} %get-tuple-element.60), channel_id=1, source_target_pairs={{0,4},{1,5},{2,6},{3,7},{4,0},{5,1},{6,2},{7,3},{8,12},{9,13},{10,... | collective-permute-start | bytes 6291464 | tf_op jit(solution)/shard_map/ppermute | solution.py:84
  75.2 13.4 %collective-permute-start.24 = (bf16[128,8192]{1,0:T(8,128)(2,1)S(1)}, bf16[128,8192]{1,0:T(8,128)(2,1)S(1)}, u32[]{:S(2)}, u32[]{:S(2)}) collective-permute-start(bf16[128,8192]{1,0:T(8,128)(2,1)S(1)} %shard_map.167), channel_id=1, source_target_pairs={{0,4},{1,5},{2,6},{3,7},{4,0},{5,1},{6,2},{7,3},{8,12},{9,13},{10,... | collective-permute-start | bytes 6291464 | tf_op jit(solution)/shard_map/ppermute | solution.py:84
  84.6 15.8 %collective-permute-start.25 = (bf16[32,8704]{1,0:T(8,128)(2,1)S(1)}, bf16[32,8704]{1,0:T(8,128)(2,1)S(1)}, u32[]{:S(2)}, u32[]{:S(2)}) collective-permute-start(bf16[32,8704]{1,0:T(8,128)(2,1)S(1)} %get-tuple-element.66), channel_id=1, source_target_pairs={{0,96},{1,97},{2,98},{3,99},{4,28},{5,29},{6,30},{7,31},{8,104},{9... | collective-permute-start | bytes 1671176 | tf_op jit(solution)/shard_map/ppermute | solution.py:84
  87.3 16.9 %collective-permute-start.26 = (bf16[32,8704]{1,0:T(8,128)(2,1)S(1)}, bf16[32,8704]{1,0:T(8,128)(2,1)S(1)}, u32[]{:S(2)}, u32[]{:S(2)}) collective-permute-start(bf16[32,8704]{1,0:T(8,128)(2,1)S(1)} %get-tuple-element.70), channel_id=1, source_target_pairs={{0,64},{1,65},{2,66},{3,67},{4,20},{5,21},{6,22},{7,23},{8,72},{9,... | collective-permute-start | bytes 1671176 | tf_op jit(solution)/shard_map/ppermute | solution.py:84
  87.8 16.5 %collective-permute-start.27 = (bf16[32,8704]{1,0:T(8,128)(2,1)S(1)}, bf16[32,8704]{1,0:T(8,128)(2,1)S(1)}, u32[]{:S(2)}, u32[]{:S(2)}) collective-permute-start(bf16[32,8704]{1,0:T(8,128)(2,1)S(1)} %get-tuple-element.71), channel_id=1, source_target_pairs={{0,32},{1,33},{2,34},{3,35},{4,12},{5,13},{6,14},{7,15},{8,40},{9,... | collective-permute-start | bytes 1671176 | tf_op jit(solution)/shard_map/ppermute | solution.py:84
  95.5 12.3 %collective-permute-start.29 = (bf16[32,8192]{1,0:T(8,128)(2,1)}, bf16[32,8192]{1,0:T(8,128)(2,1)S(1)}, u32[]{:S(2)}, u32[]{:S(2)}) collective-permute-start(bf16[32,8192]{1,0:T(8,128)(2,1)} %get-tuple-element.76), channel_id=1, source_target_pairs={{0,96},{1,97},{2,98},{3,99},{4,28},{5,29},{6,30},{7,31},{8,104},{9... | collective-permute-start | bytes 1572872 | tf_op jit(solution)/shard_map/ppermute | solution.py:84
  98.1 14.7 %collective-permute-start.30 = (bf16[32,8192]{1,0:T(8,128)(2,1)}, bf16[32,8192]{1,0:T(8,128)(2,1)S(1)}, u32[]{:S(2)}, u32[]{:S(2)}) collective-permute-start(bf16[32,8192]{1,0:T(8,128)(2,1)} %get-tuple-element.77), channel_id=1, source_target_pairs={{0,64},{1,65},{2,66},{3,67},{4,20},{5,21},{6,22},{7,23},{8,72},{9,... | collective-permute-start | bytes 1572872 | tf_op jit(solution)/shard_map/ppermute | solution.py:84
  100.4 21.6 %collective-permute-start.31 = (bf16[32,8192]{1,0:T(8,128)(2,1)S(1)}, bf16[32,8192]{1,0:T(8,128)(2,1)S(1)}, u32[]{:S(2)}, u32[]{:S(2)}) collective-permute-start(bf16[32,8192]{1,0:T(8,128)(2,1)S(1)} %get-tuple-element.78), channel_id=1, source_target_pairs={{0,32},{1,33},{2,34},{3,35},{4,12},{5,13},{6,14},{7,15},{8,40},{9,... | collective-permute-start | bytes 1572872 | tf_op jit(solution)/shard_map/ppermute | solution.py:84
  104.5 17.4 %collective-permute-start.28 = (f32[8,9216]{1,0:T(8,128)S(1)}, f32[8,9216]{1,0:T(8,128)S(1)}, u32[]{:S(2)}, u32[]{:S(2)}) collective-permute-start(f32[8,9216]{1,0:T(8,128)S(1)} %get-tuple-element.73), channel_id=1, source_target_pairs={{0,24},{1,25},{2,26},{3,27},{4,100},{5,101},{6,102},{7,103},{8,0},... | collective-permute-start | bytes 884744 | tf_op jit(solution)/shard_map/ppermute | solution.py:84
  106.6 15.3 %collective-permute-start.32 = (f32[8,9216]{1,0:T(8,128)S(1)}, f32[8,9216]{1,0:T(8,128)S(1)}, u32[]{:S(2)}, u32[]{:S(2)}) collective-permute-start(f32[8,9216]{1,0:T(8,128)S(1)} %get-tuple-element.80), channel_id=1, source_target_pairs={{0,16},{1,17},{2,18},{3,19},{4,68},{5,69},{6,70},{7,71},{8,24},{9,... | collective-permute-start | bytes 884744 | tf_op jit(solution)/shard_map/ppermute | solution.py:84
  107.8 14.1 %collective-permute-start.33 = (f32[8,9216]{1,0:T(8,128)S(1)}, f32[8,9216]{1,0:T(8,128)S(1)}, u32[]{:S(2)}, u32[]{:S(2)}) collective-permute-start(f32[8,9216]{1,0:T(8,128)S(1)} %get-tuple-element.81), channel_id=1, source_target_pairs={{0,8},{1,9},{2,10},{3,11},{4,36},{5,37},{6,38},{7,39},{8,16},{9,17... | collective-permute-start | bytes 884744 | tf_op jit(solution)/shard_map/ppermute | solution.py:84
  112.7 25.6 %copy-start.47 = (bf16[16,128,16]{1,2,0:T(8,128)(2,1)S(1)}, bf16[16,128,16]{1,2,0:T(8,128)(2,1)}, u32[]{:S(2)}) copy-start(bf16[16,128,16]{1,2,0:T(8,128)(2,1)} %copy-done.46) | copy-start | bytes 196612
  112.7 25.7 %copy-start.49 = (bf16[2,8,16,128]{3,2,1,0:T(8,128)(2,1)S(1)}, bf16[2,8,16,128]{3,2,1,0:T(8,128)(2,1)}, u32[]{:S(2)}) copy-start(bf16[2,8,16,128]{3,2,1,0:T(8,128)(2,1)} %copy-done.48) | copy-start | bytes 196612
  112.7 26.6 %copy-start.45 = (bf16[2,8,16,128]{3,2,1,0:T(8,128)(2,1)S(1)}, bf16[2,8,16,128]{3,2,1,0:T(8,128)(2,1)}, u32[]{:S(2)}) copy-start(bf16[2,8,16,128]{3,2,1,0:T(8,128)(2,1)} %copy-done.44) | copy-start | bytes 196612
  112.7 32.1 %copy-start.43 = (bf16[2,8,16,128]{3,2,1,0:T(8,128)(2,1)S(1)}, bf16[2,8,16,128]{3,2,1,0:T(8,128)(2,1)}, u32[]{:S(2)}) copy-start(bf16[2,8,16,128]{3,2,1,0:T(8,128)(2,1)} %copy-done.42) | copy-start | bytes 196612
  122.0 8.1 %collective-permute-start.35 = (bf16[8,10240]{1,0:T(8,128)(2,1)S(1)}, bf16[8,10240]{1,0:T(8,128)(2,1)S(1)}, u32[]{:S(2)}, u32[]{:S(2)}) collective-permute-start(bf16[8,10240]{1,0:T(8,128)(2,1)S(1)} %shard_map.173.refs_0_), channel_id=1, source_target_pairs={{0,1},{1,2},{2,3},{3,0},{4,5},{5,6},{6,7},{7,4},{8,9},{9,10},{10,1... | collective-permute-start | bytes 491528 | tf_op jit(solution)/shard_map/ppermute | solution.py:84
  122.4 10.7 %collective-permute-start.36 = (bf16[8,10240]{1,0:T(8,128)(2,1)S(1)}, bf16[8,10240]{1,0:T(8,128)(2,1)S(1)}, u32[]{:S(2)}, u32[]{:S(2)}) collective-permute-start(bf16[8,10240]{1,0:T(8,128)(2,1)S(1)} %shard_map.173.refs_0_), channel_id=1, source_target_pairs={{0,2},{1,3},{2,0},{3,1},{4,6},{5,7},{6,4},{7,5},{8,10},{9,11},{10,... | collective-permute-start | bytes 491528 | tf_op jit(solution)/shard_map/ppermute | solution.py:84
  126.5 6.5 %collective-permute-start.37 = (bf16[8,10240]{1,0:T(8,128)(2,1)S(1)}, bf16[8,10240]{1,0:T(8,128)(2,1)S(1)}, u32[]{:S(2)}, u32[]{:S(2)}) collective-permute-start(bf16[8,10240]{1,0:T(8,128)(2,1)S(1)} %shard_map.173.refs_0_), channel_id=1, source_target_pairs={{0,3},{1,0},{2,1},{3,2},{4,7},{5,4},{6,5},{7,6},{8,11},{9,8},{10,9... | collective-permute-start | bytes 491528 | tf_op jit(solution)/shard_map/ppermute | solution.py:84
  126.9 8.2 %collective-permute-start.34 = (bf16[8,8192]{1,0:T(8,128)(2,1)S(1)}, bf16[8,8192]{1,0:T(8,128)(2,1)S(1)}, u32[]{:S(2)}, u32[]{:S(2)}) collective-permute-start(bf16[8,8192]{1,0:T(8,128)(2,1)S(1)} %get-tuple-element.96), channel_id=1, source_target_pairs={{0,24},{1,25},{2,26},{3,27},{4,100},{5,101},{6,102},{7,103},{8,0},... | collective-permute-start | bytes 393224 | tf_op jit(solution)/shard_map/ppermute | solution.py:84
  128.3 6.8 %collective-permute-start.38 = (bf16[8,8192]{1,0:T(8,128)(2,1)S(1)}, bf16[8,8192]{1,0:T(8,128)(2,1)S(1)}, u32[]{:S(2)}, u32[]{:S(2)}) collective-permute-start(bf16[8,8192]{1,0:T(8,128)(2,1)S(1)} %get-tuple-element.95), channel_id=1, source_target_pairs={{0,16},{1,17},{2,18},{3,19},{4,68},{5,69},{6,70},{7,71},{8,24},{9,... | collective-permute-start | bytes 393224 | tf_op jit(solution)/shard_map/ppermute | solution.py:84
  130.1 6.2 %collective-permute-start.39 = (bf16[8,8192]{1,0:T(8,128)(2,1)S(1)}, bf16[8,8192]{1,0:T(8,128)(2,1)S(1)}, u32[]{:S(2)}, u32[]{:S(2)}) collective-permute-start(bf16[8,8192]{1,0:T(8,128)(2,1)S(1)} %get-tuple-element.94), channel_id=1, source_target_pairs={{0,8},{1,9},{2,10},{3,11},{4,36},{5,37},{6,38},{7,39},{8,16},{9,17... | collective-permute-start | bytes 393224 | tf_op jit(solution)/shard_map/ppermute | solution.py:84
  135.1 12.8 %collective-permute-start.43 = (f32[24,1024]{1,0:T(8,128)S(1)}, f32[24,1024]{1,0:T(8,128)S(1)}, u32[]{:S(2)}, u32[]{:S(2)}) collective-permute-start(f32[24,1024]{1,0:T(8,128)S(1)} %get-tuple-element.91), channel_id=1, source_target_pairs={{0,4},{1,5},{2,6},{3,7},{4,0},{5,1},{6,2},{7,3},{8,12},{9,13},{10,... | collective-permute-start | bytes 294920 | tf_op jit(solution)/shard_map/ppermute | solution.py:84
  139.5 6.3 %collective-permute-start.40 = (bf16[4,8192]{1,0:T(4,128)(2,1)S(1)}, bf16[4,8192]{1,0:T(4,128)(2,1)S(1)}, u32[]{:S(2)}, u32[]{:S(2)}) collective-permute-start(bf16[4,8192]{1,0:T(4,128)(2,1)S(1)} %get-tuple-element.86), channel_id=1, source_target_pairs={{0,1},{1,2},{2,3},{3,0},{4,5},{5,6},{6,7},{7,4},{8,9},{9,10},{10,1... | collective-permute-start | bytes 196616 | tf_op jit(solution)/shard_map/ppermute | solution.py:84
  141.5 5.8 %collective-permute-start.41 = (bf16[4,8192]{1,0:T(4,128)(2,1)S(1)}, bf16[4,8192]{1,0:T(4,128)(2,1)S(1)}, u32[]{:S(2)}, u32[]{:S(2)}) collective-permute-start(bf16[4,8192]{1,0:T(4,128)(2,1)S(1)} %get-tuple-element.87), channel_id=1, source_target_pairs={{0,2},{1,3},{2,0},{3,1},{4,6},{5,7},{6,4},{7,5},{8,10},{9,11},{10,... | collective-permute-start | bytes 196616 | tf_op jit(solution)/shard_map/ppermute | solution.py:84
  142.7 4.5 %collective-permute-start.42 = (bf16[4,8192]{1,0:T(4,128)(2,1)S(1)}, bf16[4,8192]{1,0:T(4,128)(2,1)S(1)}, u32[]{:S(2)}, u32[]{:S(2)}) collective-permute-start(bf16[4,8192]{1,0:T(4,128)(2,1)S(1)} %get-tuple-element.88), channel_id=1, source_target_pairs={{0,3},{1,0},{2,1},{3,2},{4,7},{5,4},{6,5},{7,6},{8,11},{9,8},{10,9... | collective-permute-start | bytes 196616 | tf_op jit(solution)/shard_map/ppermute | solution.py:84
  (49 other events, 543.5 us)

commit v4 on v3

--- a/solution.py
+++ b/solution.py
@@ -17,7 +17,7 @@
 BF = jnp.bfloat16
 F32 = jnp.float32
 CAP = 8
-VMEM = 46 * 1024 * 1024
+VMEM = 26 * 1024 * 1024
 
 
 def causal_forward(queries, keys, values):
@@ -124,7 +124,7 @@
 
 def _slot_spreader(labels, kind):
     length = labels.shape[0]
-    keep = jnp.broadcast_to((labels == kind).astype(F32), (length, CAP))
+    keep = jnp.broadcast_to((labels == kind.astype(F32)).astype(F32), (length, CAP))
     first = lax.broadcasted_iota(jnp.int32, (length, length), 0)
     second = lax.broadcasted_iota(jnp.int32, (length, length), 1)
     rank = jnp.dot((second <= first).astype(F32), keep, preferred_element_type=F32)
@@ -139,59 +139,99 @@
 
 
 RAW = pl.BlockSpec(memory_space=pl.ANY)
-
-
-def _pack_kernel(slot_ref, kinds_ref, labels_ref, rows_ref, out_ref):
-    select = _slot_selector(labels_ref[...], kinds_ref[slot_ref[0]]).astype(BF)
+HELD = pl.BlockSpec(memory_space=pltpu.VMEM)
+
+
+def _pack_kernel(slot_ref, kinds_hbm, labels_hbm, rows_hbm, out_ref, select_ref, column_ref, *refs):
+    kinds_ref, labels_ref, rows_ref, sems = refs
+    copies = [
+        pltpu.make_async_copy(kinds_hbm, kinds_ref, sems.at[0]),
+        pltpu.make_async_copy(labels_hbm, labels_ref, sems.at[1]),
+        pltpu.make_async_copy(rows_hbm, rows_ref, sems.at[2]),
+    ]
+    for copy in copies:
+        copy.start()
+    copies[0].wait()
+    copies[1].wait()
+    labels = labels_ref[...]
+    length = labels.shape[1]
+    select = _slot_selector(labels, kinds_ref[slot_ref[0]]).astype(BF)
+    select_ref[...] = select
+    first = lax.broadcasted_iota(jnp.int32, (length, length), 0)
+    second = lax.broadcasted_iota(jnp.int32, (length, length), 1)
+    spread = jnp.where(first == second, jnp.broadcast_to(labels, (length, length)), 0)
+    column_ref[...] = jnp.sum(spread.astype(F32), axis=1, keepdims=True)
+    copies[2].wait()
     out_ref[...] = jnp.dot(select, rows_ref[...], preferred_element_type=F32).astype(BF)
 
 
 def pack_rows(slot, kinds, labels, rows):
-    out = jax.ShapeDtypeStruct((CAP, rows.shape[1]), BF)
+    length, width = rows.shape
+    outs = [
+        jax.ShapeDtypeStruct((CAP, width), BF),
+        jax.ShapeDtypeStruct((CAP, length), BF),
+        jax.ShapeDtypeStruct((length, 1), F32),
+    ]
     return pl.pallas_call(
         _pack_kernel,
-        grid=(1,),
-        in_specs=[SMALL, SMALL] + _whole(labels, rows),
-        out_specs=_whole(out)[0],
-        out_shape=out,
+        in_specs=[SMALL, RAW, RAW, RAW],
+        out_specs=[HELD] * 3,
+        out_shape=outs,
+        scratch_shapes=[
+            pltpu.SMEM(kinds.shape, jnp.int32),
+            pltpu.VMEM(labels.shape, jnp.int32),
+            pltpu.VMEM(rows.shape, BF),
+            pltpu.SemaphoreType.DMA((3,)),
+        ],
         compiler_params=_params(),
         cost_estimate=SMALL_COST,
     )(slot, kinds, labels, rows)
 
 
 def _gain_rows(labels, gains):
-    return jnp.where(labels == 0, gains[0:1], jnp.where(labels == 1, gains[1:2], gains[2:3]))
-
-
-def _norm_kernel(slot_ref, kinds_ref, labels_ref, column_ref, residual_ref, gains_ref, *refs):
-    blocks, (hidden_ref, packed_ref, joined_ref) = refs[:NS], refs[NS:]
+    return jnp.where(labels == 0.0, gains[0:1], jnp.where(labels == 1.0, gains[1:2], gains[2:3]))
+
+
+def _norm_kernel(slot_ref, select_ref, column_ref, residual_hbm, gains_hbm, *refs):
+    blocks, (hidden_ref, packed_ref, joined_ref, residual_ref, gains_ref, sems) = refs[:NS], refs[NS:]
+    copies = [
+        pltpu.make_async_copy(residual_hbm, residual_ref, sems.at[0]),
+        pltpu.make_async_copy(gains_hbm, gains_ref, sems.at[1]),
+    ]
+    for copy in copies:
+        copy.start()
     slot = slot_ref[0]
     width = blocks[0].shape[1]
     for k, block in enumerate(blocks):
         owner = lax.rem(slot - k + NS, NS)
         joined_ref[:, pl.ds(pl.multiple_of(owner * width, width), width)] = block[...]
+    for copy in copies:
+        copy.wait()
     hidden = (residual_ref[...].astype(F32) + joined_ref[...].astype(F32)).astype(BF)
     hidden_ref[...] = hidden
     hidden_f = hidden.astype(F32)
     inverse = lax.rsqrt(jnp.mean(hidden_f * hidden_f, axis=-1, keepdims=True) + 1e-05)
     normed = (hidden_f * inverse * _gain_rows(column_ref[...], gains_ref[...])).astype(BF)
-    select = _slot_selector(labels_ref[...], kinds_ref[slot]).astype(BF)
-    packed_ref[...] = jnp.dot(select, normed, preferred_element_type=F32).astype(BF)
-
-
-def norm_rows_of(slot, kinds, labels, column, residual, gains, blocks):
+    packed_ref[...] = jnp.dot(select_ref[...], normed, preferred_element_type=F32).astype(BF)
+
+
+def norm_rows_of(slot, select, column, residual, gains, blocks):
     length, width = residual.shape
     outs = [jax.ShapeDtypeStruct((length, width), BF), jax.ShapeDtypeStruct((CAP, width), BF)]
     return pl.pallas_call(
         _norm_kernel,
-        grid=(1,),
-        in_specs=[SMALL, SMALL] + _whole(labels, column, residual, gains, *blocks),
-        out_specs=_whole(*outs),
+        in_specs=[SMALL, HELD, HELD, RAW, RAW] + [HELD] * NS,
+        out_specs=[HELD, HELD],
         out_shape=outs,
-        scratch_shapes=[pltpu.VMEM((length, width), BF)],
-        compiler_params=_params(),
-        cost_estimate=SMALL_COST,
-    )(slot, kinds, labels, column, residual, gains, *blocks)
+        scratch_shapes=[
+            pltpu.VMEM((length, width), BF),
+            pltpu.VMEM((length, width), BF),
+            pltpu.VMEM(gains.shape, F32),
+            pltpu.SemaphoreType.DMA((2,)),
+        ],
+        compiler_params=_params(),
+        cost_estimate=SMALL_COST,
+    )(slot, select, column, residual, gains, *blocks)
 
 
 def _finish_kernel(slot_ref, kinds_ref, column_ref, hidden_ref, cot_ref, gains_ref, *refs):
@@ -249,9 +289,6 @@
     )(slot, kinds, column, hidden, cot, gains, *sums)
 
 
-HELD = pl.BlockSpec(memory_space=pltpu.VMEM)
-
-
 def _load_kernel(w_hbm, out_ref, sem):
     copy = pltpu.make_async_copy(w_hbm.at[0], out_ref, sem)
     copy.start()
@@ -413,10 +450,9 @@
     return high, (value - high.astype(F32)).astype(BF)
 
 
-def _own_kernel(count, left_ref, w_ref, in_hbm, *refs):
-    rows_hbm, outs_hbm = refs[:count], refs[count : count + 4]
-    in_ref, rows_ref, gain_ref = refs[count + 4 : count + 7]
-    outs, (sems, out_sems) = refs[count + 7 : count + 11], refs[count + 11 :]
+def _own_kernel(count, left_ref, w_ref, in_ref, *refs):
+    rows_hbm, outs = refs[:count], refs[count : count + 4]
+    rows_ref, gain_ref, sems = refs[count + 4 :]
     width = w_ref.shape[1]
     half = in_ref.shape[0]
     part = half // 4
@@ -424,34 +460,22 @@
     groups = []
     for n in range(width // OUT_STEP):
         span = pl.ds(n * OUT_STEP, OUT_STEP)
-        group = [pltpu.make_async_copy(in_hbm.at[:, span], in_ref.at[:, span], sems.at[n, 0])]
-        for p, piece in enumerate(rows_hbm):
-            group.append(
-                pltpu.make_async_copy(
-                    piece.at[:, span], rows_ref.at[pl.ds(p * part, part), span], sems.at[n, p + 1]
-                )
-            )
+        group = [
+            pltpu.make_async_copy(piece.at[:, span], rows_ref.at[pl.ds(p * part, part), span], sems.at[n, p])
+            for p, piece in enumerate(rows_hbm)
+        ]
         for copy in group:
             copy.start()
         groups.append(group)
-    copies = []
-
-    def put(span, n):
-        for k in range(4):
-            copy = pltpu.make_async_copy(outs[k].at[:, span], outs_hbm[k].at[:, span], out_sems.at[n, k])
-            copy.start()
-            copies.append(copy)
-
     for n, group in enumerate(groups):
         span = pl.ds(n * OUT_STEP, OUT_STEP)
         total = jnp.dot(left_ref[:half, :], w_ref[:, span], preferred_element_type=F32)
-        for copy in group:
-            copy.wait()
         total = total + in_ref[:, span].astype(F32)
         for k, out_ref in enumerate(outs):
             out_ref[:, span] = total[k * part : (k + 1) * part].astype(out_ref.dtype)
-        put(span, n)
         if count:
+            for copy in group:
+                copy.wait()
             gain = jnp.sum(rows_ref[:, span].astype(F32) * total, axis=0, keepdims=True)
             for j in range(OUT_STEP // short):
                 row = n * (OUT_STEP // short) + j
@@ -463,9 +487,6 @@
         for out_ref in outs[1:]:
             out_ref[:, width : width + short] = high
             out_ref[:, width + short :] = low
-        put(pl.ds(width, 2 * short), len(groups))
-    for copy in copies:
-        copy.wait()
 
 
 def own_product(left, weight, arrived, rows=()):
@@ -477,18 +498,13 @@
     kinds = [F32, BF, BF, BF]
     return pl.pallas_call(
         functools.partial(_own_kernel, len(rows)),
-        in_specs=[HELD, HELD] + [RAW] * (1 + len(rows)),
-        out_specs=[RAW] * 4,
+        in_specs=[HELD, HELD, HELD] + [RAW] * len(rows),
+        out_specs=[HELD] * 4,
         out_shape=[jax.ShapeDtypeStruct((part, wide), kind) for kind in kinds],
         scratch_shapes=[
-            pltpu.VMEM((half, width), BF),
             pltpu.VMEM((half, width) if rows else (16, 128), BF),
             pltpu.VMEM((part, short), F32),
-        ]
-        + [pltpu.VMEM((part, wide), kind) for kind in kinds]
-        + [
-            pltpu.SemaphoreType.DMA((width // OUT_STEP, 1 + len(rows))),
-            pltpu.SemaphoreType.DMA((width // OUT_STEP + 1, 4)),
+            pltpu.SemaphoreType.DMA((width // OUT_STEP, max(1, len(rows)))),
         ],
         compiler_params=_params(),
         cost_estimate=SMALL_COST,
@@ -627,19 +643,16 @@
 ):
     slot_index = lax.axis_index("sect")
     slot = slot_index.astype(jnp.int32).reshape(1)
-    column = labels.reshape(-1, 1)
     length = labels.shape[1]
     grad_full = cotangent[0]
-    packed_cot = pack_rows(slot, slot_modality, labels, grad_full)
+    packed_cot, select, column = pack_rows(slot, slot_modality, labels, grad_full)
     queries, keys, values, _ = lax.optimization_barrier((queries, keys, values, packed_cot))
     cot_near = gather_near(packed_cot)
 
     attended_block, probs, probs_b = causal_forward(queries, keys, values)
     block = attended_block[0]
     blocks = [block] + [send_sect(block, k) for k in (1, 2, 3)]
-    hidden, packed = norm_rows_of(
-        slot, slot_modality, labels, column, after(residual[0], cot_near), gains, blocks
-    )
+    hidden, packed = norm_rows_of(slot, after(select, cot_near), column, residual[0], gains, blocks)
     cot_far = gather_far(cot_near)
     cot_rows = cot_far + [swap_core(piece) for piece in cot_far]
     near = gather_near(after(packed, *cot_far[1:]))

time: 149 us -> 139 us (0.933)
  Pallas kernels: 49.5 us -> 28.9 us
  waiting for transfers between devices: 26.5 us -> 38.5 us
    ppermute x44, waiting for transfers between devices: 26.5 us -> 38.5 us  [send(): return lax.ppermute(block, AXES, pairs)]
    pallas_call x2, Pallas kernels: 13.1 us -> 4.82 us  [own_product(): pl.pallas_call(functools.partial(_own_kernel, len(rows)), in_specs=[HELD,...]
    pallas_call x2, Pallas kernels: 7.25 us -> 1.11 us  [load_weight(): pl.pallas_call(_load_kernel, in_specs=[RAW], out_specs=HELD, out_shape=pl...]
    pallas_call x1, Pallas kernels: 5.85 us -> 2.63 us  [back_product(): pl.pallas_call(_back_kernel, grid=(width // tile,), in_specs=[pl.BlockSpe...]
    pallas_call x1, Pallas kernels: 8.62 us -> 5.86 us  [pre_product(): pl.pallas_call(_pre_kernel, in_specs=[RAW] * 8 + [HELD, HELD], out_specs=...]
    unnamed x115 -> x36, local copies, waits for them, and re-layouts: 9.7 us -> 9.88 us
  transfers between devices with their start and end apart: 44 -> 44, of which waited for: 18 -> 22; matrix products, arithmetic and copies ran while one was open for 6% -> 6% of each run, Pallas kernels for 27% -> 16%
where the time goes in v4:
time: 139 us
  starting transfers between devices  54.3 us (39%)
  waiting for transfers between devices  38.5 us (28%)
  Pallas kernels  28.9 us (21%)
  local copies, waits for them, and re-layouts  11.3 us (8%)
  matrix products  2.93 us (2%)
  other arithmetic  1.82 us (1%)
    ppermute x44, starting transfers between devices, send(): return lax.ppermute(block, AXES, pairs)  54.3 us
    ppermute x44, waiting for transfers between devices, send(): return lax.ppermute(block, AXES, pairs)  38.5 us
    unnamed x36, local copies, waits for them, and re-layouts  9.88 us
    pallas_call x2, Pallas kernels, weight_grad(): pl.pallas_call(_down_kernel, grid=(width // tile,), in_specs=[pl.BlockSpe...  7.5 us
    pallas_call x1, Pallas kernels, pre_product(): pl.pallas_call(_pre_kernel, in_specs=[RAW] * 8 + [HELD, HELD], out_specs=...  5.86 us
    pallas_call x2, Pallas kernels, own_product(): pl.pallas_call(functools.partial(_own_kernel, len(rows)), in_specs=[HELD,...  4.82 us
  transfers between devices with their start and end apart: 44, of which 22 were waited for; matrix products, arithmetic and copies ran while one was open for 6% of the time, Pallas kernels for 16%

profile of v4, /device:TPU:0, one launch (start us, length us, event | category | flops | bytes accessed | tf_op | source)
XLA Modules:
  0.0 138.7 jit_solution(6558279737272278255)
XLA Ops:
  3.8 1.6 %collective-permute-start = (bf16[8,8192]{1,0:T(8,128)(2,1)S(1)}, bf16[8,8192]{1,0:T(8,128)(2,1)S(1)}, u32[]{:S(2)}, u32[]{:S(2)}) collective-permute-start(bf16[8,8192]{1,0:T(8,128)(2,1)S(1)} %get-tuple-element.54), channel_id=1, source_target_pairs={{0,8},{1,9},{2,10},{3,11},{4,36},{5,37},{6,38},{7,39},{8,16},{9,17... | collective-permute-start | bytes 393224 | tf_op jit(solution)/shard_map/ppermute | solution.py:84
  5.4 2.7 %collective-permute-start.1 = (bf16[8,8192]{1,0:T(8,128)(2,1)S(1)}, bf16[8,8192]{1,0:T(8,128)(2,1)S(1)}, u32[]{:S(2)}, u32[]{:S(2)}) collective-permute-start(bf16[8,8192]{1,0:T(8,128)(2,1)S(1)} %get-tuple-element.54), channel_id=1, source_target_pairs={{0,16},{1,17},{2,18},{3,19},{4,68},{5,69},{6,70},{7,71},{8,24},{9,... | collective-permute-start | bytes 393224 | tf_op jit(solution)/shard_map/ppermute | solution.py:84
  8.2 1.4 %collective-permute-start.2 = (bf16[8,8192]{1,0:T(8,128)(2,1)S(1)}, bf16[8,8192]{1,0:T(8,128)(2,1)S(1)}, u32[]{:S(2)}, u32[]{:S(2)}) collective-permute-start(bf16[8,8192]{1,0:T(8,128)(2,1)S(1)} %get-tuple-element.54), channel_id=1, source_target_pairs={{0,24},{1,25},{2,26},{3,27},{4,100},{5,101},{6,102},{7,103},{8,0},... | collective-permute-start | bytes 393224 | tf_op jit(solution)/shard_map/ppermute | solution.py:84
  13.2 2.0 %collective-permute-start.6 = (bf16[32,8192]{1,0:T(8,128)(2,1)S(1)}, bf16[32,8192]{1,0:T(8,128)(2,1)S(1)}, u32[]{:S(2)}, u32[]{:S(2)}) collective-permute-start(bf16[32,8192]{1,0:T(8,128)(2,1)S(1)} %constant_dynamic-update-slice_fusion.refs_0_), channel_id=1, source_target_pairs={{0,32},{1,33},{2,34},{3,35},{4,12},{5,13},{6,14},{7,15},{8,40},{9,... | collective-permute-start | bytes 1572872 | tf_op jit(solution)/shard_map/ppermute | solution.py:84
  15.1 3.6 %collective-permute-start.7 = (bf16[32,8192]{1,0:T(8,128)(2,1)S(1)}, bf16[32,8192]{1,0:T(8,128)(2,1)S(1)}, u32[]{:S(2)}, u32[]{:S(2)}) collective-permute-start(bf16[32,8192]{1,0:T(8,128)(2,1)S(1)} %constant_dynamic-update-slice_fusion.refs_0_), channel_id=1, source_target_pairs={{0,64},{1,65},{2,66},{3,67},{4,20},{5,21},{6,22},{7,23},{8,72},{9,... | collective-permute-start | bytes 1572872 | tf_op jit(solution)/shard_map/ppermute | solution.py:84
  20.7 1.6 %collective-permute-start.3 = (bf16[16,2048]{1,0:T(8,128)(2,1)S(1)}, bf16[16,2048]{1,0:T(8,128)(2,1)S(1)}, u32[]{:S(2)}, u32[]{:S(2)}) collective-permute-start(bf16[16,2048]{1,0:T(8,128)(2,1)S(1)} %bitcast.79), channel_id=1, source_target_pairs={{0,1},{1,2},{2,3},{3,0},{4,5},{5,6},{6,7},{7,4},{8,9},{9,10},{10,1... | collective-permute-start | bytes 196616 | tf_op jit(solution)/shard_map/ppermute | solution.py:84
  22.3 2.9 %collective-permute-start.4 = (bf16[16,2048]{1,0:T(8,128)(2,1)S(1)}, bf16[16,2048]{1,0:T(8,128)(2,1)S(1)}, u32[]{:S(2)}, u32[]{:S(2)}) collective-permute-start(bf16[16,2048]{1,0:T(8,128)(2,1)S(1)} %bitcast.80), channel_id=1, source_target_pairs={{0,2},{1,3},{2,0},{3,1},{4,6},{5,7},{6,4},{7,5},{8,10},{9,11},{10,... | collective-permute-start | bytes 196616 | tf_op jit(solution)/shard_map/ppermute | solution.py:84
  26.2 1.8 %collective-permute-start.5 = (bf16[16,2048]{1,0:T(8,128)(2,1)S(1)}, bf16[16,2048]{1,0:T(8,128)(2,1)S(1)}, u32[]{:S(2)}, u32[]{:S(2)}) collective-permute-start(bf16[16,2048]{1,0:T(8,128)(2,1)S(1)} %bitcast.81), channel_id=1, source_target_pairs={{0,3},{1,0},{2,1},{3,2},{4,7},{5,4},{6,5},{7,6},{8,11},{9,8},{10,9... | collective-permute-start | bytes 196616 | tf_op jit(solution)/shard_map/ppermute | solution.py:84
  28.1 2.3 %collective-permute-done.5.refs_3_ = bf16[16,2048]{1,0:T(8,128)(2,1)S(1)} collective-permute-done((bf16[16,2048]{1,0:T(8,128)(2,1)S(1)}, bf16[16,2048]{1,0:T(8,128)(2,1)S(1)}, u32[]{:S(2)}, u32[]{:S(2)}) %collective-permute-start.5) | collective-permute-done | bytes 65568 | tf_op jit(solution)/shard_map/ppermute | solution.py:84
  33.0 1.3 collective-permute-start.9
  34.3 2.9 %collective-permute-start.10 = (bf16[8,8192]{1,0:T(8,128)(2,1)S(1)}, bf16[8,8192]{1,0:T(8,128)(2,1)S(1)}, u32[]{:S(2)}, u32[]{:S(2)}) collective-permute-start(bf16[8,8192]{1,0:T(8,128)(2,1)S(1)} %get-tuple-element.62), channel_id=1, source_target_pairs={{0,16},{1,17},{2,18},{3,19},{4,68},{5,69},{6,70},{7,71},{8,24},{9,... | collective-permute-start | bytes 393224 | tf_op jit(solution)/shard_map/ppermute | solution.py:84
  38.1 1.1 collective-permute-done.9
  39.3 2.3 %collective-permute-done.10 = bf16[8,8192]{1,0:T(8,128)(2,1)S(1)} collective-permute-done((bf16[8,8192]{1,0:T(8,128)(2,1)S(1)}, bf16[8,8192]{1,0:T(8,128)(2,1)S(1)}, u32[]{:S(2)}, u32[]{:S(2)}) %collective-permute-start.10) | collective-permute-done | bytes 131104 | tf_op jit(solution)/shard_map/ppermute | solution.py:84
  42.9 1.4 %collective-permute-start.12 = (bf16[32,8192]{1,0:T(8,128)(2,1)S(1)}, bf16[32,8192]{1,0:T(8,128)(2,1)S(1)}, u32[]{:S(2)}, u32[]{:S(2)}) collective-permute-start(bf16[32,8192]{1,0:T(8,128)(2,1)S(1)} %constant_dynamic-update-slice_fusion.4.refs_0_), channel_id=1, source_target_pairs={{0,32},{1,33},{2,34},{3,35},{4,12},{5,13},{6,14},{7,15},{8,40},{9,... | collective-permute-start | bytes 1572872 | tf_op jit(solution)/shard_map/ppermute | solution.py:84
  44.4 1.1 collective-permute-start.13
  45.5 2.6 %copy-done = bf16[1,344,8192]{2,1,0:T(8,128)(2,1)S(1)} copy-done((bf16[1,344,8192]{2,1,0:T(8,128)(2,1)S(1)}, bf16[1,344,8192]{2,1,0:T(8,128)(2,1)}, u32[]{:S(2)}) %copy-start) | copy-done | bytes 5636120
  49.4 2.6 %shard_map.163.refs_9_ = f32[344,256]{1,0:T(8,128)S(1)} custom-call(bf16[32,8192]{1,0:T(8,128)(2,1)S(1)} %constant_dynamic-update-slice_fusion.refs_0_, bf16[32,8192]{1,0:T(8,128)(2,1)S(1)} %collective-permute-done.6.refs_1_, bf16[32,8192]{1,0:T(8,128)(2,1)S(1)} %collective-permute-done.7.refs_2_, bf16[32,8192]{1,0:T(8,128)(2,1)S(1)} %collective-permute-done.8.refs_3_, ...), custom_call_target="tpu_custom_call" | custom-call | flops 1000 | bytes 1000 | tf_op jit(solution)/shard_map/pallas_call | solution.py:327
  52.6 6.4 %collective-permute-done.12.refs_1_ = bf16[32,8192]{1,0:T(8,128)(2,1)S(1)} collective-permute-done((bf16[32,8192]{1,0:T(8,128)(2,1)S(1)}, bf16[32,8192]{1,0:T(8,128)(2,1)S(1)}, u32[]{:S(2)}, u32[]{:S(2)}) %collective-permute-start.12) | collective-permute-done | bytes 524320 | tf_op jit(solution)/shard_map/ppermute | solution.py:84
  59.5 1.4 %collective-permute-done.20.refs_5_ = bf16[32,8192]{1,0:T(8,128)(2,1)S(1)} collective-permute-done((bf16[32,8192]{1,0:T(8,128)(2,1)S(1)}, bf16[32,8192]{1,0:T(8,128)(2,1)S(1)}, u32[]{:S(2)}, u32[]{:S(2)}) %collective-permute-start.20) | collective-permute-done | bytes 524320 | tf_op jit(solution)/shard_map/ppermute | solution.py:84
  61.6 5.9 %shard_map.166 = (bf16[344,256]{1,0:T(8,128)(2,1)S(1)}, bf16[344,256]{1,0:T(8,128)(2,1)S(1)}, bf16[256,344]{1,0:T(8,128)(2,1)S(1)}, bf16[256,344]{1,0:T(8,128)(2,1)S(1)}, bf16[128,8192]{1,0:T(8,128)(2,1)S(1)}) custom-call(bf16[32,8192]{1,0:T(8,128)(2,1)S(1)} %constant_dynamic-update-slice_fusion.4.refs_0_, ...), custom_call_target="tpu_custom_call" | custom-call | flops 1000 | bytes 1000 | tf_op jit(solution)/shard_map/pallas_call | solution.py:403
  67.7 2.0 %shard_map.167 = bf16[128,8192]{1,0:T(8,128)(2,1)S(1)} custom-call(bf16[256,344]{1,0:T(8,128)(2,1)S(1)} %get-tuple-element.70.left_ref, bf16[344,8192]{1,0:T(8,128)(2,1)S(1)} %shard_map.165.w_ref), custom_call_target="tpu_custom_call" | custom-call | flops 1000 | bytes 1000 | tf_op jit(solution)/shard_map/pallas_call | solution.py:437
  70.1 1.6 %collective-permute-done.23.in_ref = bf16[128,8192]{1,0:T(8,128)(2,1)S(1)} collective-permute-done((bf16[128,8192]{1,0:T(8,128)(2,1)S(1)}, bf16[128,8192]{1,0:T(8,128)(2,1)S(1)}, u32[]{:S(2)}, u32[]{:S(2)}) %collective-permute-start.23) | collective-permute-done | bytes 2097184 | tf_op jit(solution)/shard_map/ppermute | solution.py:84
  71.7 3.5 %shard_map.168 = (f32[32,8704]{1,0:T(8,128)S(1)}, bf16[32,8704]{1,0:T(8,128)(2,1)S(1)}, bf16[32,8704]{1,0:T(8,128)(2,1)S(1)}, bf16[32,8704]{1,0:T(8,128)(2,1)S(1)}) custom-call(bf16[256,344]{1,0:T(8,128)(2,1)S(1)} %get-tuple-element.68.left_ref, bf16[344,8192]{1,0:T(8,128)(2,1)S(1)} %shard_map.164.refs_8_.w_ref, ...), custom_call_target="tpu_custom_call" | custom-call | flops 1000 | bytes 1000 | tf_op jit(solution)/shard_map/pallas_call | solution.py:499
  75.3 1.9 %collective-permute-start.26 = (bf16[32,8704]{1,0:T(8,128)(2,1)S(1)}, bf16[32,8704]{1,0:T(8,128)(2,1)S(1)}, u32[]{:S(2)}, u32[]{:S(2)}) collective-permute-start(bf16[32,8704]{1,0:T(8,128)(2,1)S(1)} %get-tuple-element.76), channel_id=1, source_target_pairs={{0,64},{1,65},{2,66},{3,67},{4,20},{5,21},{6,22},{7,23},{8,72},{9,... | collective-permute-start | bytes 1671176 | tf_op jit(solution)/shard_map/ppermute | solution.py:84
  77.6 1.3 shard_map.169
  79.0 2.9 %collective-permute-start.29 = (bf16[32,8192]{1,0:T(8,128)(2,1)S(1)}, bf16[32,8192]{1,0:T(8,128)(2,1)S(1)}, u32[]{:S(2)}, u32[]{:S(2)}) collective-permute-start(bf16[32,8192]{1,0:T(8,128)(2,1)S(1)} %get-tuple-element.82), channel_id=1, source_target_pairs={{0,96},{1,97},{2,98},{3,99},{4,28},{5,29},{6,30},{7,31},{8,104},{9... | collective-permute-start | bytes 1572872 | tf_op jit(solution)/shard_map/ppermute | solution.py:84
  82.9 1.9 %collective-permute-done.25.refs_0_ = bf16[32,8704]{1,0:T(8,128)(2,1)S(1)} collective-permute-done((bf16[32,8704]{1,0:T(8,128)(2,1)S(1)}, bf16[32,8704]{1,0:T(8,128)(2,1)S(1)}, u32[]{:S(2)}, u32[]{:S(2)}) %collective-permute-start.25) | collective-permute-done | bytes 557088 | tf_op jit(solution)/shard_map/ppermute | solution.py:84
  84.8 3.7 %shard_map.170 = bf16[1,344,8192]{2,1,0:T(8,128)(2,1)} custom-call(bf16[32,8192]{1,0:T(8,128)(2,1)S(1)} %constant_dynamic-update-slice_fusion.refs_0_, bf16[32,8192]{1,0:T(8,128)(2,1)S(1)} %collective-permute-done.6.refs_1_, bf16[32,8192]{1,0:T(8,128)(2,1)S(1)} %collective-permute-done.7.refs_2_, bf16[32,8192]{1,0:T(8,128)(2,1)S(1)} %collective-permute-done.8.refs_3_, ...), custom_call_target="tpu_custom_call" | custom-call | flops 1442840576 | bytes 9830400 | tf_op jit(solution)/shard_map/pallas_call | solution.py:621
  88.6 3.8 %collective-permute-done.27.refs_2_ = bf16[32,8704]{1,0:T(8,128)(2,1)S(1)} collective-permute-done((bf16[32,8704]{1,0:T(8,128)(2,1)S(1)}, bf16[32,8704]{1,0:T(8,128)(2,1)S(1)}, u32[]{:S(2)}, u32[]{:S(2)}) %collective-permute-start.27) | collective-permute-done | bytes 557088 | tf_op jit(solution)/shard_map/ppermute | solution.py:84
  92.6 2.1 %collective-permute-start.28 = (f32[8,9216]{1,0:T(8,128)S(1)}, f32[8,9216]{1,0:T(8,128)S(1)}, u32[]{:S(2)}, u32[]{:S(2)}) collective-permute-start(f32[8,9216]{1,0:T(8,128)S(1)} %get-tuple-element.79), channel_id=1, source_target_pairs={{0,24},{1,25},{2,26},{3,27},{4,100},{5,101},{6,102},{7,103},{8,0},... | collective-permute-start | bytes 884744 | tf_op jit(solution)/shard_map/ppermute | solution.py:84
  94.7 1.1 collective-permute-start.32
  96.6 2.5 %collective-permute-start.33 = (f32[8,9216]{1,0:T(8,128)S(1)}, f32[8,9216]{1,0:T(8,128)S(1)}, u32[]{:S(2)}, u32[]{:S(2)}) collective-permute-start(f32[8,9216]{1,0:T(8,128)S(1)} %get-tuple-element.87), channel_id=1, source_target_pairs={{0,8},{1,9},{2,10},{3,11},{4,36},{5,37},{6,38},{7,39},{8,16},{9,17... | collective-permute-start | bytes 884744 | tf_op jit(solution)/shard_map/ppermute | solution.py:84
  99.0 3.8 %shard_map.172 = bf16[1,344,8192]{2,1,0:T(8,128)(2,1)} custom-call(bf16[32,8192]{1,0:T(8,128)(2,1)S(1)} %constant_dynamic-update-slice_fusion.4.refs_0_, bf16[32,8192]{1,0:T(8,128)(2,1)S(1)} %collective-permute-done.12.refs_1_, bf16[32,8192]{1,0:T(8,128)(2,1)S(1)} %collective-permute-done.13.refs_2_, bf16[32,8192]{1,0:T(8,128)(2,1)S(1)} %collective-permute-done.14.refs_3_, ...), custom_call_target="tpu_custom_call" | custom-call | flops 1442840576 | bytes 9830400 | tf_op jit(solution)/shard_map/pallas_call | solution.py:621
  102.8 7.1 %collective-permute-done.31 = bf16[32,8192]{1,0:T(8,128)(2,1)S(1)} collective-permute-done((bf16[32,8192]{1,0:T(8,128)(2,1)S(1)}, bf16[32,8192]{1,0:T(8,128)(2,1)S(1)}, u32[]{:S(2)}, u32[]{:S(2)}) %collective-permute-start.31) | collective-permute-done | bytes 524320 | tf_op jit(solution)/shard_map/ppermute | solution.py:84
  110.2 2.1 %collective-permute-start.35 = (bf16[8,10240]{1,0:T(8,128)(2,1)S(1)}, bf16[8,10240]{1,0:T(8,128)(2,1)S(1)}, u32[]{:S(2)}, u32[]{:S(2)}) collective-permute-start(bf16[8,10240]{1,0:T(8,128)(2,1)S(1)} %shard_map.173.refs_0_), channel_id=1, source_target_pairs={{0,1},{1,2},{2,3},{3,0},{4,5},{5,6},{6,7},{7,4},{8,9},{9,10},{10,1... | collective-permute-start | bytes 491528 | tf_op jit(solution)/shard_map/ppermute | solution.py:84
  112.3 2.4 %collective-permute-start.36 = (bf16[8,10240]{1,0:T(8,128)(2,1)S(1)}, bf16[8,10240]{1,0:T(8,128)(2,1)S(1)}, u32[]{:S(2)}, u32[]{:S(2)}) collective-permute-start(bf16[8,10240]{1,0:T(8,128)(2,1)S(1)} %shard_map.173.refs_0_), channel_id=1, source_target_pairs={{0,2},{1,3},{2,0},{3,1},{4,6},{5,7},{6,4},{7,5},{8,10},{9,11},{10,... | collective-permute-start | bytes 491528 | tf_op jit(solution)/shard_map/ppermute | solution.py:84
  114.7 1.8 %collective-permute-start.37 = (bf16[8,10240]{1,0:T(8,128)(2,1)S(1)}, bf16[8,10240]{1,0:T(8,128)(2,1)S(1)}, u32[]{:S(2)}, u32[]{:S(2)}) collective-permute-start(bf16[8,10240]{1,0:T(8,128)(2,1)S(1)} %shard_map.173.refs_0_), channel_id=1, source_target_pairs={{0,3},{1,0},{2,1},{3,2},{4,7},{5,4},{6,5},{7,6},{8,11},{9,8},{10,9... | collective-permute-start | bytes 491528 | tf_op jit(solution)/shard_map/ppermute | solution.py:84
  116.8 1.8 %collective-permute-start.34 = (bf16[8,8192]{1,0:T(8,128)(2,1)S(1)}, bf16[8,8192]{1,0:T(8,128)(2,1)S(1)}, u32[]{:S(2)}, u32[]{:S(2)}) collective-permute-start(bf16[8,8192]{1,0:T(8,128)(2,1)S(1)} %get-tuple-element.102), channel_id=1, source_target_pairs={{0,24},{1,25},{2,26},{3,27},{4,100},{5,101},{6,102},{7,103},{8,0},... | collective-permute-start | bytes 393224 | tf_op jit(solution)/shard_map/ppermute | solution.py:84
  118.7 1.4 collective-permute-start.38
  120.1 2.8 %collective-permute-done.36.refs_2_ = bf16[8,10240]{1,0:T(8,128)(2,1)S(1)} collective-permute-done((bf16[8,10240]{1,0:T(8,128)(2,1)S(1)}, bf16[8,10240]{1,0:T(8,128)(2,1)S(1)}, u32[]{:S(2)}, u32[]{:S(2)}) %collective-permute-start.36) | collective-permute-done | bytes 163872 | tf_op jit(solution)/shard_map/ppermute | solution.py:84
  122.9 2.1 %shard_map.174 = (bf16[4,8192]{1,0:T(4,128)(2,1)}, bf16[16,2048]{1,0:T(8,128)(2,1)S(1)}, f32[24,1024]{1,0:T(8,128)S(1)}) custom-call(s32[1]{0:T(128)} %bitcast.2.slot_ref, s32[4]{0:T(128)S(1)} %copy-done.7, f32[16,1]{1,0:T(8,128)S(1)} %get-tuple-element.56.column_ref, bf16[16,8192]{1,0:T(8,128)(2,1)S(1)} %get-tuple-element.60.hidden_ref, ...), custom_call_target="tpu_custom_call" | custom-call | flops 1000 | bytes 1000 | tf_op jit(solution)/shard_map/pallas_call | solution.py:280
  125.2 1.4 collective-permute-done.39.refs_3_
  126.5 1.0 shard_map.175
  127.6 1.1 fusion.9
  128.8 1.1 fusion.6
  130.2 2.0 %collective-permute-start.41 = (bf16[4,8192]{1,0:T(4,128)(2,1)S(1)}, bf16[4,8192]{1,0:T(4,128)(2,1)S(1)}, u32[]{:S(2)}, u32[]{:S(2)}) collective-permute-start(bf16[4,8192]{1,0:T(4,128)(2,1)S(1)} %get-tuple-element.93), channel_id=1, source_target_pairs={{0,2},{1,3},{2,0},{3,1},{4,6},{5,7},{6,4},{7,5},{8,10},{9,11},{10,... | collective-permute-start | bytes 196616 | tf_op jit(solution)/shard_map/ppermute | solution.py:84
  132.2 1.7 %collective-permute-start.42 = (bf16[4,8192]{1,0:T(4,128)(2,1)S(1)}, bf16[4,8192]{1,0:T(4,128)(2,1)S(1)}, u32[]{:S(2)}, u32[]{:S(2)}) collective-permute-start(bf16[4,8192]{1,0:T(4,128)(2,1)S(1)} %get-tuple-element.94), channel_id=1, source_target_pairs={{0,3},{1,0},{2,1},{3,2},{4,7},{5,4},{6,5},{7,6},{8,11},{9,8},{10,9... | collective-permute-start | bytes 196616 | tf_op jit(solution)/shard_map/ppermute | solution.py:84
  135.3 1.4 collective-permute-done.40
  (112 shorter events, 25.5 us)
Async XLA Ops:
  3.8 8.4 %collective-permute-start = (bf16[8,8192]{1,0:T(8,128)(2,1)S(1)}, bf16[8,8192]{1,0:T(8,128)(2,1)S(1)}, u32[]{:S(2)}, u32[]{:S(2)}) collective-permute-start(bf16[8,8192]{1,0:T(8,128)(2,1)S(1)} %get-tuple-element.54), channel_id=1, source_target_pairs={{0,8},{1,9},{2,10},{3,11},{4,36},{5,37},{6,38},{7,39},{8,16},{9,17... | collective-permute-start | bytes 393224 | tf_op jit(solution)/shard_map/ppermute | solution.py:84
  5.4 7.1 %collective-permute-start.1 = (bf16[8,8192]{1,0:T(8,128)(2,1)S(1)}, bf16[8,8192]{1,0:T(8,128)(2,1)S(1)}, u32[]{:S(2)}, u32[]{:S(2)}) collective-permute-start(bf16[8,8192]{1,0:T(8,128)(2,1)S(1)} %get-tuple-element.54), channel_id=1, source_target_pairs={{0,16},{1,17},{2,18},{3,19},{4,68},{5,69},{6,70},{7,71},{8,24},{9,... | collective-permute-start | bytes 393224 | tf_op jit(solution)/shard_map/ppermute | solution.py:84
  8.2 5.0 %collective-permute-start.2 = (bf16[8,8192]{1,0:T(8,128)(2,1)S(1)}, bf16[8,8192]{1,0:T(8,128)(2,1)S(1)}, u32[]{:S(2)}, u32[]{:S(2)}) collective-permute-start(bf16[8,8192]{1,0:T(8,128)(2,1)S(1)} %get-tuple-element.54), channel_id=1, source_target_pairs={{0,24},{1,25},{2,26},{3,27},{4,100},{5,101},{6,102},{7,103},{8,0},... | collective-permute-start | bytes 393224 | tf_op jit(solution)/shard_map/ppermute | solution.py:84
  13.2 19.8 %collective-permute-start.6 = (bf16[32,8192]{1,0:T(8,128)(2,1)S(1)}, bf16[32,8192]{1,0:T(8,128)(2,1)S(1)}, u32[]{:S(2)}, u32[]{:S(2)}) collective-permute-start(bf16[32,8192]{1,0:T(8,128)(2,1)S(1)} %constant_dynamic-update-slice_fusion.refs_0_), channel_id=1, source_target_pairs={{0,32},{1,33},{2,34},{3,35},{4,12},{5,13},{6,14},{7,15},{8,40},{9,... | collective-permute-start | bytes 1572872 | tf_op jit(solution)/shard_map/ppermute | solution.py:84
  15.1 17.8 %collective-permute-start.7 = (bf16[32,8192]{1,0:T(8,128)(2,1)S(1)}, bf16[32,8192]{1,0:T(8,128)(2,1)S(1)}, u32[]{:S(2)}, u32[]{:S(2)}) collective-permute-start(bf16[32,8192]{1,0:T(8,128)(2,1)S(1)} %constant_dynamic-update-slice_fusion.refs_0_), channel_id=1, source_target_pairs={{0,64},{1,65},{2,66},{3,67},{4,20},{5,21},{6,22},{7,23},{8,72},{9,... | collective-permute-start | bytes 1572872 | tf_op jit(solution)/shard_map/ppermute | solution.py:84
  18.7 14.3 %collective-permute-start.8 = (bf16[32,8192]{1,0:T(8,128)(2,1)S(1)}, bf16[32,8192]{1,0:T(8,128)(2,1)S(1)}, u32[]{:S(2)}, u32[]{:S(2)}) collective-permute-start(bf16[32,8192]{1,0:T(8,128)(2,1)S(1)} %constant_dynamic-update-slice_fusion.refs_0_), channel_id=1, source_target_pairs={{0,96},{1,97},{2,98},{3,99},{4,28},{5,29},{6,30},{7,31},{8,104},{9... | collective-permute-start | bytes 1572872 | tf_op jit(solution)/shard_map/ppermute | solution.py:84
  20.7 5.5 %collective-permute-start.3 = (bf16[16,2048]{1,0:T(8,128)(2,1)S(1)}, bf16[16,2048]{1,0:T(8,128)(2,1)S(1)}, u32[]{:S(2)}, u32[]{:S(2)}) collective-permute-start(bf16[16,2048]{1,0:T(8,128)(2,1)S(1)} %bitcast.79), channel_id=1, source_target_pairs={{0,1},{1,2},{2,3},{3,0},{4,5},{5,6},{6,7},{7,4},{8,9},{9,10},{10,1... | collective-permute-start | bytes 196616 | tf_op jit(solution)/shard_map/ppermute | solution.py:84
  22.3 5.8 %collective-permute-start.4 = (bf16[16,2048]{1,0:T(8,128)(2,1)S(1)}, bf16[16,2048]{1,0:T(8,128)(2,1)S(1)}, u32[]{:S(2)}, u32[]{:S(2)}) collective-permute-start(bf16[16,2048]{1,0:T(8,128)(2,1)S(1)} %bitcast.80), channel_id=1, source_target_pairs={{0,2},{1,3},{2,0},{3,1},{4,6},{5,7},{6,4},{7,5},{8,10},{9,11},{10,... | collective-permute-start | bytes 196616 | tf_op jit(solution)/shard_map/ppermute | solution.py:84
  26.2 4.3 %collective-permute-start.5 = (bf16[16,2048]{1,0:T(8,128)(2,1)S(1)}, bf16[16,2048]{1,0:T(8,128)(2,1)S(1)}, u32[]{:S(2)}, u32[]{:S(2)}) collective-permute-start(bf16[16,2048]{1,0:T(8,128)(2,1)S(1)} %bitcast.81), channel_id=1, source_target_pairs={{0,3},{1,0},{2,1},{3,2},{4,7},{5,4},{6,5},{7,6},{8,11},{9,8},{10,9... | collective-permute-start | bytes 196616 | tf_op jit(solution)/shard_map/ppermute | solution.py:84
  28.1 14.8 %collective-permute-start.15 = (bf16[32,8192]{1,0:T(8,128)(2,1)S(1)}, bf16[32,8192]{1,0:T(8,128)(2,1)S(1)}, u32[]{:S(2)}, u32[]{:S(2)}) collective-permute-start(bf16[32,8192]{1,0:T(8,128)(2,1)S(1)} %constant_dynamic-update-slice_fusion.refs_0_), channel_id=1, source_target_pairs={{0,4},{1,5},{2,6},{3,7},{4,0},{5,1},{6,2},{7,3},{8,12},{9,13},{10,... | collective-permute-start | bytes 1572872 | tf_op jit(solution)/shard_map/ppermute | solution.py:84
  33.0 6.2 %collective-permute-start.9 = (bf16[8,8192]{1,0:T(8,128)(2,1)S(1)}, bf16[8,8192]{1,0:T(8,128)(2,1)S(1)}, u32[]{:S(2)}, u32[]{:S(2)}) collective-permute-start(bf16[8,8192]{1,0:T(8,128)(2,1)S(1)} %get-tuple-element.62), channel_id=1, source_target_pairs={{0,8},{1,9},{2,10},{3,11},{4,36},{5,37},{6,38},{7,39},{8,16},{9,17... | collective-permute-start | bytes 393224 | tf_op jit(solution)/shard_map/ppermute | solution.py:84
  34.3 7.2 %collective-permute-start.10 = (bf16[8,8192]{1,0:T(8,128)(2,1)S(1)}, bf16[8,8192]{1,0:T(8,128)(2,1)S(1)}, u32[]{:S(2)}, u32[]{:S(2)}) collective-permute-start(bf16[8,8192]{1,0:T(8,128)(2,1)S(1)} %get-tuple-element.62), channel_id=1, source_target_pairs={{0,16},{1,17},{2,18},{3,19},{4,68},{5,69},{6,70},{7,71},{8,24},{9,... | collective-permute-start | bytes 393224 | tf_op jit(solution)/shard_map/ppermute | solution.py:84
  37.3 5.0 %collective-permute-start.11 = (bf16[8,8192]{1,0:T(8,128)(2,1)S(1)}, bf16[8,8192]{1,0:T(8,128)(2,1)S(1)}, u32[]{:S(2)}, u32[]{:S(2)}) collective-permute-start(bf16[8,8192]{1,0:T(8,128)(2,1)S(1)} %get-tuple-element.62), channel_id=1, source_target_pairs={{0,24},{1,25},{2,26},{3,27},{4,100},{5,101},{6,102},{7,103},{8,0},... | collective-permute-start | bytes 393224 | tf_op jit(solution)/shard_map/ppermute | solution.py:84
  38.1 6.2 %collective-permute-start.16 = (bf16[32,8192]{1,0:T(8,128)(2,1)S(1)}, bf16[32,8192]{1,0:T(8,128)(2,1)S(1)}, u32[]{:S(2)}, u32[]{:S(2)}) collective-permute-start(bf16[32,8192]{1,0:T(8,128)(2,1)S(1)} %collective-permute-done.6.refs_1_), channel_id=1, source_target_pairs={{0,4},{1,5},{2,6},{3,7},{4,0},{5,1},{6,2},{7,3},{8,12},{9,13},{10,... | collective-permute-start | bytes 1572872 | tf_op jit(solution)/shard_map/ppermute | solution.py:84
  39.2 10.0 %collective-permute-start.17 = (bf16[32,8192]{1,0:T(8,128)(2,1)S(1)}, bf16[32,8192]{1,0:T(8,128)(2,1)S(1)}, u32[]{:S(2)}, u32[]{:S(2)}) collective-permute-start(bf16[32,8192]{1,0:T(8,128)(2,1)S(1)} %collective-permute-done.7.refs_2_), channel_id=1, source_target_pairs={{0,4},{1,5},{2,6},{3,7},{4,0},{5,1},{6,2},{7,3},{8,12},{9,13},{10,... | collective-permute-start | bytes 1572872 | tf_op jit(solution)/shard_map/ppermute | solution.py:84
  41.5 7.9 %collective-permute-start.18 = (bf16[32,8192]{1,0:T(8,128)(2,1)S(1)}, bf16[32,8192]{1,0:T(8,128)(2,1)S(1)}, u32[]{:S(2)}, u32[]{:S(2)}) collective-permute-start(bf16[32,8192]{1,0:T(8,128)(2,1)S(1)} %collective-permute-done.8.refs_3_), channel_id=1, source_target_pairs={{0,4},{1,5},{2,6},{3,7},{4,0},{5,1},{6,2},{7,3},{8,12},{9,13},{10,... | collective-permute-start | bytes 1572872 | tf_op jit(solution)/shard_map/ppermute | solution.py:84
  42.2 6.4 %slice-start = ((s8[5636096]{0:T(1024)(128)(4,1)}), s8[4194304]{0:T(1024)(128)(4,1)S(1)}, s32[]{:S(2)}) async-start(s8[5636096]{0:T(1024)(128)(4,1)} %bitcast.75), calls=%async_computation | async-start | bytes 8388608
  42.3 9.8 %collective-permute-start.14 = (bf16[32,8192]{1,0:T(8,128)(2,1)S(1)}, bf16[32,8192]{1,0:T(8,128)(2,1)S(1)}, u32[]{:S(2)}, u32[]{:S(2)}) collective-permute-start(bf16[32,8192]{1,0:T(8,128)(2,1)S(1)} %constant_dynamic-update-slice_fusion.4.refs_0_), channel_id=1, source_target_pairs={{0,96},{1,97},{2,98},{3,99},{4,28},{5,29},{6,30},{7,31},{8,104},{9... | collective-permute-start | bytes 1572872 | tf_op jit(solution)/shard_map/ppermute | solution.py:84
  42.9 16.0 %collective-permute-start.12 = (bf16[32,8192]{1,0:T(8,128)(2,1)S(1)}, bf16[32,8192]{1,0:T(8,128)(2,1)S(1)}, u32[]{:S(2)}, u32[]{:S(2)}) collective-permute-start(bf16[32,8192]{1,0:T(8,128)(2,1)S(1)} %constant_dynamic-update-slice_fusion.4.refs_0_), channel_id=1, source_target_pairs={{0,32},{1,33},{2,34},{3,35},{4,12},{5,13},{6,14},{7,15},{8,40},{9,... | collective-permute-start | bytes 1572872 | tf_op jit(solution)/shard_map/ppermute | solution.py:84
  44.4 14.6 %collective-permute-start.13 = (bf16[32,8192]{1,0:T(8,128)(2,1)S(1)}, bf16[32,8192]{1,0:T(8,128)(2,1)S(1)}, u32[]{:S(2)}, u32[]{:S(2)}) collective-permute-start(bf16[32,8192]{1,0:T(8,128)(2,1)S(1)} %constant_dynamic-update-slice_fusion.4.refs_0_), channel_id=1, source_target_pairs={{0,64},{1,65},{2,66},{3,67},{4,20},{5,21},{6,22},{7,23},{8,72},{9,... | collective-permute-start | bytes 1572872 | tf_op jit(solution)/shard_map/ppermute | solution.py:84
  49.3 10.2 %collective-permute-start.19 = (bf16[32,8192]{1,0:T(8,128)(2,1)S(1)}, bf16[32,8192]{1,0:T(8,128)(2,1)S(1)}, u32[]{:S(2)}, u32[]{:S(2)}) collective-permute-start(bf16[32,8192]{1,0:T(8,128)(2,1)S(1)} %constant_dynamic-update-slice_fusion.4.refs_0_), channel_id=1, source_target_pairs={{0,4},{1,5},{2,6},{3,7},{4,0},{5,1},{6,2},{7,3},{8,12},{9,13},{10,... | collective-permute-start | bytes 1572872 | tf_op jit(solution)/shard_map/ppermute | solution.py:84
  52.1 7.4 %collective-permute-start.22 = (bf16[32,8192]{1,0:T(8,128)(2,1)S(1)}, bf16[32,8192]{1,0:T(8,128)(2,1)S(1)}, u32[]{:S(2)}, u32[]{:S(2)}) collective-permute-start(bf16[32,8192]{1,0:T(8,128)(2,1)S(1)} %collective-permute-done.14.refs_3_), channel_id=1, source_target_pairs={{0,4},{1,5},{2,6},{3,7},{4,0},{5,1},{6,2},{7,3},{8,12},{9,13},{10,... | collective-permute-start | bytes 1572872 | tf_op jit(solution)/shard_map/ppermute | solution.py:84
  58.9 1.9 %collective-permute-start.20 = (bf16[32,8192]{1,0:T(8,128)(2,1)S(1)}, bf16[32,8192]{1,0:T(8,128)(2,1)S(1)}, u32[]{:S(2)}, u32[]{:S(2)}) collective-permute-start(bf16[32,8192]{1,0:T(8,128)(2,1)S(1)} %collective-permute-done.12.refs_1_), channel_id=1, source_target_pairs={{0,4},{1,5},{2,6},{3,7},{4,0},{5,1},{6,2},{7,3},{8,12},{9,13},{10,... | collective-permute-start | bytes 1572872 | tf_op jit(solution)/shard_map/ppermute | solution.py:84
  58.9 2.7 %collective-permute-start.21 = (bf16[32,8192]{1,0:T(8,128)(2,1)S(1)}, bf16[32,8192]{1,0:T(8,128)(2,1)S(1)}, u32[]{:S(2)}, u32[]{:S(2)}) collective-permute-start(bf16[32,8192]{1,0:T(8,128)(2,1)S(1)} %collective-permute-done.13.refs_2_), channel_id=1, source_target_pairs={{0,4},{1,5},{2,6},{3,7},{4,0},{5,1},{6,2},{7,3},{8,12},{9,13},{10,... | collective-permute-start | bytes 1572872 | tf_op jit(solution)/shard_map/ppermute | solution.py:84
  67.5 4.2 %collective-permute-start.23 = (bf16[128,8192]{1,0:T(8,128)(2,1)S(1)}, bf16[128,8192]{1,0:T(8,128)(2,1)S(1)}, u32[]{:S(2)}, u32[]{:S(2)}) collective-permute-start(bf16[128,8192]{1,0:T(8,128)(2,1)S(1)} %get-tuple-element.66), channel_id=1, source_target_pairs={{0,4},{1,5},{2,6},{3,7},{4,0},{5,1},{6,2},{7,3},{8,12},{9,13},{10,... | collective-permute-start | bytes 6291464 | tf_op jit(solution)/shard_map/ppermute | solution.py:84
  69.7 8.0 %collective-permute-start.24 = (bf16[128,8192]{1,0:T(8,128)(2,1)S(1)}, bf16[128,8192]{1,0:T(8,128)(2,1)S(1)}, u32[]{:S(2)}, u32[]{:S(2)}) collective-permute-start(bf16[128,8192]{1,0:T(8,128)(2,1)S(1)} %shard_map.167), channel_id=1, source_target_pairs={{0,4},{1,5},{2,6},{3,7},{4,0},{5,1},{6,2},{7,3},{8,12},{9,13},{10,... | collective-permute-start | bytes 6291464 | tf_op jit(solution)/shard_map/ppermute | solution.py:84
  75.2 9.6 %collective-permute-start.25 = (bf16[32,8704]{1,0:T(8,128)(2,1)S(1)}, bf16[32,8704]{1,0:T(8,128)(2,1)S(1)}, u32[]{:S(2)}, u32[]{:S(2)}) collective-permute-start(bf16[32,8704]{1,0:T(8,128)(2,1)S(1)} %get-tuple-element.72), channel_id=1, source_target_pairs={{0,96},{1,97},{2,98},{3,99},{4,28},{5,29},{6,30},{7,31},{8,104},{9... | collective-permute-start | bytes 1671176 | tf_op jit(solution)/shard_map/ppermute | solution.py:84
  75.3 13.2 %collective-permute-start.26 = (bf16[32,8704]{1,0:T(8,128)(2,1)S(1)}, bf16[32,8704]{1,0:T(8,128)(2,1)S(1)}, u32[]{:S(2)}, u32[]{:S(2)}) collective-permute-start(bf16[32,8704]{1,0:T(8,128)(2,1)S(1)} %get-tuple-element.76), channel_id=1, source_target_pairs={{0,64},{1,65},{2,66},{3,67},{4,20},{5,21},{6,22},{7,23},{8,72},{9,... | collective-permute-start | bytes 1671176 | tf_op jit(solution)/shard_map/ppermute | solution.py:84
  77.2 15.1 %collective-permute-start.27 = (bf16[32,8704]{1,0:T(8,128)(2,1)S(1)}, bf16[32,8704]{1,0:T(8,128)(2,1)S(1)}, u32[]{:S(2)}, u32[]{:S(2)}) collective-permute-start(bf16[32,8704]{1,0:T(8,128)(2,1)S(1)} %get-tuple-element.77), channel_id=1, source_target_pairs={{0,32},{1,33},{2,34},{3,35},{4,12},{5,13},{6,14},{7,15},{8,40},{9,... | collective-permute-start | bytes 1671176 | tf_op jit(solution)/shard_map/ppermute | solution.py:84
  79.0 17.6 %collective-permute-start.29 = (bf16[32,8192]{1,0:T(8,128)(2,1)S(1)}, bf16[32,8192]{1,0:T(8,128)(2,1)S(1)}, u32[]{:S(2)}, u32[]{:S(2)}) collective-permute-start(bf16[32,8192]{1,0:T(8,128)(2,1)S(1)} %get-tuple-element.82), channel_id=1, source_target_pairs={{0,96},{1,97},{2,98},{3,99},{4,28},{5,29},{6,30},{7,31},{8,104},{9... | collective-permute-start | bytes 1572872 | tf_op jit(solution)/shard_map/ppermute | solution.py:84
  81.9 20.9 %collective-permute-start.30 = (bf16[32,8192]{1,0:T(8,128)(2,1)S(1)}, bf16[32,8192]{1,0:T(8,128)(2,1)S(1)}, u32[]{:S(2)}, u32[]{:S(2)}) collective-permute-start(bf16[32,8192]{1,0:T(8,128)(2,1)S(1)} %get-tuple-element.83), channel_id=1, source_target_pairs={{0,64},{1,65},{2,66},{3,67},{4,20},{5,21},{6,22},{7,23},{8,72},{9,... | collective-permute-start | bytes 1572872 | tf_op jit(solution)/shard_map/ppermute | solution.py:84
  84.8 25.1 %collective-permute-start.31 = (bf16[32,8192]{1,0:T(8,128)(2,1)S(1)}, bf16[32,8192]{1,0:T(8,128)(2,1)S(1)}, u32[]{:S(2)}, u32[]{:S(2)}) collective-permute-start(bf16[32,8192]{1,0:T(8,128)(2,1)S(1)} %get-tuple-element.84), channel_id=1, source_target_pairs={{0,32},{1,33},{2,34},{3,35},{4,12},{5,13},{6,14},{7,15},{8,40},{9,... | collective-permute-start | bytes 1572872 | tf_op jit(solution)/shard_map/ppermute | solution.py:84
  92.6 17.3 %collective-permute-start.28 = (f32[8,9216]{1,0:T(8,128)S(1)}, f32[8,9216]{1,0:T(8,128)S(1)}, u32[]{:S(2)}, u32[]{:S(2)}) collective-permute-start(f32[8,9216]{1,0:T(8,128)S(1)} %get-tuple-element.79), channel_id=1, source_target_pairs={{0,24},{1,25},{2,26},{3,27},{4,100},{5,101},{6,102},{7,103},{8,0},... | collective-permute-start | bytes 884744 | tf_op jit(solution)/shard_map/ppermute | solution.py:84
  94.7 15.2 %collective-permute-start.32 = (f32[8,9216]{1,0:T(8,128)S(1)}, f32[8,9216]{1,0:T(8,128)S(1)}, u32[]{:S(2)}, u32[]{:S(2)}) collective-permute-start(f32[8,9216]{1,0:T(8,128)S(1)} %get-tuple-element.86), channel_id=1, source_target_pairs={{0,16},{1,17},{2,18},{3,19},{4,68},{5,69},{6,70},{7,71},{8,24},{9,... | collective-permute-start | bytes 884744 | tf_op jit(solution)/shard_map/ppermute | solution.py:84
  96.6 13.6 %collective-permute-start.33 = (f32[8,9216]{1,0:T(8,128)S(1)}, f32[8,9216]{1,0:T(8,128)S(1)}, u32[]{:S(2)}, u32[]{:S(2)}) collective-permute-start(f32[8,9216]{1,0:T(8,128)S(1)} %get-tuple-element.87), channel_id=1, source_target_pairs={{0,8},{1,9},{2,10},{3,11},{4,36},{5,37},{6,38},{7,39},{8,16},{9,17... | collective-permute-start | bytes 884744 | tf_op jit(solution)/shard_map/ppermute | solution.py:84
  102.8 20.0 %copy-start.2 = (f32[3,8192]{1,0:T(4,128)S(1)}, f32[3,8192]{1,0:T(4,128)}, u32[]{:S(2)}) copy-start(f32[3,8192]{1,0:T(4,128)} %gains_ref.1) | copy-start | bytes 294916
  102.8 20.0 %copy-start.4 = (bf16[1,16,8192]{2,1,0:T(8,128)(2,1)S(1)}, bf16[1,16,8192]{2,1,0:T(8,128)(2,1)}, u32[]{:S(2)}) copy-start(bf16[1,16,8192]{2,1,0:T(8,128)(2,1)} %param.19) | copy-start | bytes 786436
  102.8 20.0 %copy-start.7 = (s32[4]{0:T(128)S(1)}, s32[4]{0:T(128)}, u32[]{:S(2)}) copy-start(s32[4]{0:T(128)} %kinds_ref.3) | copy-start | bytes 52
  110.2 9.8 %collective-permute-start.35 = (bf16[8,10240]{1,0:T(8,128)(2,1)S(1)}, bf16[8,10240]{1,0:T(8,128)(2,1)S(1)}, u32[]{:S(2)}, u32[]{:S(2)}) collective-permute-start(bf16[8,10240]{1,0:T(8,128)(2,1)S(1)} %shard_map.173.refs_0_), channel_id=1, source_target_pairs={{0,1},{1,2},{2,3},{3,0},{4,5},{5,6},{6,7},{7,4},{8,9},{9,10},{10,1... | collective-permute-start | bytes 491528 | tf_op jit(solution)/shard_map/ppermute | solution.py:84
  112.3 10.5 %collective-permute-start.36 = (bf16[8,10240]{1,0:T(8,128)(2,1)S(1)}, bf16[8,10240]{1,0:T(8,128)(2,1)S(1)}, u32[]{:S(2)}, u32[]{:S(2)}) collective-permute-start(bf16[8,10240]{1,0:T(8,128)(2,1)S(1)} %shard_map.173.refs_0_), channel_id=1, source_target_pairs={{0,2},{1,3},{2,0},{3,1},{4,6},{5,7},{6,4},{7,5},{8,10},{9,11},{10,... | collective-permute-start | bytes 491528 | tf_op jit(solution)/shard_map/ppermute | solution.py:84
  114.7 8.1 %collective-permute-start.37 = (bf16[8,10240]{1,0:T(8,128)(2,1)S(1)}, bf16[8,10240]{1,0:T(8,128)(2,1)S(1)}, u32[]{:S(2)}, u32[]{:S(2)}) collective-permute-start(bf16[8,10240]{1,0:T(8,128)(2,1)S(1)} %shard_map.173.refs_0_), channel_id=1, source_target_pairs={{0,3},{1,0},{2,1},{3,2},{4,7},{5,4},{6,5},{7,6},{8,11},{9,8},{10,9... | collective-permute-start | bytes 491528 | tf_op jit(solution)/shard_map/ppermute | solution.py:84
  116.8 8.1 %collective-permute-start.34 = (bf16[8,8192]{1,0:T(8,128)(2,1)S(1)}, bf16[8,8192]{1,0:T(8,128)(2,1)S(1)}, u32[]{:S(2)}, u32[]{:S(2)}) collective-permute-start(bf16[8,8192]{1,0:T(8,128)(2,1)S(1)} %get-tuple-element.102), channel_id=1, source_target_pairs={{0,24},{1,25},{2,26},{3,27},{4,100},{5,101},{6,102},{7,103},{8,0},... | collective-permute-start | bytes 393224 | tf_op jit(solution)/shard_map/ppermute | solution.py:84
  118.7 6.5 %collective-permute-start.38 = (bf16[8,8192]{1,0:T(8,128)(2,1)S(1)}, bf16[8,8192]{1,0:T(8,128)(2,1)S(1)}, u32[]{:S(2)}, u32[]{:S(2)}) collective-permute-start(bf16[8,8192]{1,0:T(8,128)(2,1)S(1)} %get-tuple-element.101), channel_id=1, source_target_pairs={{0,16},{1,17},{2,18},{3,19},{4,68},{5,69},{6,70},{7,71},{8,24},{9,... | collective-permute-start | bytes 393224 | tf_op jit(solution)/shard_map/ppermute | solution.py:84
  120.0 6.5 %collective-permute-start.39 = (bf16[8,8192]{1,0:T(8,128)(2,1)S(1)}, bf16[8,8192]{1,0:T(8,128)(2,1)S(1)}, u32[]{:S(2)}, u32[]{:S(2)}) collective-permute-start(bf16[8,8192]{1,0:T(8,128)(2,1)S(1)} %get-tuple-element.100), channel_id=1, source_target_pairs={{0,8},{1,9},{2,10},{3,11},{4,36},{5,37},{6,38},{7,39},{8,16},{9,17... | collective-permute-start | bytes 393224 | tf_op jit(solution)/shard_map/ppermute | solution.py:84
  124.9 13.0 %collective-permute-start.43 = (f32[24,1024]{1,0:T(8,128)S(1)}, f32[24,1024]{1,0:T(8,128)S(1)}, u32[]{:S(2)}, u32[]{:S(2)}) collective-permute-start(f32[24,1024]{1,0:T(8,128)S(1)} %get-tuple-element.97), channel_id=1, source_target_pairs={{0,4},{1,5},{2,6},{3,7},{4,0},{5,1},{6,2},{7,3},{8,12},{9,13},{10,... | collective-permute-start | bytes 294920 | tf_op jit(solution)/shard_map/ppermute | solution.py:84
  130.1 6.6 %collective-permute-start.40 = (bf16[4,8192]{1,0:T(4,128)(2,1)S(1)}, bf16[4,8192]{1,0:T(4,128)(2,1)S(1)}, u32[]{:S(2)}, u32[]{:S(2)}) collective-permute-start(bf16[4,8192]{1,0:T(4,128)(2,1)S(1)} %get-tuple-element.92), channel_id=1, source_target_pairs={{0,1},{1,2},{2,3},{3,0},{4,5},{5,6},{6,7},{7,4},{8,9},{9,10},{10,1... | collective-permute-start | bytes 196616 | tf_op jit(solution)/shard_map/ppermute | solution.py:84
  130.2 6.5 %collective-permute-start.41 = (bf16[4,8192]{1,0:T(4,128)(2,1)S(1)}, bf16[4,8192]{1,0:T(4,128)(2,1)S(1)}, u32[]{:S(2)}, u32[]{:S(2)}) collective-permute-start(bf16[4,8192]{1,0:T(4,128)(2,1)S(1)} %get-tuple-element.93), channel_id=1, source_target_pairs={{0,2},{1,3},{2,0},{3,1},{4,6},{5,7},{6,4},{7,5},{8,10},{9,11},{10,... | collective-permute-start | bytes 196616 | tf_op jit(solution)/shard_map/ppermute | solution.py:84
  132.2 5.0 %collective-permute-start.42 = (bf16[4,8192]{1,0:T(4,128)(2,1)S(1)}, bf16[4,8192]{1,0:T(4,128)(2,1)S(1)}, u32[]{:S(2)}, u32[]{:S(2)}) collective-permute-start(bf16[4,8192]{1,0:T(4,128)(2,1)S(1)} %get-tuple-element.94), channel_id=1, source_target_pairs={{0,3},{1,0},{2,1},{3,2},{4,7},{5,4},{6,5},{7,6},{8,11},{9,8},{10,9... | collective-permute-start | bytes 196616 | tf_op jit(solution)/shard_map/ppermute | solution.py:84
  (8 other events, 13.8 us)

commit v5 on v4

--- a/solution.py
+++ b/solution.py
@@ -17,7 +17,7 @@
 BF = jnp.bfloat16
 F32 = jnp.float32
 CAP = 8
-VMEM = 26 * 1024 * 1024
+VMEM = 20 * 1024 * 1024
 
 
 def causal_forward(queries, keys, values):
@@ -139,6 +139,7 @@
 
 
 RAW = pl.BlockSpec(memory_space=pl.ANY)
+FAR = pl.BlockSpec(memory_space=pltpu.HBM)
 HELD = pl.BlockSpec(memory_space=pltpu.VMEM)
 
 
@@ -174,7 +175,7 @@
     ]
     return pl.pallas_call(
         _pack_kernel,
-        in_specs=[SMALL, RAW, RAW, RAW],
+        in_specs=[SMALL, FAR, FAR, FAR],
         out_specs=[HELD] * 3,
         out_shape=outs,
         scratch_shapes=[
@@ -220,7 +221,7 @@
     outs = [jax.ShapeDtypeStruct((length, width), BF), jax.ShapeDtypeStruct((CAP, width), BF)]
     return pl.pallas_call(
         _norm_kernel,
-        in_specs=[SMALL, HELD, HELD, RAW, RAW] + [HELD] * NS,
+        in_specs=[SMALL, HELD, HELD, FAR, FAR] + [HELD] * NS,
         out_specs=[HELD, HELD],
         out_shape=outs,
         scratch_shapes=[

time: 139 us -> 139 us (level)
  no operation moved by 1% of the time
where the time goes in v5:
time: 139 us
  starting transfers between devices  54.3 us (39%)
  waiting for transfers between devices  38.5 us (28%)
  Pallas kernels  28.9 us (21%)
  local copies, waits for them, and re-layouts  11.3 us (8%)
  matrix products  2.93 us (2%)
  other arithmetic  1.82 us (1%)
    ppermute x44, starting transfers between devices, send(): return lax.ppermute(block, AXES, pairs)  54.3 us
    ppermute x44, waiting for transfers between devices, send(): return lax.ppermute(block, AXES, pairs)  38.5 us
    unnamed x36, local copies, waits for them, and re-layouts  9.88 us
    pallas_call x2, Pallas kernels, weight_grad(): pl.pallas_call(_down_kernel, grid=(width // tile,), in_specs=[pl.BlockSpe...  7.5 us
    pallas_call x1, Pallas kernels, pre_product(): pl.pallas_call(_pre_kernel, in_specs=[RAW] * 8 + [HELD, HELD], out_specs=...  5.86 us
    pallas_call x2, Pallas kernels, own_product(): pl.pallas_call(functools.partial(_own_kernel, len(rows)), in_specs=[HELD,...  4.82 us
  transfers between devices with their start and end apart: 44, of which 22 were waited for; matrix products, arithmetic and copies ran while one was open for 6% of the time, Pallas kernels for 16%

profile of v5, /device:TPU:0, one launch (start us, length us, event | category | flops | bytes accessed | tf_op | source)
XLA Modules:
  0.0 138.7 jit_solution(14742664827793225392)
XLA Ops:
  3.8 1.6 %collective-permute-start = (bf16[8,8192]{1,0:T(8,128)(2,1)S(1)}, bf16[8,8192]{1,0:T(8,128)(2,1)S(1)}, u32[]{:S(2)}, u32[]{:S(2)}) collective-permute-start(bf16[8,8192]{1,0:T(8,128)(2,1)S(1)} %get-tuple-element.54), channel_id=1, source_target_pairs={{0,8},{1,9},{2,10},{3,11},{4,36},{5,37},{6,38},{7,39},{8,16},{9,17... | collective-permute-start | bytes 393224 | tf_op jit(solution)/shard_map/ppermute | solution.py:84
  5.4 2.7 %collective-permute-start.1 = (bf16[8,8192]{1,0:T(8,128)(2,1)S(1)}, bf16[8,8192]{1,0:T(8,128)(2,1)S(1)}, u32[]{:S(2)}, u32[]{:S(2)}) collective-permute-start(bf16[8,8192]{1,0:T(8,128)(2,1)S(1)} %get-tuple-element.54), channel_id=1, source_target_pairs={{0,16},{1,17},{2,18},{3,19},{4,68},{5,69},{6,70},{7,71},{8,24},{9,... | collective-permute-start | bytes 393224 | tf_op jit(solution)/shard_map/ppermute | solution.py:84
  8.2 1.4 %collective-permute-start.2 = (bf16[8,8192]{1,0:T(8,128)(2,1)S(1)}, bf16[8,8192]{1,0:T(8,128)(2,1)S(1)}, u32[]{:S(2)}, u32[]{:S(2)}) collective-permute-start(bf16[8,8192]{1,0:T(8,128)(2,1)S(1)} %get-tuple-element.54), channel_id=1, source_target_pairs={{0,24},{1,25},{2,26},{3,27},{4,100},{5,101},{6,102},{7,103},{8,0},... | collective-permute-start | bytes 393224 | tf_op jit(solution)/shard_map/ppermute | solution.py:84
  13.2 2.0 %collective-permute-start.6 = (bf16[32,8192]{1,0:T(8,128)(2,1)S(1)}, bf16[32,8192]{1,0:T(8,128)(2,1)S(1)}, u32[]{:S(2)}, u32[]{:S(2)}) collective-permute-start(bf16[32,8192]{1,0:T(8,128)(2,1)S(1)} %constant_dynamic-update-slice_fusion.refs_0_), channel_id=1, source_target_pairs={{0,32},{1,33},{2,34},{3,35},{4,12},{5,13},{6,14},{7,15},{8,40},{9,... | collective-permute-start | bytes 1572872 | tf_op jit(solution)/shard_map/ppermute | solution.py:84
  15.1 3.6 %collective-permute-start.7 = (bf16[32,8192]{1,0:T(8,128)(2,1)S(1)}, bf16[32,8192]{1,0:T(8,128)(2,1)S(1)}, u32[]{:S(2)}, u32[]{:S(2)}) collective-permute-start(bf16[32,8192]{1,0:T(8,128)(2,1)S(1)} %constant_dynamic-update-slice_fusion.refs_0_), channel_id=1, source_target_pairs={{0,64},{1,65},{2,66},{3,67},{4,20},{5,21},{6,22},{7,23},{8,72},{9,... | collective-permute-start | bytes 1572872 | tf_op jit(solution)/shard_map/ppermute | solution.py:84
  20.7 1.6 %collective-permute-start.3 = (bf16[16,2048]{1,0:T(8,128)(2,1)S(1)}, bf16[16,2048]{1,0:T(8,128)(2,1)S(1)}, u32[]{:S(2)}, u32[]{:S(2)}) collective-permute-start(bf16[16,2048]{1,0:T(8,128)(2,1)S(1)} %bitcast.79), channel_id=1, source_target_pairs={{0,1},{1,2},{2,3},{3,0},{4,5},{5,6},{6,7},{7,4},{8,9},{9,10},{10,1... | collective-permute-start | bytes 196616 | tf_op jit(solution)/shard_map/ppermute | solution.py:84
  22.3 2.9 %collective-permute-start.4 = (bf16[16,2048]{1,0:T(8,128)(2,1)S(1)}, bf16[16,2048]{1,0:T(8,128)(2,1)S(1)}, u32[]{:S(2)}, u32[]{:S(2)}) collective-permute-start(bf16[16,2048]{1,0:T(8,128)(2,1)S(1)} %bitcast.80), channel_id=1, source_target_pairs={{0,2},{1,3},{2,0},{3,1},{4,6},{5,7},{6,4},{7,5},{8,10},{9,11},{10,... | collective-permute-start | bytes 196616 | tf_op jit(solution)/shard_map/ppermute | solution.py:84
  26.2 1.8 %collective-permute-start.5 = (bf16[16,2048]{1,0:T(8,128)(2,1)S(1)}, bf16[16,2048]{1,0:T(8,128)(2,1)S(1)}, u32[]{:S(2)}, u32[]{:S(2)}) collective-permute-start(bf16[16,2048]{1,0:T(8,128)(2,1)S(1)} %bitcast.81), channel_id=1, source_target_pairs={{0,3},{1,0},{2,1},{3,2},{4,7},{5,4},{6,5},{7,6},{8,11},{9,8},{10,9... | collective-permute-start | bytes 196616 | tf_op jit(solution)/shard_map/ppermute | solution.py:84
  28.1 2.3 %collective-permute-done.5.refs_3_ = bf16[16,2048]{1,0:T(8,128)(2,1)S(1)} collective-permute-done((bf16[16,2048]{1,0:T(8,128)(2,1)S(1)}, bf16[16,2048]{1,0:T(8,128)(2,1)S(1)}, u32[]{:S(2)}, u32[]{:S(2)}) %collective-permute-start.5) | collective-permute-done | bytes 65568 | tf_op jit(solution)/shard_map/ppermute | solution.py:84
  33.0 1.3 collective-permute-start.9
  34.3 2.9 %collective-permute-start.10 = (bf16[8,8192]{1,0:T(8,128)(2,1)S(1)}, bf16[8,8192]{1,0:T(8,128)(2,1)S(1)}, u32[]{:S(2)}, u32[]{:S(2)}) collective-permute-start(bf16[8,8192]{1,0:T(8,128)(2,1)S(1)} %get-tuple-element.62), channel_id=1, source_target_pairs={{0,16},{1,17},{2,18},{3,19},{4,68},{5,69},{6,70},{7,71},{8,24},{9,... | collective-permute-start | bytes 393224 | tf_op jit(solution)/shard_map/ppermute | solution.py:84
  38.1 1.1 collective-permute-done.9
  39.3 2.3 %collective-permute-done.10 = bf16[8,8192]{1,0:T(8,128)(2,1)S(1)} collective-permute-done((bf16[8,8192]{1,0:T(8,128)(2,1)S(1)}, bf16[8,8192]{1,0:T(8,128)(2,1)S(1)}, u32[]{:S(2)}, u32[]{:S(2)}) %collective-permute-start.10) | collective-permute-done | bytes 131104 | tf_op jit(solution)/shard_map/ppermute | solution.py:84
  42.9 1.4 %collective-permute-start.12 = (bf16[32,8192]{1,0:T(8,128)(2,1)S(1)}, bf16[32,8192]{1,0:T(8,128)(2,1)S(1)}, u32[]{:S(2)}, u32[]{:S(2)}) collective-permute-start(bf16[32,8192]{1,0:T(8,128)(2,1)S(1)} %constant_dynamic-update-slice_fusion.4.refs_0_), channel_id=1, source_target_pairs={{0,32},{1,33},{2,34},{3,35},{4,12},{5,13},{6,14},{7,15},{8,40},{9,... | collective-permute-start | bytes 1572872 | tf_op jit(solution)/shard_map/ppermute | solution.py:84
  44.4 1.1 collective-permute-start.13
  45.5 2.6 %copy-done = bf16[1,344,8192]{2,1,0:T(8,128)(2,1)S(1)} copy-done((bf16[1,344,8192]{2,1,0:T(8,128)(2,1)S(1)}, bf16[1,344,8192]{2,1,0:T(8,128)(2,1)}, u32[]{:S(2)}) %copy-start) | copy-done | bytes 5636120
  49.4 2.6 %shard_map.163.refs_9_ = f32[344,256]{1,0:T(8,128)S(1)} custom-call(bf16[32,8192]{1,0:T(8,128)(2,1)S(1)} %constant_dynamic-update-slice_fusion.refs_0_, bf16[32,8192]{1,0:T(8,128)(2,1)S(1)} %collective-permute-done.6.refs_1_, bf16[32,8192]{1,0:T(8,128)(2,1)S(1)} %collective-permute-done.7.refs_2_, bf16[32,8192]{1,0:T(8,128)(2,1)S(1)} %collective-permute-done.8.refs_3_, ...), custom_call_target="tpu_custom_call" | custom-call | flops 1000 | bytes 1000 | tf_op jit(solution)/shard_map/pallas_call | solution.py:328
  52.6 6.4 %collective-permute-done.12.refs_1_ = bf16[32,8192]{1,0:T(8,128)(2,1)S(1)} collective-permute-done((bf16[32,8192]{1,0:T(8,128)(2,1)S(1)}, bf16[32,8192]{1,0:T(8,128)(2,1)S(1)}, u32[]{:S(2)}, u32[]{:S(2)}) %collective-permute-start.12) | collective-permute-done | bytes 524320 | tf_op jit(solution)/shard_map/ppermute | solution.py:84
  59.5 1.4 %collective-permute-done.20.refs_5_ = bf16[32,8192]{1,0:T(8,128)(2,1)S(1)} collective-permute-done((bf16[32,8192]{1,0:T(8,128)(2,1)S(1)}, bf16[32,8192]{1,0:T(8,128)(2,1)S(1)}, u32[]{:S(2)}, u32[]{:S(2)}) %collective-permute-start.20) | collective-permute-done | bytes 524320 | tf_op jit(solution)/shard_map/ppermute | solution.py:84
  61.6 5.9 %shard_map.166 = (bf16[344,256]{1,0:T(8,128)(2,1)S(1)}, bf16[344,256]{1,0:T(8,128)(2,1)S(1)}, bf16[256,344]{1,0:T(8,128)(2,1)S(1)}, bf16[256,344]{1,0:T(8,128)(2,1)S(1)}, bf16[128,8192]{1,0:T(8,128)(2,1)S(1)}) custom-call(bf16[32,8192]{1,0:T(8,128)(2,1)S(1)} %constant_dynamic-update-slice_fusion.4.refs_0_, ...), custom_call_target="tpu_custom_call" | custom-call | flops 1000 | bytes 1000 | tf_op jit(solution)/shard_map/pallas_call | solution.py:404
  67.7 2.0 %shard_map.167 = bf16[128,8192]{1,0:T(8,128)(2,1)S(1)} custom-call(bf16[256,344]{1,0:T(8,128)(2,1)S(1)} %get-tuple-element.70.left_ref, bf16[344,8192]{1,0:T(8,128)(2,1)S(1)} %shard_map.165.w_ref), custom_call_target="tpu_custom_call" | custom-call | flops 1000 | bytes 1000 | tf_op jit(solution)/shard_map/pallas_call | solution.py:438
  70.1 1.6 %collective-permute-done.23.in_ref = bf16[128,8192]{1,0:T(8,128)(2,1)S(1)} collective-permute-done((bf16[128,8192]{1,0:T(8,128)(2,1)S(1)}, bf16[128,8192]{1,0:T(8,128)(2,1)S(1)}, u32[]{:S(2)}, u32[]{:S(2)}) %collective-permute-start.23) | collective-permute-done | bytes 2097184 | tf_op jit(solution)/shard_map/ppermute | solution.py:84
  71.7 3.5 %shard_map.168 = (f32[32,8704]{1,0:T(8,128)S(1)}, bf16[32,8704]{1,0:T(8,128)(2,1)S(1)}, bf16[32,8704]{1,0:T(8,128)(2,1)S(1)}, bf16[32,8704]{1,0:T(8,128)(2,1)S(1)}) custom-call(bf16[256,344]{1,0:T(8,128)(2,1)S(1)} %get-tuple-element.68.left_ref, bf16[344,8192]{1,0:T(8,128)(2,1)S(1)} %shard_map.164.refs_8_.w_ref, ...), custom_call_target="tpu_custom_call" | custom-call | flops 1000 | bytes 1000 | tf_op jit(solution)/shard_map/pallas_call | solution.py:500
  75.3 1.9 %collective-permute-start.26 = (bf16[32,8704]{1,0:T(8,128)(2,1)S(1)}, bf16[32,8704]{1,0:T(8,128)(2,1)S(1)}, u32[]{:S(2)}, u32[]{:S(2)}) collective-permute-start(bf16[32,8704]{1,0:T(8,128)(2,1)S(1)} %get-tuple-element.76), channel_id=1, source_target_pairs={{0,64},{1,65},{2,66},{3,67},{4,20},{5,21},{6,22},{7,23},{8,72},{9,... | collective-permute-start | bytes 1671176 | tf_op jit(solution)/shard_map/ppermute | solution.py:84
  77.6 1.3 shard_map.169
  79.0 2.9 %collective-permute-start.29 = (bf16[32,8192]{1,0:T(8,128)(2,1)S(1)}, bf16[32,8192]{1,0:T(8,128)(2,1)S(1)}, u32[]{:S(2)}, u32[]{:S(2)}) collective-permute-start(bf16[32,8192]{1,0:T(8,128)(2,1)S(1)} %get-tuple-element.82), channel_id=1, source_target_pairs={{0,96},{1,97},{2,98},{3,99},{4,28},{5,29},{6,30},{7,31},{8,104},{9... | collective-permute-start | bytes 1572872 | tf_op jit(solution)/shard_map/ppermute | solution.py:84
  82.9 1.9 %collective-permute-done.25.refs_0_ = bf16[32,8704]{1,0:T(8,128)(2,1)S(1)} collective-permute-done((bf16[32,8704]{1,0:T(8,128)(2,1)S(1)}, bf16[32,8704]{1,0:T(8,128)(2,1)S(1)}, u32[]{:S(2)}, u32[]{:S(2)}) %collective-permute-start.25) | collective-permute-done | bytes 557088 | tf_op jit(solution)/shard_map/ppermute | solution.py:84
  84.8 3.7 %shard_map.170 = bf16[1,344,8192]{2,1,0:T(8,128)(2,1)} custom-call(bf16[32,8192]{1,0:T(8,128)(2,1)S(1)} %constant_dynamic-update-slice_fusion.refs_0_, bf16[32,8192]{1,0:T(8,128)(2,1)S(1)} %collective-permute-done.6.refs_1_, bf16[32,8192]{1,0:T(8,128)(2,1)S(1)} %collective-permute-done.7.refs_2_, bf16[32,8192]{1,0:T(8,128)(2,1)S(1)} %collective-permute-done.8.refs_3_, ...), custom_call_target="tpu_custom_call" | custom-call | flops 1442840576 | bytes 9830400 | tf_op jit(solution)/shard_map/pallas_call | solution.py:622
  88.6 3.8 %collective-permute-done.27.refs_2_ = bf16[32,8704]{1,0:T(8,128)(2,1)S(1)} collective-permute-done((bf16[32,8704]{1,0:T(8,128)(2,1)S(1)}, bf16[32,8704]{1,0:T(8,128)(2,1)S(1)}, u32[]{:S(2)}, u32[]{:S(2)}) %collective-permute-start.27) | collective-permute-done | bytes 557088 | tf_op jit(solution)/shard_map/ppermute | solution.py:84
  92.6 2.1 %collective-permute-start.28 = (f32[8,9216]{1,0:T(8,128)S(1)}, f32[8,9216]{1,0:T(8,128)S(1)}, u32[]{:S(2)}, u32[]{:S(2)}) collective-permute-start(f32[8,9216]{1,0:T(8,128)S(1)} %get-tuple-element.79), channel_id=1, source_target_pairs={{0,24},{1,25},{2,26},{3,27},{4,100},{5,101},{6,102},{7,103},{8,0},... | collective-permute-start | bytes 884744 | tf_op jit(solution)/shard_map/ppermute | solution.py:84
  94.7 1.1 collective-permute-start.32
  96.6 2.5 %collective-permute-start.33 = (f32[8,9216]{1,0:T(8,128)S(1)}, f32[8,9216]{1,0:T(8,128)S(1)}, u32[]{:S(2)}, u32[]{:S(2)}) collective-permute-start(f32[8,9216]{1,0:T(8,128)S(1)} %get-tuple-element.87), channel_id=1, source_target_pairs={{0,8},{1,9},{2,10},{3,11},{4,36},{5,37},{6,38},{7,39},{8,16},{9,17... | collective-permute-start | bytes 884744 | tf_op jit(solution)/shard_map/ppermute | solution.py:84
  99.0 3.8 %shard_map.172 = bf16[1,344,8192]{2,1,0:T(8,128)(2,1)} custom-call(bf16[32,8192]{1,0:T(8,128)(2,1)S(1)} %constant_dynamic-update-slice_fusion.4.refs_0_, bf16[32,8192]{1,0:T(8,128)(2,1)S(1)} %collective-permute-done.12.refs_1_, bf16[32,8192]{1,0:T(8,128)(2,1)S(1)} %collective-permute-done.13.refs_2_, bf16[32,8192]{1,0:T(8,128)(2,1)S(1)} %collective-permute-done.14.refs_3_, ...), custom_call_target="tpu_custom_call" | custom-call | flops 1442840576 | bytes 9830400 | tf_op jit(solution)/shard_map/pallas_call | solution.py:622
  102.8 7.1 %collective-permute-done.31 = bf16[32,8192]{1,0:T(8,128)(2,1)S(1)} collective-permute-done((bf16[32,8192]{1,0:T(8,128)(2,1)S(1)}, bf16[32,8192]{1,0:T(8,128)(2,1)S(1)}, u32[]{:S(2)}, u32[]{:S(2)}) %collective-permute-start.31) | collective-permute-done | bytes 524320 | tf_op jit(solution)/shard_map/ppermute | solution.py:84
  110.2 2.1 %collective-permute-start.35 = (bf16[8,10240]{1,0:T(8,128)(2,1)S(1)}, bf16[8,10240]{1,0:T(8,128)(2,1)S(1)}, u32[]{:S(2)}, u32[]{:S(2)}) collective-permute-start(bf16[8,10240]{1,0:T(8,128)(2,1)S(1)} %shard_map.173.refs_0_), channel_id=1, source_target_pairs={{0,1},{1,2},{2,3},{3,0},{4,5},{5,6},{6,7},{7,4},{8,9},{9,10},{10,1... | collective-permute-start | bytes 491528 | tf_op jit(solution)/shard_map/ppermute | solution.py:84
  112.3 2.4 %collective-permute-start.36 = (bf16[8,10240]{1,0:T(8,128)(2,1)S(1)}, bf16[8,10240]{1,0:T(8,128)(2,1)S(1)}, u32[]{:S(2)}, u32[]{:S(2)}) collective-permute-start(bf16[8,10240]{1,0:T(8,128)(2,1)S(1)} %shard_map.173.refs_0_), channel_id=1, source_target_pairs={{0,2},{1,3},{2,0},{3,1},{4,6},{5,7},{6,4},{7,5},{8,10},{9,11},{10,... | collective-permute-start | bytes 491528 | tf_op jit(solution)/shard_map/ppermute | solution.py:84
  114.7 1.8 %collective-permute-start.37 = (bf16[8,10240]{1,0:T(8,128)(2,1)S(1)}, bf16[8,10240]{1,0:T(8,128)(2,1)S(1)}, u32[]{:S(2)}, u32[]{:S(2)}) collective-permute-start(bf16[8,10240]{1,0:T(8,128)(2,1)S(1)} %shard_map.173.refs_0_), channel_id=1, source_target_pairs={{0,3},{1,0},{2,1},{3,2},{4,7},{5,4},{6,5},{7,6},{8,11},{9,8},{10,9... | collective-permute-start | bytes 491528 | tf_op jit(solution)/shard_map/ppermute | solution.py:84
  116.8 1.8 %collective-permute-start.34 = (bf16[8,8192]{1,0:T(8,128)(2,1)S(1)}, bf16[8,8192]{1,0:T(8,128)(2,1)S(1)}, u32[]{:S(2)}, u32[]{:S(2)}) collective-permute-start(bf16[8,8192]{1,0:T(8,128)(2,1)S(1)} %get-tuple-element.102), channel_id=1, source_target_pairs={{0,24},{1,25},{2,26},{3,27},{4,100},{5,101},{6,102},{7,103},{8,0},... | collective-permute-start | bytes 393224 | tf_op jit(solution)/shard_map/ppermute | solution.py:84
  118.7 1.4 collective-permute-start.38
  120.1 2.8 %collective-permute-done.36.refs_2_ = bf16[8,10240]{1,0:T(8,128)(2,1)S(1)} collective-permute-done((bf16[8,10240]{1,0:T(8,128)(2,1)S(1)}, bf16[8,10240]{1,0:T(8,128)(2,1)S(1)}, u32[]{:S(2)}, u32[]{:S(2)}) %collective-permute-start.36) | collective-permute-done | bytes 163872 | tf_op jit(solution)/shard_map/ppermute | solution.py:84
  122.9 2.1 %shard_map.174 = (bf16[4,8192]{1,0:T(4,128)(2,1)}, bf16[16,2048]{1,0:T(8,128)(2,1)S(1)}, f32[24,1024]{1,0:T(8,128)S(1)}) custom-call(s32[1]{0:T(128)} %bitcast.2.slot_ref, s32[4]{0:T(128)S(1)} %copy-done.7, f32[16,1]{1,0:T(8,128)S(1)} %get-tuple-element.56.column_ref, bf16[16,8192]{1,0:T(8,128)(2,1)S(1)} %get-tuple-element.60.hidden_ref, ...), custom_call_target="tpu_custom_call" | custom-call | flops 1000 | bytes 1000 | tf_op jit(solution)/shard_map/pallas_call | solution.py:281
  125.2 1.4 collective-permute-done.39.refs_3_
  126.5 1.0 shard_map.175
  127.6 1.1 fusion.9
  128.8 1.1 fusion.6
  130.2 2.0 %collective-permute-start.41 = (bf16[4,8192]{1,0:T(4,128)(2,1)S(1)}, bf16[4,8192]{1,0:T(4,128)(2,1)S(1)}, u32[]{:S(2)}, u32[]{:S(2)}) collective-permute-start(bf16[4,8192]{1,0:T(4,128)(2,1)S(1)} %get-tuple-element.93), channel_id=1, source_target_pairs={{0,2},{1,3},{2,0},{3,1},{4,6},{5,7},{6,4},{7,5},{8,10},{9,11},{10,... | collective-permute-start | bytes 196616 | tf_op jit(solution)/shard_map/ppermute | solution.py:84
  132.2 1.7 %collective-permute-start.42 = (bf16[4,8192]{1,0:T(4,128)(2,1)S(1)}, bf16[4,8192]{1,0:T(4,128)(2,1)S(1)}, u32[]{:S(2)}, u32[]{:S(2)}) collective-permute-start(bf16[4,8192]{1,0:T(4,128)(2,1)S(1)} %get-tuple-element.94), channel_id=1, source_target_pairs={{0,3},{1,0},{2,1},{3,2},{4,7},{5,4},{6,5},{7,6},{8,11},{9,8},{10,9... | collective-permute-start | bytes 196616 | tf_op jit(solution)/shard_map/ppermute | solution.py:84
  135.3 1.4 collective-permute-done.40
  (112 shorter events, 25.5 us)
Async XLA Ops:
  3.8 8.4 %collective-permute-start = (bf16[8,8192]{1,0:T(8,128)(2,1)S(1)}, bf16[8,8192]{1,0:T(8,128)(2,1)S(1)}, u32[]{:S(2)}, u32[]{:S(2)}) collective-permute-start(bf16[8,8192]{1,0:T(8,128)(2,1)S(1)} %get-tuple-element.54), channel_id=1, source_target_pairs={{0,8},{1,9},{2,10},{3,11},{4,36},{5,37},{6,38},{7,39},{8,16},{9,17... | collective-permute-start | bytes 393224 | tf_op jit(solution)/shard_map/ppermute | solution.py:84
  5.4 7.1 %collective-permute-start.1 = (bf16[8,8192]{1,0:T(8,128)(2,1)S(1)}, bf16[8,8192]{1,0:T(8,128)(2,1)S(1)}, u32[]{:S(2)}, u32[]{:S(2)}) collective-permute-start(bf16[8,8192]{1,0:T(8,128)(2,1)S(1)} %get-tuple-element.54), channel_id=1, source_target_pairs={{0,16},{1,17},{2,18},{3,19},{4,68},{5,69},{6,70},{7,71},{8,24},{9,... | collective-permute-start | bytes 393224 | tf_op jit(solution)/shard_map/ppermute | solution.py:84
  8.2 5.0 %collective-permute-start.2 = (bf16[8,8192]{1,0:T(8,128)(2,1)S(1)}, bf16[8,8192]{1,0:T(8,128)(2,1)S(1)}, u32[]{:S(2)}, u32[]{:S(2)}) collective-permute-start(bf16[8,8192]{1,0:T(8,128)(2,1)S(1)} %get-tuple-element.54), channel_id=1, source_target_pairs={{0,24},{1,25},{2,26},{3,27},{4,100},{5,101},{6,102},{7,103},{8,0},... | collective-permute-start | bytes 393224 | tf_op jit(solution)/shard_map/ppermute | solution.py:84
  13.2 19.8 %collective-permute-start.6 = (bf16[32,8192]{1,0:T(8,128)(2,1)S(1)}, bf16[32,8192]{1,0:T(8,128)(2,1)S(1)}, u32[]{:S(2)}, u32[]{:S(2)}) collective-permute-start(bf16[32,8192]{1,0:T(8,128)(2,1)S(1)} %constant_dynamic-update-slice_fusion.refs_0_), channel_id=1, source_target_pairs={{0,32},{1,33},{2,34},{3,35},{4,12},{5,13},{6,14},{7,15},{8,40},{9,... | collective-permute-start | bytes 1572872 | tf_op jit(solution)/shard_map/ppermute | solution.py:84
  15.1 17.8 %collective-permute-start.7 = (bf16[32,8192]{1,0:T(8,128)(2,1)S(1)}, bf16[32,8192]{1,0:T(8,128)(2,1)S(1)}, u32[]{:S(2)}, u32[]{:S(2)}) collective-permute-start(bf16[32,8192]{1,0:T(8,128)(2,1)S(1)} %constant_dynamic-update-slice_fusion.refs_0_), channel_id=1, source_target_pairs={{0,64},{1,65},{2,66},{3,67},{4,20},{5,21},{6,22},{7,23},{8,72},{9,... | collective-permute-start | bytes 1572872 | tf_op jit(solution)/shard_map/ppermute | solution.py:84
  18.7 14.3 %collective-permute-start.8 = (bf16[32,8192]{1,0:T(8,128)(2,1)S(1)}, bf16[32,8192]{1,0:T(8,128)(2,1)S(1)}, u32[]{:S(2)}, u32[]{:S(2)}) collective-permute-start(bf16[32,8192]{1,0:T(8,128)(2,1)S(1)} %constant_dynamic-update-slice_fusion.refs_0_), channel_id=1, source_target_pairs={{0,96},{1,97},{2,98},{3,99},{4,28},{5,29},{6,30},{7,31},{8,104},{9... | collective-permute-start | bytes 1572872 | tf_op jit(solution)/shard_map/ppermute | solution.py:84
  20.7 5.5 %collective-permute-start.3 = (bf16[16,2048]{1,0:T(8,128)(2,1)S(1)}, bf16[16,2048]{1,0:T(8,128)(2,1)S(1)}, u32[]{:S(2)}, u32[]{:S(2)}) collective-permute-start(bf16[16,2048]{1,0:T(8,128)(2,1)S(1)} %bitcast.79), channel_id=1, source_target_pairs={{0,1},{1,2},{2,3},{3,0},{4,5},{5,6},{6,7},{7,4},{8,9},{9,10},{10,1... | collective-permute-start | bytes 196616 | tf_op jit(solution)/shard_map/ppermute | solution.py:84
  22.3 5.8 %collective-permute-start.4 = (bf16[16,2048]{1,0:T(8,128)(2,1)S(1)}, bf16[16,2048]{1,0:T(8,128)(2,1)S(1)}, u32[]{:S(2)}, u32[]{:S(2)}) collective-permute-start(bf16[16,2048]{1,0:T(8,128)(2,1)S(1)} %bitcast.80), channel_id=1, source_target_pairs={{0,2},{1,3},{2,0},{3,1},{4,6},{5,7},{6,4},{7,5},{8,10},{9,11},{10,... | collective-permute-start | bytes 196616 | tf_op jit(solution)/shard_map/ppermute | solution.py:84
  26.2 4.3 %collective-permute-start.5 = (bf16[16,2048]{1,0:T(8,128)(2,1)S(1)}, bf16[16,2048]{1,0:T(8,128)(2,1)S(1)}, u32[]{:S(2)}, u32[]{:S(2)}) collective-permute-start(bf16[16,2048]{1,0:T(8,128)(2,1)S(1)} %bitcast.81), channel_id=1, source_target_pairs={{0,3},{1,0},{2,1},{3,2},{4,7},{5,4},{6,5},{7,6},{8,11},{9,8},{10,9... | collective-permute-start | bytes 196616 | tf_op jit(solution)/shard_map/ppermute | solution.py:84
  28.1 14.8 %collective-permute-start.15 = (bf16[32,8192]{1,0:T(8,128)(2,1)S(1)}, bf16[32,8192]{1,0:T(8,128)(2,1)S(1)}, u32[]{:S(2)}, u32[]{:S(2)}) collective-permute-start(bf16[32,8192]{1,0:T(8,128)(2,1)S(1)} %constant_dynamic-update-slice_fusion.refs_0_), channel_id=1, source_target_pairs={{0,4},{1,5},{2,6},{3,7},{4,0},{5,1},{6,2},{7,3},{8,12},{9,13},{10,... | collective-permute-start | bytes 1572872 | tf_op jit(solution)/shard_map/ppermute | solution.py:84
  33.0 6.2 %collective-permute-start.9 = (bf16[8,8192]{1,0:T(8,128)(2,1)S(1)}, bf16[8,8192]{1,0:T(8,128)(2,1)S(1)}, u32[]{:S(2)}, u32[]{:S(2)}) collective-permute-start(bf16[8,8192]{1,0:T(8,128)(2,1)S(1)} %get-tuple-element.62), channel_id=1, source_target_pairs={{0,8},{1,9},{2,10},{3,11},{4,36},{5,37},{6,38},{7,39},{8,16},{9,17... | collective-permute-start | bytes 393224 | tf_op jit(solution)/shard_map/ppermute | solution.py:84
  34.3 7.2 %collective-permute-start.10 = (bf16[8,8192]{1,0:T(8,128)(2,1)S(1)}, bf16[8,8192]{1,0:T(8,128)(2,1)S(1)}, u32[]{:S(2)}, u32[]{:S(2)}) collective-permute-start(bf16[8,8192]{1,0:T(8,128)(2,1)S(1)} %get-tuple-element.62), channel_id=1, source_target_pairs={{0,16},{1,17},{2,18},{3,19},{4,68},{5,69},{6,70},{7,71},{8,24},{9,... | collective-permute-start | bytes 393224 | tf_op jit(solution)/shard_map/ppermute | solution.py:84
  37.3 5.0 %collective-permute-start.11 = (bf16[8,8192]{1,0:T(8,128)(2,1)S(1)}, bf16[8,8192]{1,0:T(8,128)(2,1)S(1)}, u32[]{:S(2)}, u32[]{:S(2)}) collective-permute-start(bf16[8,8192]{1,0:T(8,128)(2,1)S(1)} %get-tuple-element.62), channel_id=1, source_target_pairs={{0,24},{1,25},{2,26},{3,27},{4,100},{5,101},{6,102},{7,103},{8,0},... | collective-permute-start | bytes 393224 | tf_op jit(solution)/shard_map/ppermute | solution.py:84
  38.1 6.2 %collective-permute-start.16 = (bf16[32,8192]{1,0:T(8,128)(2,1)S(1)}, bf16[32,8192]{1,0:T(8,128)(2,1)S(1)}, u32[]{:S(2)}, u32[]{:S(2)}) collective-permute-start(bf16[32,8192]{1,0:T(8,128)(2,1)S(1)} %collective-permute-done.6.refs_1_), channel_id=1, source_target_pairs={{0,4},{1,5},{2,6},{3,7},{4,0},{5,1},{6,2},{7,3},{8,12},{9,13},{10,... | collective-permute-start | bytes 1572872 | tf_op jit(solution)/shard_map/ppermute | solution.py:84
  39.2 10.0 %collective-permute-start.17 = (bf16[32,8192]{1,0:T(8,128)(2,1)S(1)}, bf16[32,8192]{1,0:T(8,128)(2,1)S(1)}, u32[]{:S(2)}, u32[]{:S(2)}) collective-permute-start(bf16[32,8192]{1,0:T(8,128)(2,1)S(1)} %collective-permute-done.7.refs_2_), channel_id=1, source_target_pairs={{0,4},{1,5},{2,6},{3,7},{4,0},{5,1},{6,2},{7,3},{8,12},{9,13},{10,... | collective-permute-start | bytes 1572872 | tf_op jit(solution)/shard_map/ppermute | solution.py:84
  41.5 7.9 %collective-permute-start.18 = (bf16[32,8192]{1,0:T(8,128)(2,1)S(1)}, bf16[32,8192]{1,0:T(8,128)(2,1)S(1)}, u32[]{:S(2)}, u32[]{:S(2)}) collective-permute-start(bf16[32,8192]{1,0:T(8,128)(2,1)S(1)} %collective-permute-done.8.refs_3_), channel_id=1, source_target_pairs={{0,4},{1,5},{2,6},{3,7},{4,0},{5,1},{6,2},{7,3},{8,12},{9,13},{10,... | collective-permute-start | bytes 1572872 | tf_op jit(solution)/shard_map/ppermute | solution.py:84
  42.2 6.4 %slice-start = ((s8[5636096]{0:T(1024)(128)(4,1)}), s8[4194304]{0:T(1024)(128)(4,1)S(1)}, s32[]{:S(2)}) async-start(s8[5636096]{0:T(1024)(128)(4,1)} %bitcast.75), calls=%async_computation | async-start | bytes 8388608
  42.3 9.8 %collective-permute-start.14 = (bf16[32,8192]{1,0:T(8,128)(2,1)S(1)}, bf16[32,8192]{1,0:T(8,128)(2,1)S(1)}, u32[]{:S(2)}, u32[]{:S(2)}) collective-permute-start(bf16[32,8192]{1,0:T(8,128)(2,1)S(1)} %constant_dynamic-update-slice_fusion.4.refs_0_), channel_id=1, source_target_pairs={{0,96},{1,97},{2,98},{3,99},{4,28},{5,29},{6,30},{7,31},{8,104},{9... | collective-permute-start | bytes 1572872 | tf_op jit(solution)/shard_map/ppermute | solution.py:84
  42.9 16.0 %collective-permute-start.12 = (bf16[32,8192]{1,0:T(8,128)(2,1)S(1)}, bf16[32,8192]{1,0:T(8,128)(2,1)S(1)}, u32[]{:S(2)}, u32[]{:S(2)}) collective-permute-start(bf16[32,8192]{1,0:T(8,128)(2,1)S(1)} %constant_dynamic-update-slice_fusion.4.refs_0_), channel_id=1, source_target_pairs={{0,32},{1,33},{2,34},{3,35},{4,12},{5,13},{6,14},{7,15},{8,40},{9,... | collective-permute-start | bytes 1572872 | tf_op jit(solution)/shard_map/ppermute | solution.py:84
  44.4 14.6 %collective-permute-start.13 = (bf16[32,8192]{1,0:T(8,128)(2,1)S(1)}, bf16[32,8192]{1,0:T(8,128)(2,1)S(1)}, u32[]{:S(2)}, u32[]{:S(2)}) collective-permute-start(bf16[32,8192]{1,0:T(8,128)(2,1)S(1)} %constant_dynamic-update-slice_fusion.4.refs_0_), channel_id=1, source_target_pairs={{0,64},{1,65},{2,66},{3,67},{4,20},{5,21},{6,22},{7,23},{8,72},{9,... | collective-permute-start | bytes 1572872 | tf_op jit(solution)/shard_map/ppermute | solution.py:84
  49.3 10.2 %collective-permute-start.19 = (bf16[32,8192]{1,0:T(8,128)(2,1)S(1)}, bf16[32,8192]{1,0:T(8,128)(2,1)S(1)}, u32[]{:S(2)}, u32[]{:S(2)}) collective-permute-start(bf16[32,8192]{1,0:T(8,128)(2,1)S(1)} %constant_dynamic-update-slice_fusion.4.refs_0_), channel_id=1, source_target_pairs={{0,4},{1,5},{2,6},{3,7},{4,0},{5,1},{6,2},{7,3},{8,12},{9,13},{10,... | collective-permute-start | bytes 1572872 | tf_op jit(solution)/shard_map/ppermute | solution.py:84
  52.1 7.4 %collective-permute-start.22 = (bf16[32,8192]{1,0:T(8,128)(2,1)S(1)}, bf16[32,8192]{1,0:T(8,128)(2,1)S(1)}, u32[]{:S(2)}, u32[]{:S(2)}) collective-permute-start(bf16[32,8192]{1,0:T(8,128)(2,1)S(1)} %collective-permute-done.14.refs_3_), channel_id=1, source_target_pairs={{0,4},{1,5},{2,6},{3,7},{4,0},{5,1},{6,2},{7,3},{8,12},{9,13},{10,... | collective-permute-start | bytes 1572872 | tf_op jit(solution)/shard_map/ppermute | solution.py:84
  58.9 1.9 %collective-permute-start.20 = (bf16[32,8192]{1,0:T(8,128)(2,1)S(1)}, bf16[32,8192]{1,0:T(8,128)(2,1)S(1)}, u32[]{:S(2)}, u32[]{:S(2)}) collective-permute-start(bf16[32,8192]{1,0:T(8,128)(2,1)S(1)} %collective-permute-done.12.refs_1_), channel_id=1, source_target_pairs={{0,4},{1,5},{2,6},{3,7},{4,0},{5,1},{6,2},{7,3},{8,12},{9,13},{10,... | collective-permute-start | bytes 1572872 | tf_op jit(solution)/shard_map/ppermute | solution.py:84
  58.9 2.7 %collective-permute-start.21 = (bf16[32,8192]{1,0:T(8,128)(2,1)S(1)}, bf16[32,8192]{1,0:T(8,128)(2,1)S(1)}, u32[]{:S(2)}, u32[]{:S(2)}) collective-permute-start(bf16[32,8192]{1,0:T(8,128)(2,1)S(1)} %collective-permute-done.13.refs_2_), channel_id=1, source_target_pairs={{0,4},{1,5},{2,6},{3,7},{4,0},{5,1},{6,2},{7,3},{8,12},{9,13},{10,... | collective-permute-start | bytes 1572872 | tf_op jit(solution)/shard_map/ppermute | solution.py:84
  67.5 4.2 %collective-permute-start.23 = (bf16[128,8192]{1,0:T(8,128)(2,1)S(1)}, bf16[128,8192]{1,0:T(8,128)(2,1)S(1)}, u32[]{:S(2)}, u32[]{:S(2)}) collective-permute-start(bf16[128,8192]{1,0:T(8,128)(2,1)S(1)} %get-tuple-element.66), channel_id=1, source_target_pairs={{0,4},{1,5},{2,6},{3,7},{4,0},{5,1},{6,2},{7,3},{8,12},{9,13},{10,... | collective-permute-start | bytes 6291464 | tf_op jit(solution)/shard_map/ppermute | solution.py:84
  69.7 8.0 %collective-permute-start.24 = (bf16[128,8192]{1,0:T(8,128)(2,1)S(1)}, bf16[128,8192]{1,0:T(8,128)(2,1)S(1)}, u32[]{:S(2)}, u32[]{:S(2)}) collective-permute-start(bf16[128,8192]{1,0:T(8,128)(2,1)S(1)} %shard_map.167), channel_id=1, source_target_pairs={{0,4},{1,5},{2,6},{3,7},{4,0},{5,1},{6,2},{7,3},{8,12},{9,13},{10,... | collective-permute-start | bytes 6291464 | tf_op jit(solution)/shard_map/ppermute | solution.py:84
  75.2 9.6 %collective-permute-start.25 = (bf16[32,8704]{1,0:T(8,128)(2,1)S(1)}, bf16[32,8704]{1,0:T(8,128)(2,1)S(1)}, u32[]{:S(2)}, u32[]{:S(2)}) collective-permute-start(bf16[32,8704]{1,0:T(8,128)(2,1)S(1)} %get-tuple-element.72), channel_id=1, source_target_pairs={{0,96},{1,97},{2,98},{3,99},{4,28},{5,29},{6,30},{7,31},{8,104},{9... | collective-permute-start | bytes 1671176 | tf_op jit(solution)/shard_map/ppermute | solution.py:84
  75.3 13.2 %collective-permute-start.26 = (bf16[32,8704]{1,0:T(8,128)(2,1)S(1)}, bf16[32,8704]{1,0:T(8,128)(2,1)S(1)}, u32[]{:S(2)}, u32[]{:S(2)}) collective-permute-start(bf16[32,8704]{1,0:T(8,128)(2,1)S(1)} %get-tuple-element.76), channel_id=1, source_target_pairs={{0,64},{1,65},{2,66},{3,67},{4,20},{5,21},{6,22},{7,23},{8,72},{9,... | collective-permute-start | bytes 1671176 | tf_op jit(solution)/shard_map/ppermute | solution.py:84
  77.2 15.1 %collective-permute-start.27 = (bf16[32,8704]{1,0:T(8,128)(2,1)S(1)}, bf16[32,8704]{1,0:T(8,128)(2,1)S(1)}, u32[]{:S(2)}, u32[]{:S(2)}) collective-permute-start(bf16[32,8704]{1,0:T(8,128)(2,1)S(1)} %get-tuple-element.77), channel_id=1, source_target_pairs={{0,32},{1,33},{2,34},{3,35},{4,12},{5,13},{6,14},{7,15},{8,40},{9,... | collective-permute-start | bytes 1671176 | tf_op jit(solution)/shard_map/ppermute | solution.py:84
  79.0 17.6 %collective-permute-start.29 = (bf16[32,8192]{1,0:T(8,128)(2,1)S(1)}, bf16[32,8192]{1,0:T(8,128)(2,1)S(1)}, u32[]{:S(2)}, u32[]{:S(2)}) collective-permute-start(bf16[32,8192]{1,0:T(8,128)(2,1)S(1)} %get-tuple-element.82), channel_id=1, source_target_pairs={{0,96},{1,97},{2,98},{3,99},{4,28},{5,29},{6,30},{7,31},{8,104},{9... | collective-permute-start | bytes 1572872 | tf_op jit(solution)/shard_map/ppermute | solution.py:84
  81.9 20.9 %collective-permute-start.30 = (bf16[32,8192]{1,0:T(8,128)(2,1)S(1)}, bf16[32,8192]{1,0:T(8,128)(2,1)S(1)}, u32[]{:S(2)}, u32[]{:S(2)}) collective-permute-start(bf16[32,8192]{1,0:T(8,128)(2,1)S(1)} %get-tuple-element.83), channel_id=1, source_target_pairs={{0,64},{1,65},{2,66},{3,67},{4,20},{5,21},{6,22},{7,23},{8,72},{9,... | collective-permute-start | bytes 1572872 | tf_op jit(solution)/shard_map/ppermute | solution.py:84
  84.8 25.1 %collective-permute-start.31 = (bf16[32,8192]{1,0:T(8,128)(2,1)S(1)}, bf16[32,8192]{1,0:T(8,128)(2,1)S(1)}, u32[]{:S(2)}, u32[]{:S(2)}) collective-permute-start(bf16[32,8192]{1,0:T(8,128)(2,1)S(1)} %get-tuple-element.84), channel_id=1, source_target_pairs={{0,32},{1,33},{2,34},{3,35},{4,12},{5,13},{6,14},{7,15},{8,40},{9,... | collective-permute-start | bytes 1572872 | tf_op jit(solution)/shard_map/ppermute | solution.py:84
  92.6 17.3 %collective-permute-start.28 = (f32[8,9216]{1,0:T(8,128)S(1)}, f32[8,9216]{1,0:T(8,128)S(1)}, u32[]{:S(2)}, u32[]{:S(2)}) collective-permute-start(f32[8,9216]{1,0:T(8,128)S(1)} %get-tuple-element.79), channel_id=1, source_target_pairs={{0,24},{1,25},{2,26},{3,27},{4,100},{5,101},{6,102},{7,103},{8,0},... | collective-permute-start | bytes 884744 | tf_op jit(solution)/shard_map/ppermute | solution.py:84
  94.7 15.2 %collective-permute-start.32 = (f32[8,9216]{1,0:T(8,128)S(1)}, f32[8,9216]{1,0:T(8,128)S(1)}, u32[]{:S(2)}, u32[]{:S(2)}) collective-permute-start(f32[8,9216]{1,0:T(8,128)S(1)} %get-tuple-element.86), channel_id=1, source_target_pairs={{0,16},{1,17},{2,18},{3,19},{4,68},{5,69},{6,70},{7,71},{8,24},{9,... | collective-permute-start | bytes 884744 | tf_op jit(solution)/shard_map/ppermute | solution.py:84
  96.6 13.6 %collective-permute-start.33 = (f32[8,9216]{1,0:T(8,128)S(1)}, f32[8,9216]{1,0:T(8,128)S(1)}, u32[]{:S(2)}, u32[]{:S(2)}) collective-permute-start(f32[8,9216]{1,0:T(8,128)S(1)} %get-tuple-element.87), channel_id=1, source_target_pairs={{0,8},{1,9},{2,10},{3,11},{4,36},{5,37},{6,38},{7,39},{8,16},{9,17... | collective-permute-start | bytes 884744 | tf_op jit(solution)/shard_map/ppermute | solution.py:84
  102.8 20.0 %copy-start.2 = (f32[3,8192]{1,0:T(4,128)S(1)}, f32[3,8192]{1,0:T(4,128)}, u32[]{:S(2)}) copy-start(f32[3,8192]{1,0:T(4,128)} %gains_ref.1) | copy-start | bytes 294916
  102.8 20.0 %copy-start.4 = (bf16[1,16,8192]{2,1,0:T(8,128)(2,1)S(1)}, bf16[1,16,8192]{2,1,0:T(8,128)(2,1)}, u32[]{:S(2)}) copy-start(bf16[1,16,8192]{2,1,0:T(8,128)(2,1)} %param.19) | copy-start | bytes 786436
  102.8 20.0 %copy-start.7 = (s32[4]{0:T(128)S(1)}, s32[4]{0:T(128)}, u32[]{:S(2)}) copy-start(s32[4]{0:T(128)} %kinds_ref.3) | copy-start | bytes 52
  110.2 9.8 %collective-permute-start.35 = (bf16[8,10240]{1,0:T(8,128)(2,1)S(1)}, bf16[8,10240]{1,0:T(8,128)(2,1)S(1)}, u32[]{:S(2)}, u32[]{:S(2)}) collective-permute-start(bf16[8,10240]{1,0:T(8,128)(2,1)S(1)} %shard_map.173.refs_0_), channel_id=1, source_target_pairs={{0,1},{1,2},{2,3},{3,0},{4,5},{5,6},{6,7},{7,4},{8,9},{9,10},{10,1... | collective-permute-start | bytes 491528 | tf_op jit(solution)/shard_map/ppermute | solution.py:84
  112.3 10.5 %collective-permute-start.36 = (bf16[8,10240]{1,0:T(8,128)(2,1)S(1)}, bf16[8,10240]{1,0:T(8,128)(2,1)S(1)}, u32[]{:S(2)}, u32[]{:S(2)}) collective-permute-start(bf16[8,10240]{1,0:T(8,128)(2,1)S(1)} %shard_map.173.refs_0_), channel_id=1, source_target_pairs={{0,2},{1,3},{2,0},{3,1},{4,6},{5,7},{6,4},{7,5},{8,10},{9,11},{10,... | collective-permute-start | bytes 491528 | tf_op jit(solution)/shard_map/ppermute | solution.py:84
  114.7 8.1 %collective-permute-start.37 = (bf16[8,10240]{1,0:T(8,128)(2,1)S(1)}, bf16[8,10240]{1,0:T(8,128)(2,1)S(1)}, u32[]{:S(2)}, u32[]{:S(2)}) collective-permute-start(bf16[8,10240]{1,0:T(8,128)(2,1)S(1)} %shard_map.173.refs_0_), channel_id=1, source_target_pairs={{0,3},{1,0},{2,1},{3,2},{4,7},{5,4},{6,5},{7,6},{8,11},{9,8},{10,9... | collective-permute-start | bytes 491528 | tf_op jit(solution)/shard_map/ppermute | solution.py:84
  116.8 8.1 %collective-permute-start.34 = (bf16[8,8192]{1,0:T(8,128)(2,1)S(1)}, bf16[8,8192]{1,0:T(8,128)(2,1)S(1)}, u32[]{:S(2)}, u32[]{:S(2)}) collective-permute-start(bf16[8,8192]{1,0:T(8,128)(2,1)S(1)} %get-tuple-element.102), channel_id=1, source_target_pairs={{0,24},{1,25},{2,26},{3,27},{4,100},{5,101},{6,102},{7,103},{8,0},... | collective-permute-start | bytes 393224 | tf_op jit(solution)/shard_map/ppermute | solution.py:84
  118.7 6.5 %collective-permute-start.38 = (bf16[8,8192]{1,0:T(8,128)(2,1)S(1)}, bf16[8,8192]{1,0:T(8,128)(2,1)S(1)}, u32[]{:S(2)}, u32[]{:S(2)}) collective-permute-start(bf16[8,8192]{1,0:T(8,128)(2,1)S(1)} %get-tuple-element.101), channel_id=1, source_target_pairs={{0,16},{1,17},{2,18},{3,19},{4,68},{5,69},{6,70},{7,71},{8,24},{9,... | collective-permute-start | bytes 393224 | tf_op jit(solution)/shard_map/ppermute | solution.py:84
  120.0 6.5 %collective-permute-start.39 = (bf16[8,8192]{1,0:T(8,128)(2,1)S(1)}, bf16[8,8192]{1,0:T(8,128)(2,1)S(1)}, u32[]{:S(2)}, u32[]{:S(2)}) collective-permute-start(bf16[8,8192]{1,0:T(8,128)(2,1)S(1)} %get-tuple-element.100), channel_id=1, source_target_pairs={{0,8},{1,9},{2,10},{3,11},{4,36},{5,37},{6,38},{7,39},{8,16},{9,17... | collective-permute-start | bytes 393224 | tf_op jit(solution)/shard_map/ppermute | solution.py:84
  124.9 13.0 %collective-permute-start.43 = (f32[24,1024]{1,0:T(8,128)S(1)}, f32[24,1024]{1,0:T(8,128)S(1)}, u32[]{:S(2)}, u32[]{:S(2)}) collective-permute-start(f32[24,1024]{1,0:T(8,128)S(1)} %get-tuple-element.97), channel_id=1, source_target_pairs={{0,4},{1,5},{2,6},{3,7},{4,0},{5,1},{6,2},{7,3},{8,12},{9,13},{10,... | collective-permute-start | bytes 294920 | tf_op jit(solution)/shard_map/ppermute | solution.py:84
  130.1 6.6 %collective-permute-start.40 = (bf16[4,8192]{1,0:T(4,128)(2,1)S(1)}, bf16[4,8192]{1,0:T(4,128)(2,1)S(1)}, u32[]{:S(2)}, u32[]{:S(2)}) collective-permute-start(bf16[4,8192]{1,0:T(4,128)(2,1)S(1)} %get-tuple-element.92), channel_id=1, source_target_pairs={{0,1},{1,2},{2,3},{3,0},{4,5},{5,6},{6,7},{7,4},{8,9},{9,10},{10,1... | collective-permute-start | bytes 196616 | tf_op jit(solution)/shard_map/ppermute | solution.py:84
  130.2 6.5 %collective-permute-start.41 = (bf16[4,8192]{1,0:T(4,128)(2,1)S(1)}, bf16[4,8192]{1,0:T(4,128)(2,1)S(1)}, u32[]{:S(2)}, u32[]{:S(2)}) collective-permute-start(bf16[4,8192]{1,0:T(4,128)(2,1)S(1)} %get-tuple-element.93), channel_id=1, source_target_pairs={{0,2},{1,3},{2,0},{3,1},{4,6},{5,7},{6,4},{7,5},{8,10},{9,11},{10,... | collective-permute-start | bytes 196616 | tf_op jit(solution)/shard_map/ppermute | solution.py:84
  132.2 5.0 %collective-permute-start.42 = (bf16[4,8192]{1,0:T(4,128)(2,1)S(1)}, bf16[4,8192]{1,0:T(4,128)(2,1)S(1)}, u32[]{:S(2)}, u32[]{:S(2)}) collective-permute-start(bf16[4,8192]{1,0:T(4,128)(2,1)S(1)} %get-tuple-element.94), channel_id=1, source_target_pairs={{0,3},{1,0},{2,1},{3,2},{4,7},{5,4},{6,5},{7,6},{8,11},{9,8},{10,9... | collective-permute-start | bytes 196616 | tf_op jit(solution)/shard_map/ppermute | solution.py:84
  (8 other events, 13.8 us)
